TPU v7x, 512 devices: a whole 4x8x8 slice. The times are simulated.
512 devices in a mesh: row: 16 (over z, core), col: 32 (over y, x).
Axes of the slice: x: 4, y: 8, z: 8, core: 2. Of those that a mesh axis runs over, the one named last changes fastest.
Arguments:
- joined_grad: bfloat16 [256, 1024, 384], P('row', 'col'), may hold values from -6 to 6
- join_weight: bfloat16 [1536, 384], replicated, may hold values from -0.15625 to 0.15625
- linear_first: bfloat16 [64, 384], replicated, may hold values from -0.75 to 0.75
- linear_second: bfloat16 [128, 384], replicated, may hold values from -0.5 to 0.5
- linear_third: bfloat16 [320, 384], replicated, may hold values from -0.3125 to 0.3125
- linear_fourth: bfloat16 [512, 384], replicated, may hold values from -0.25 to 0.25
- feature_second: bfloat16 [128, 512, 128], P('row', 'col'), may hold values from -6 to 6
- feature_third: bfloat16 [64, 256, 320], P('row', 'col'), may hold values from -6 to 6
- feature_fourth: bfloat16 [32, 128, 512], P('row', 'col'), may hold values from -6 to 6
- block_input: bfloat16 [256, 1024, 64], P('row', 'col'), may hold values from -36 to 36
- later_grad: bfloat16 [256, 1024, 64], P('row', 'col'), may hold values from -6 to 6
- norm_gain: float32 [64], replicated, may hold values from 0.1 to 1.9
- norm_shift: float32 [64], replicated, may hold values from -3 to 3
- expand_weight: bfloat16 [64, 256], replicated, may hold values from -0.75 to 0.75
- expand_bias: float32 [256], replicated, may hold values from -3 to 3
- depth_weight: float32 [9, 256], replicated, may hold values from -2 to 2
- depth_bias: float32 [256], replicated, may hold values from -3 to 3
- reduce_weight: bfloat16 [256, 64], replicated, may hold values from -0.375 to 0.375
- reduce_bias: float32 [64], replicated, may hold values from -3 to 3
Outputs:
- input_grad: bfloat16 [256, 1024, 64], P('row', 'col')
- second_grad: bfloat16 [128, 512, 128], P('row', 'col')
- third_grad: bfloat16 [64, 256, 320], P('row', 'col')
- fourth_grad: bfloat16 [32, 128, 512], P('row', 'col')
- linear_grads: float32 [393216], P(('row', 'col'))
- biases_grad: float32 [4, 384], replicated
- expand_grad: float32 [64, 256], replicated
- reduce_grad: float32 [256, 64], replicated
- depth_grad: float32 [9, 256], replicated
- hidden_grads: float32 [2, 256], replicated
- channel_grads: float32 [3, 64], replicated
All inputs are finite; a program needn't handle non-finite values.
Results may differ from a plain program's by a relative error of at most 0.0083.
Values may be sent and summed in bfloat16 or wider, within the bound.
No kernel may reach another device: no remote copies, remote signals or barrier semaphores. Data moves between devices by JAX's collectives and lax.ppermute only.
A program may use at most 64 MiB of HBM per device.

v0:
```python
import math

import jax
import jax.numpy as jnp
from jax import lax
from jax.sharding import PartitionSpec as P

D1 = 64
D2 = 128
D3 = 320
D4 = 512
HID = 256
DEC = 384
TH = 16
TW = 32


norm_eps = 1e-06
inv_root_two = 0.7071067811865476
inv_root_tau = 0.3989422804014327


def with_halo(shard, sides, width):
    for axis, dim in sides:
        devices, length = (lax.axis_size(axis), shard.shape[dim])
        up = [(i, (i + 1) % devices) for i in range(devices - 1)]
        down = [(j, i) for i, j in up]
        last = lax.slice_in_dim(shard, length - width, length, axis=dim)
        initial = lax.slice_in_dim(shard, 0, width, axis=dim)
        before = lax.ppermute(last, axis, up)
        after = lax.ppermute(initial, axis, down)
        shard = jnp.concatenate([before, shard, after], axis=dim)
    return shard


def interp_local(fine_start, fine_count, coarse_start, coarse_count, factor, coarse_total):
    fine_pos = (fine_start + jnp.arange(fine_count)).astype(jnp.float32)
    coordinate = jnp.maximum((fine_pos + 0.5) / factor - 0.5, 0.0)
    lower = jnp.floor(coordinate)
    weight = coordinate - lower
    upper = jnp.minimum(lower + 1.0, coarse_total - 1.0)
    coarse_pos = (coarse_start + jnp.arange(coarse_count)).astype(jnp.float32)
    return jnp.where(coarse_pos[None, :] == lower[:, None], 1.0 - weight[:, None], 0.0) + jnp.where(
        coarse_pos[None, :] == upper[:, None], weight[:, None], 0.0
    )


def contract_grid(grid, row_matrix, col_matrix):
    fine_rows = grid.shape[0]
    fine_cols = grid.shape[1]
    left_sum = jnp.dot(
        row_matrix.T.astype(jnp.bfloat16),
        grid.reshape(fine_rows, -1),
        preferred_element_type=jnp.float32,
    )
    left_sum = left_sum.reshape(row_matrix.shape[1], fine_cols, grid.shape[2])
    return jnp.einsum("awc,wb->abc", left_sum, col_matrix, precision=lax.Precision.HIGHEST)


def layer_stats(source, gain, shift):
    values = source.astype(jnp.float32)
    center = jnp.mean(values, -1, keepdims=True)
    spread = jnp.mean(jnp.square(values - center), -1, keepdims=True)
    scaling = lax.rsqrt(spread + norm_eps)
    standard = (values - center) * scaling
    normed = (standard * gain + shift).astype(jnp.bfloat16)
    return (normed, standard, scaling)


def expand_rows(normed, weight, bias):
    shape = normed.shape
    result = (
        jnp.dot(normed.reshape(-1, shape[-1]), weight, preferred_element_type=jnp.float32) + bias
    )
    return result.astype(jnp.bfloat16).reshape(shape[0], shape[1], -1)


def gelu_parts(conv):
    cumulative = 0.5 * (1.0 + lax.erf(conv * inv_root_two))
    density = inv_root_tau * jnp.exp(-0.5 * conv * conv)
    return (conv * cumulative, cumulative + conv * density)


def local(
    joined_grad,
    join_weight,
    linear_first,
    linear_second,
    linear_third,
    linear_fourth,
    feature_second,
    feature_third,
    feature_fourth,
    block_input,
    later_grad,
    norm_gain,
    norm_shift,
    expand_weight,
    expand_bias,
    depth_weight,
    depth_bias,
    reduce_weight,
    reduce_bias,
):
    row_index = lax.axis_index("row")
    col_index = lax.axis_index("col")
    height = TH * lax.axis_size("row")
    width = TW * lax.axis_size("col")
    normed, standard, scaling = layer_stats(block_input, norm_gain, norm_shift)
    hidden = expand_rows(normed, expand_weight, expand_bias)
    padded = with_halo(hidden, (("row", 0), ("col", 1)), 1)
    conv = jnp.zeros((TH, TW, HID), jnp.float32) + depth_bias
    for tap_index in range(9):
        offset_row = tap_index // 3
        offset_col = tap_index % 3
        conv = (
            conv
            + depth_weight[tap_index]
            * padded[offset_row : offset_row + TH, offset_col : offset_col + TW]
        )
    value, slope = gelu_parts(conv)
    activated = value.astype(jnp.bfloat16)
    reduced = (
        jnp.dot(activated.reshape(-1, HID), reduce_weight, preferred_element_type=jnp.float32)
        + reduce_bias
    )
    features = (block_input.reshape(-1, D1).astype(jnp.float32) + reduced).astype(jnp.bfloat16)
    wide_cotangent = with_halo(joined_grad, (("row", 0), ("col", 1)), 4)
    pooled = [joined_grad]
    for scale_index in (1, 2, 3):
        factor = 2**scale_index
        coarse_rows = TH // factor
        coarse_cols = TW // factor
        row_matrix = interp_local(
            row_index * TH - 4,
            TH + 8,
            row_index * coarse_rows,
            coarse_rows,
            factor,
            height // factor,
        )
        col_matrix = interp_local(
            col_index * TW - 4,
            TW + 8,
            col_index * coarse_cols,
            coarse_cols,
            factor,
            width // factor,
        )
        pooled.append(contract_grid(wide_cotangent, row_matrix, col_matrix).astype(jnp.bfloat16))
    scale_base = 1.0 / math.sqrt(height * width)
    sources = (features, feature_second, feature_third, feature_fourth)
    projected = []
    weight_terms = []
    bias_terms = []
    for scale_index in range(4):
        block_weight = join_weight[scale_index * DEC : (scale_index + 1) * DEC]
        projection = jnp.dot(
            pooled[scale_index].reshape(-1, DEC), block_weight.T, preferred_element_type=jnp.float32
        ).astype(jnp.bfloat16)
        factor_scale = 2**scale_index * scale_base
        source = sources[scale_index]
        source_flat = source.reshape(-1, source.shape[-1])
        weight_terms.append(
            (
                jnp.dot(source_flat.T, projection, preferred_element_type=jnp.float32)
                * factor_scale
            ).reshape(-1)
        )
        bias_terms.append(jnp.sum(projection, 0, dtype=jnp.float32) * factor_scale)
        projected.append(projection)
    linear_grads = lax.psum_scatter(
        jnp.concatenate(weight_terms), ("row", "col"), scatter_dimension=0, tiled=True
    )
    feature_grad = (
        jnp.dot(projected[0], linear_first.T, preferred_element_type=jnp.float32)
        + later_grad.reshape(-1, D1).astype(jnp.float32)
    ).astype(jnp.bfloat16)
    second_grad = (
        jnp.dot(projected[1], linear_second.T, preferred_element_type=jnp.float32)
        .astype(jnp.bfloat16)
        .reshape(TH // 2, TW // 2, D2)
    )
    third_grad = (
        jnp.dot(projected[2], linear_third.T, preferred_element_type=jnp.float32)
        .astype(jnp.bfloat16)
        .reshape(TH // 4, TW // 4, D3)
    )
    fourth_grad = (
        jnp.dot(projected[3], linear_fourth.T, preferred_element_type=jnp.float32)
        .astype(jnp.bfloat16)
        .reshape(TH // 8, TW // 8, D4)
    )
    act_grad = jnp.dot(feature_grad, reduce_weight.T, preferred_element_type=jnp.float32).reshape(
        TH, TW, HID
    )
    pre_grad = (act_grad * slope).astype(jnp.bfloat16)
    reduce_part = (
        jnp.dot(activated.reshape(-1, HID).T, feature_grad, preferred_element_type=jnp.float32)
        * scale_base
    )
    wide_grad = with_halo(pre_grad, (("row", 0), ("col", 1)), 1)
    depth_parts = []
    hidden_acc = jnp.zeros((TH, TW, HID), jnp.float32)
    for tap_index in range(9):
        offset_row = tap_index // 3
        offset_col = tap_index % 3
        window = padded[offset_row : offset_row + TH, offset_col : offset_col + TW]
        depth_parts.append(
            jnp.sum(window.astype(jnp.float32) * pre_grad.astype(jnp.float32), (0, 1)) * scale_base
        )
        hidden_acc = (
            hidden_acc
            + depth_weight[tap_index]
            * wide_grad[2 - offset_row : 2 - offset_row + TH, 2 - offset_col : 2 - offset_col + TW]
        )
    hidden_grad = hidden_acc.astype(jnp.bfloat16).reshape(-1, HID)
    expand_part = (
        jnp.dot(normed.reshape(-1, D1).T, hidden_grad, preferred_element_type=jnp.float32)
        * scale_base
    )
    normed_grad = jnp.dot(hidden_grad, expand_weight.T, preferred_element_type=jnp.float32)
    standard_flat = standard.reshape(-1, D1)
    hidden_part = jnp.stack(
        [
            jnp.sum(hidden_grad, 0, dtype=jnp.float32) * scale_base,
            jnp.sum(pre_grad.reshape(-1, HID), 0, dtype=jnp.float32) * scale_base,
        ]
    )
    channel_part = jnp.stack(
        [
            jnp.sum(feature_grad, 0, dtype=jnp.float32) * scale_base,
            jnp.sum(normed_grad * standard_flat, 0) * scale_base,
            jnp.sum(normed_grad, 0) * scale_base,
        ]
    )
    scaled = normed_grad * norm_gain
    input_grad = (
        (
            feature_grad.astype(jnp.float32)
            + scaling.reshape(-1, 1)
            * (
                scaled
                - jnp.mean(scaled, -1, keepdims=True)
                - standard_flat * jnp.mean(scaled * standard_flat, -1, keepdims=True)
            )
        )
        .astype(jnp.bfloat16)
        .reshape(TH, TW, D1)
    )
    summed = lax.psum(
        (
            jnp.stack(bias_terms),
            expand_part,
            reduce_part,
            jnp.stack(depth_parts),
            hidden_part,
            channel_part,
        ),
        ("row", "col"),
    )
    return (
        input_grad,
        second_grad,
        third_grad,
        fourth_grad,
        linear_grads,
        summed[0],
        summed[1],
        summed[2],
        summed[3],
        summed[4],
        summed[5],
    )


def solution(mesh):
    return jax.shard_map(
        local,
        mesh=mesh,
        in_specs=(
            P("row", "col", None),
            P(),
            P(),
            P(),
            P(),
            P(),
            P("row", "col", None),
            P("row", "col", None),
            P("row", "col", None),
            P("row", "col", None),
            P("row", "col", None),
            P(),
            P(),
            P(),
            P(),
            P(),
            P(),
            P(),
            P(),
        ),
        out_specs=(
            P("row", "col", None),
            P("row", "col", None),
            P("row", "col", None),
            P("row", "col", None),
            P(("row", "col")),
            P(),
            P(),
            P(),
            P(),
            P(),
            P(),
        ),
        check_vma=False,
    )
```

profile of v0, /device:TPU:1, one launch (start us, length us, event | category | flops | bytes accessed | tf_op | source)
XLA Modules:
  0.0 377.2 jit_solution(1390378230720431153)
XLA Ops:
  8.3 8.8 %collective-permute-start.9 = (bf16[4,32,384]{2,1,0:T(8,128)(2,1)S(1)}, bf16[4,32,384]{2,1,0:T(8,128)(2,1)S(1)}, u32[]{:S(2)}, u32[]{:S(2)}) collective-permute-start(bf16[4,32,384]{2,1,0:T(8,128)(2,1)S(1)} %get-tuple-element.57), channel_id=1, source_target_pairs={{32,0},{64,32},{96,64},{128,96},{160,128},{192,160},{224,192},{256... | collective-permute-start | bytes 294920 | tf_op jit(solution)/shard_map/ppermute | solution.py:31
  17.1 1.9 collective-permute-start.8
  19.0 1.0 convert_reduce_fusion.4
  20.1 1.2 multiply_reduce_fusion
  21.3 1.2 add_convert_fusion
  23.4 1.9 collective-permute-start
  25.4 2.4 collective-permute-start.1
  28.3 1.4 convert_reduce_fusion.1
  30.5 1.3 collective-permute-start.3
  31.8 4.0 %collective-permute-start.2 = (bf16[18,1,256]{2,1,0:T(2,128)(2,1)S(1)}, bf16[18,1,256]{2,1,0:T(2,128)(2,1)S(1)}, u32[]{:S(2)}, u32[]{:S(2)}) collective-permute-start(bf16[18,1,256]{2,1,0:T(2,128)(2,1)S(1)} %get-tuple-element.66), channel_id=1, source_target_pairs={{0,1},{1,2},{2,3},{3,4},{4,5},{5,6},{6,7},{7,8},{8,9},{9,10},{10,1... | collective-permute-start | bytes 27656 | tf_op jit(solution)/shard_map/ppermute | solution.py:30
  37.9 4.2 %collective-permute-start.4 = (bf16[1,32,256]{2,1,0:T(8,128)(2,1)S(1)}, bf16[1,32,256]{2,1,0:T(8,128)(2,1)S(1)}, u32[]{:S(2)}, u32[]{:S(2)}) collective-permute-start(bf16[1,32,256]{2,1,0:T(8,128)(2,1)S(1)} %get-tuple-element.67), channel_id=1, source_target_pairs={{0,32},{32,64},{64,96},{96,128},{128,160},{160,192},{192,224},{224... | collective-permute-start | bytes 49160 | tf_op jit(solution)/shard_map/ppermute | solution.py:30
  42.1 1.9 collective-permute-start.5
  45.3 1.8 collective-permute-done.5
  47.2 1.3 collective-permute-start.6
  48.5 4.6 %collective-permute-start.7 = (bf16[18,1,256]{2,1,0:T(2,128)(2,1)S(1)}, bf16[18,1,256]{2,1,0:T(2,128)(2,1)S(1)}, u32[]{:S(2)}, u32[]{:S(2)}) collective-permute-start(bf16[18,1,256]{2,1,0:T(2,128)(2,1)S(1)} %get-tuple-element.62), channel_id=1, source_target_pairs={{0,1},{1,2},{2,3},{3,4},{4,5},{5,6},{6,7},{7,8},{8,9},{9,10},{10,1... | collective-permute-start | bytes 27656 | tf_op jit(solution)/shard_map/ppermute | solution.py:30
  56.9 3.8 collective-permute-start.10
  60.7 1.3 collective-permute-start.11
  62.4 4.3 %collective-permute-done.11 = bf16[24,4,384]{2,1,0:T(4,128)(2,1)S(1)} collective-permute-done((bf16[24,4,384]{2,1,0:T(4,128)(2,1)S(1)}, bf16[24,4,384]{2,1,0:T(4,128)(2,1)S(1)}, u32[]{:S(2)}, u32[]{:S(2)}) %collective-permute-start.11) | collective-permute-done | bytes 73760 | tf_op jit(solution)/shard_map/ppermute | solution.py:31
  72.0 1.3 pad_maximum_fusion
  73.3 113.6 %all-reduce.1 = (f32[4,384]{1,0:T(4,128)}, f32[9,256]{1,0:T(8,128)}, f32[2,256]{1,0:T(2,128)}, f32[3,64]{1,0:T(4,128)}) all-reduce(f32[4,384]{1,0:T(4,128)S(1)} %pad_maximum_fusion.14, f32[9,256]{1,0:T(8,128)S(1)} %stack.9, f32[2,256]{1,0:T(2,128)S(1)} %pad_maximum_fusion.15, ...), channel_id=1, replica_groups=mesh['row'=16,'col'=32] {'row','col'}, use_global_device_ids=true, to_apply=%region_9.10 | all-reduce | flops 4544 | bytes 36352 | tf_op jit(solution)/shard_map/psum | solution.py:251
  188.5 177.6 %all-reduce.5.cloned.1.call-done = (f32[393216]{0:T(1024)}, f32[64,256]{1,0:T(8,128)}, f32[256,64]{0,1:T(8,128)}) async-done(((f32[393216]{0:T(1024)}, f32[64,256]{1,0:T(8,128)}, f32[256,64]{0,1:T(8,128)}), (f32[393216]{0:T(1024)}, f32[64,256]{1,0:T(8,128)}, f32[256,64]{0,1:T(8,128)})) %all-reduce.5.cloned.1.call-update) | async-done | bytes 1703952
  366.1 1.4 dynamic-slice
  367.5 1.5 copy.97
  368.9 1.5 copy.98
  (143 shorter events, 17.5 us)
Async XLA Ops:
  7.2 60.8 %copy-start = (bf16[512,384]{1,0:T(8,128)(2,1)S(1)}, bf16[512,384]{1,0:T(8,128)(2,1)}, u32[]{:S(2)}) copy-start(bf16[512,384]{1,0:T(8,128)(2,1)} %param.24) | copy-start | bytes 1179652
  7.2 21.1 %copy-start.2 = (bf16[16,32,384]{2,1,0:T(8,128)(2,1)S(1)}, bf16[16,32,384]{2,1,0:T(8,128)(2,1)}, u32[]{:S(2)}) copy-start(bf16[16,32,384]{2,1,0:T(8,128)(2,1)} %param.19) | copy-start | bytes 1179652
  7.2 20.8 %copy-start.13 = (f32[9,256]{1,0:T(8,128)S(1)}, f32[9,256]{1,0:T(8,128)}, u32[]{:S(2)}) copy-start(f32[9,256]{1,0:T(8,128)} %param.34) | copy-start | bytes 27652
  7.2 20.9 %copy-start.5 = (bf16[16,32,64]{2,1,0:T(8,128)(2,1)S(1)}, bf16[16,32,64]{2,1,0:T(8,128)(2,1)}, u32[]{:S(2)}) copy-start(bf16[16,32,64]{2,1,0:T(8,128)(2,1)} %param.29) | copy-start | bytes 196612
  7.2 358.9 %all-reduce.5.cloned.1.call-start = ((), (), s32[]{:S(2)}) async-start(), calls=%async_computation | async-start | bytes 3407872
  8.3 48.5 %collective-permute-start.9 = (bf16[4,32,384]{2,1,0:T(8,128)(2,1)S(1)}, bf16[4,32,384]{2,1,0:T(8,128)(2,1)S(1)}, u32[]{:S(2)}, u32[]{:S(2)}) collective-permute-start(bf16[4,32,384]{2,1,0:T(8,128)(2,1)S(1)} %get-tuple-element.57), channel_id=1, source_target_pairs={{32,0},{64,32},{96,64},{128,96},{160,128},{192,160},{224,192},{256... | collective-permute-start | bytes 294920 | tf_op jit(solution)/shard_map/ppermute | solution.py:31
  17.1 39.6 %collective-permute-start.8 = (bf16[4,32,384]{2,1,0:T(8,128)(2,1)S(1)}, bf16[4,32,384]{2,1,0:T(8,128)(2,1)S(1)}, u32[]{:S(2)}, u32[]{:S(2)}) collective-permute-start(bf16[4,32,384]{2,1,0:T(8,128)(2,1)S(1)} %get-tuple-element.58), channel_id=1, source_target_pairs={{0,32},{32,64},{64,96},{96,128},{128,160},{160,192},{192,224},{224... | collective-permute-start | bytes 294920 | tf_op jit(solution)/shard_map/ppermute | solution.py:30
  21.3 8.5 %copy-start.9 = (bf16[64,384]{1,0:T(8,128)(2,1)S(1)}, bf16[64,384]{1,0:T(8,128)(2,1)}, u32[]{:S(2)}) copy-start(bf16[64,384]{1,0:T(8,128)(2,1)} %param.21) | copy-start | bytes 147460
  23.4 6.8 %collective-permute-start = (bf16[1,32,256]{2,1,0:T(8,128)(2,1)S(1)}, bf16[1,32,256]{2,1,0:T(8,128)(2,1)S(1)}, u32[]{:S(2)}, u32[]{:S(2)}) collective-permute-start(bf16[1,32,256]{2,1,0:T(8,128)(2,1)S(1)} %get-tuple-element.69), channel_id=1, source_target_pairs={{0,32},{32,64},{64,96},{96,128},{128,160},{160,192},{192,224},{224... | collective-permute-start | bytes 49160 | tf_op jit(solution)/shard_map/ppermute | solution.py:30
  25.4 5.1 %collective-permute-start.1 = (bf16[1,32,256]{2,1,0:T(8,128)(2,1)S(1)}, bf16[1,32,256]{2,1,0:T(8,128)(2,1)S(1)}, u32[]{:S(2)}, u32[]{:S(2)}) collective-permute-start(bf16[1,32,256]{2,1,0:T(8,128)(2,1)S(1)} %get-tuple-element.70), channel_id=1, source_target_pairs={{32,0},{64,32},{96,64},{128,96},{160,128},{192,160},{224,192},{256... | collective-permute-start | bytes 49160 | tf_op jit(solution)/shard_map/ppermute | solution.py:31
  28.2 8.1 %copy-start.12 = (bf16[2,4,512]{2,1,0:T(4,128)(2,1)S(1)}, bf16[2,4,512]{2,1,0:T(4,128)(2,1)}, u32[]{:S(2)}) copy-start(bf16[2,4,512]{2,1,0:T(4,128)(2,1)} %param.27) | copy-start | bytes 24580
  28.2 8.1 %copy-start.1 = (bf16[16,32,64]{2,1,0:T(8,128)(2,1)S(1)}, bf16[16,32,64]{2,1,0:T(8,128)(2,1)}, u32[]{:S(2)}) copy-start(bf16[16,32,64]{2,1,0:T(8,128)(2,1)} %param.28) | copy-start | bytes 196612
  30.5 6.2 %collective-permute-start.3 = (bf16[18,1,256]{2,1,0:T(2,128)(2,1)S(1)}, bf16[18,1,256]{2,1,0:T(2,128)(2,1)S(1)}, u32[]{:S(2)}, u32[]{:S(2)}) collective-permute-start(bf16[18,1,256]{2,1,0:T(2,128)(2,1)S(1)} %get-tuple-element.65), channel_id=1, source_target_pairs={{1,0},{2,1},{3,2},{4,3},{5,4},{6,5},{7,6},{8,7},{9,8},{10,9},{11,1... | collective-permute-start | bytes 27656 | tf_op jit(solution)/shard_map/ppermute | solution.py:31
  31.8 4.9 %collective-permute-start.2 = (bf16[18,1,256]{2,1,0:T(2,128)(2,1)S(1)}, bf16[18,1,256]{2,1,0:T(2,128)(2,1)S(1)}, u32[]{:S(2)}, u32[]{:S(2)}) collective-permute-start(bf16[18,1,256]{2,1,0:T(2,128)(2,1)S(1)} %get-tuple-element.66), channel_id=1, source_target_pairs={{0,1},{1,2},{2,3},{3,4},{4,5},{5,6},{6,7},{7,8},{8,9},{9,10},{10,1... | collective-permute-start | bytes 27656 | tf_op jit(solution)/shard_map/ppermute | solution.py:30
  37.9 7.4 %collective-permute-start.4 = (bf16[1,32,256]{2,1,0:T(8,128)(2,1)S(1)}, bf16[1,32,256]{2,1,0:T(8,128)(2,1)S(1)}, u32[]{:S(2)}, u32[]{:S(2)}) collective-permute-start(bf16[1,32,256]{2,1,0:T(8,128)(2,1)S(1)} %get-tuple-element.67), channel_id=1, source_target_pairs={{0,32},{32,64},{64,96},{96,128},{128,160},{160,192},{192,224},{224... | collective-permute-start | bytes 49160 | tf_op jit(solution)/shard_map/ppermute | solution.py:30
  42.1 5.1 %collective-permute-start.5 = (bf16[1,32,256]{2,1,0:T(8,128)(2,1)S(1)}, bf16[1,32,256]{2,1,0:T(8,128)(2,1)S(1)}, u32[]{:S(2)}, u32[]{:S(2)}) collective-permute-start(bf16[1,32,256]{2,1,0:T(8,128)(2,1)S(1)} %get-tuple-element.68), channel_id=1, source_target_pairs={{32,0},{64,32},{96,64},{128,96},{160,128},{192,160},{224,192},{256... | collective-permute-start | bytes 49160 | tf_op jit(solution)/shard_map/ppermute | solution.py:31
  47.2 5.9 %collective-permute-start.6 = (bf16[18,1,256]{2,1,0:T(2,128)(2,1)S(1)}, bf16[18,1,256]{2,1,0:T(2,128)(2,1)S(1)}, u32[]{:S(2)}, u32[]{:S(2)}) collective-permute-start(bf16[18,1,256]{2,1,0:T(2,128)(2,1)S(1)} %get-tuple-element.61), channel_id=1, source_target_pairs={{1,0},{2,1},{3,2},{4,3},{5,4},{6,5},{7,6},{8,7},{9,8},{10,9},{11,1... | collective-permute-start | bytes 27656 | tf_op jit(solution)/shard_map/ppermute | solution.py:31
  48.5 5.4 %collective-permute-start.7 = (bf16[18,1,256]{2,1,0:T(2,128)(2,1)S(1)}, bf16[18,1,256]{2,1,0:T(2,128)(2,1)S(1)}, u32[]{:S(2)}, u32[]{:S(2)}) collective-permute-start(bf16[18,1,256]{2,1,0:T(2,128)(2,1)S(1)} %get-tuple-element.62), channel_id=1, source_target_pairs={{0,1},{1,2},{2,3},{3,4},{4,5},{5,6},{6,7},{7,8},{8,9},{9,10},{10,1... | collective-permute-start | bytes 27656 | tf_op jit(solution)/shard_map/ppermute | solution.py:30
  56.7 10.4 %copy-start.17 = (f32[2]{0:T(128)S(1)}, f32[2]{0:T(128)}, u32[]{:S(2)}) copy-start(f32[2]{0:T(128)} %add_convert_fusion.3) | copy-start | bytes 28
  56.9 10.8 %copy-start.3 = (bf16[1536,384]{1,0:T(8,128)(2,1)S(1)}, bf16[1536,384]{1,0:T(8,128)(2,1)}, u32[]{:S(2)}) copy-start(bf16[1536,384]{1,0:T(8,128)(2,1)} %param.20) | copy-start | bytes 3538948
  56.9 5.5 %collective-permute-start.10 = (bf16[24,4,384]{2,1,0:T(4,128)(2,1)S(1)}, bf16[24,4,384]{2,1,0:T(4,128)(2,1)S(1)}, u32[]{:S(2)}, u32[]{:S(2)}) collective-permute-start(bf16[24,4,384]{2,1,0:T(4,128)(2,1)S(1)} %get-tuple-element.55), channel_id=1, source_target_pairs={{0,1},{1,2},{2,3},{3,4},{4,5},{5,6},{6,7},{7,8},{8,9},{9,10},{10,1... | collective-permute-start | bytes 221192 | tf_op jit(solution)/shard_map/ppermute | solution.py:30
  60.7 6.0 %collective-permute-start.11 = (bf16[24,4,384]{2,1,0:T(4,128)(2,1)S(1)}, bf16[24,4,384]{2,1,0:T(4,128)(2,1)S(1)}, u32[]{:S(2)}, u32[]{:S(2)}) collective-permute-start(bf16[24,4,384]{2,1,0:T(4,128)(2,1)S(1)} %get-tuple-element.56), channel_id=1, source_target_pairs={{1,0},{2,1},{3,2},{4,3},{5,4},{6,5},{7,6},{8,7},{9,8},{10,9},{11,1... | collective-permute-start | bytes 221192 | tf_op jit(solution)/shard_map/ppermute | solution.py:31
  73.2 113.7 %copy-start.4 = (bf16[320,384]{1,0:T(8,128)(2,1)S(1)}, bf16[320,384]{1,0:T(8,128)(2,1)}, u32[]{:S(2)}) copy-start(bf16[320,384]{1,0:T(8,128)(2,1)} %param.23) | copy-start | bytes 737284
  73.2 114.5 %copy-start.8 = (bf16[128,384]{1,0:T(8,128)(2,1)S(1)}, bf16[128,384]{1,0:T(8,128)(2,1)}, u32[]{:S(2)}) copy-start(bf16[128,384]{1,0:T(8,128)(2,1)} %param.22) | copy-start | bytes 294916
  (7 other events, 26.9 us)
Sparse Core Ops, SparseCore 0:
  73.4 292.6 all-reduce.4
where the time goes:
time: 378 us; the launch traced here: 377 us
  waiting for transfers between devices  185 us (49%)
  blocking collectives  114 us (30%)
  starting transfers between devices  37.3 us (10%)
  between operations  14.9 us (4%)
  matrix products  10.4 us (3%)
  other arithmetic  8.03 us (2%)
  local copies, waits for them, and re-layouts  7.98 us (2%)
    unnamed x2, waiting for transfers between devices  178 us
    psum x1, blocking collectives, local(): lax.psum((jnp.stack(bias_terms), expand_part, reduce_part, jnp.stack(dept...  114 us
    ppermute x6, starting transfers between devices, with_halo(): before = lax.ppermute(last, axis, up)  20.3 us
    ppermute x6, starting transfers between devices, with_halo(): after = lax.ppermute(initial, axis, down)  17 us
  transfers between devices with their start and end apart: 13, of which 6 were waited for; matrix products, arithmetic and copies ran while one was open for 4% of the time, Pallas kernels for 0%

commit v1 on v0

--- a/solution.py
+++ b/solution.py
@@ -79,6 +79,40 @@
     cumulative = 0.5 * (1.0 + lax.erf(conv * inv_root_two))
     density = inv_root_tau * jnp.exp(-0.5 * conv * conv)
     return (conv * cumulative, cumulative + conv * density)
+
+
+def swap_cores(shard):
+    devices = lax.axis_size("row")
+    return lax.ppermute(shard, "row", [(i, i ^ 1) for i in range(devices)])
+
+
+def sum_over_mesh(linear, small):
+    rows = lax.axis_size("row")
+    cols = lax.axis_size("col")
+    chips = rows // 2
+    core = lax.axis_index("row") % 2
+    share = -(-small.size // (rows * 128)) * 128
+    padded = jnp.pad(small, (0, rows * share - small.size)).reshape(chips, 2, share)
+    both = jnp.concatenate([linear.reshape(chips, 2, -1), padded], axis=2)
+    mine = lax.dynamic_index_in_dim(both, core, 1, False)
+    other = lax.dynamic_index_in_dim(both, 1 - core, 1, False)
+    summed = (mine + swap_cores(other)).reshape(chips, -1, 128)
+    groups = [[2 * z + c for z in range(chips)] for c in range(2)]
+    along_z = lax.all_to_all(summed, "row", 0, 0, tiled=True, axis_index_groups=groups)
+    block = jnp.sum(along_z, 0).reshape(-1)
+    lin_size = block.size - share
+    out = jnp.concatenate(
+        [
+            block[:lin_size].reshape(cols, -1),
+            jnp.broadcast_to(block[lin_size:], (cols, share)),
+        ],
+        axis=1,
+    ).reshape(cols, -1, 128)
+    along_cols = jnp.sum(lax.all_to_all(out, "col", 0, 0, tiled=True), 0).reshape(-1)
+    lin_part = along_cols[: lin_size // cols]
+    rest = jnp.broadcast_to(along_cols[lin_size // cols :].reshape(1, -1, 128), (rows, share // 128, 128))
+    everything = lax.all_to_all(rest, "row", 0, 0, tiled=True).reshape(-1)
+    return lin_part, everything[: small.size]
 
 
 def local(
@@ -169,9 +203,6 @@
         )
         bias_terms.append(jnp.sum(projection, 0, dtype=jnp.float32) * factor_scale)
         projected.append(projection)
-    linear_grads = lax.psum_scatter(
-        jnp.concatenate(weight_terms), ("row", "col"), scatter_dimension=0, tiled=True
-    )
     feature_grad = (
         jnp.dot(projected[0], linear_first.T, preferred_element_type=jnp.float32)
         + later_grad.reshape(-1, D1).astype(jnp.float32)
@@ -248,17 +279,22 @@
         .astype(jnp.bfloat16)
         .reshape(TH, TW, D1)
     )
-    summed = lax.psum(
-        (
-            jnp.stack(bias_terms),
-            expand_part,
-            reduce_part,
-            jnp.stack(depth_parts),
-            hidden_part,
-            channel_part,
-        ),
-        ("row", "col"),
-    )
+    parts = (
+        jnp.stack(bias_terms),
+        expand_part,
+        reduce_part,
+        jnp.stack(depth_parts),
+        hidden_part,
+        channel_part,
+    )
+    linear_grads, flat = sum_over_mesh(
+        jnp.concatenate(weight_terms), jnp.concatenate([part.reshape(-1) for part in parts])
+    )
+    summed = []
+    start = 0
+    for part in parts:
+        summed.append(flat[start : start + part.size].reshape(part.shape))
+        start += part.size
     return (
         input_grad,
         second_grad,

time: 378 us -> 182 us (0.48)
  waiting for transfers between devices: 185 us -> 32.2 us
  blocking collectives: 114 us -> 37.3 us
  starting transfers between devices: 37.3 us -> 65.8 us
  between operations: 14.9 us -> 2.36 us
  other arithmetic: 8.03 us -> 17.5 us
  local copies, waits for them, and re-layouts: 7.98 us -> 16.8 us
    unnamed x2 -> x0, waiting for transfers between devices: 178 us -> none
    psum x1 -> x0, blocking collectives: 114 us -> none  [local(): lax.psum((jnp.stack(bias_terms), expand_part, reduce_part, jnp.stack(dept...]
    all_to_all x0 -> x1, blocking collectives: none -> 37.3 us  [sum_over_mesh(): lax.all_to_all(summed, 'row', 0, 0, tiled=True, axis_index_groups=groups)]
    all_to_all x0 -> x2, starting transfers between devices: none -> 29.2 us  [the longest x1 21.8 us: sum_over_mesh(): lax.all_to_all(out, 'col', 0, 0, tiled=True)]
    all_to_all x0 -> x2, waiting for transfers between devices: none -> 21.3 us  [the longest x1 12.4 us: sum_over_mesh(): lax.all_to_all(out, 'col', 0, 0, tiled=True)]
    ppermute x6, starting transfers between devices: 17 us -> 13.1 us  [with_halo(): after = lax.ppermute(initial, axis, down)]
  transfers between devices with their start and end apart: 13 -> 15, of which waited for: 6 -> 8; matrix products, arithmetic and copies ran while one was open for 4% -> 13% of each run, Pallas kernels for 0% -> 0%
where the time goes in v1:
time: 182 us; the launch traced here: 181 us
  starting transfers between devices  65.8 us (36%)
  blocking collectives  37.3 us (20%)
  waiting for transfers between devices  32.2 us (18%)
  other arithmetic  17.5 us (10%)
  local copies, waits for them, and re-layouts  16.8 us (9%)
  matrix products  9.11 us (5%)
  between operations  2.36 us (1%)
    all_to_all x1, blocking collectives, sum_over_mesh(): lax.all_to_all(summed, 'row', 0, 0, tiled=True, axis_index_groups=groups)  37.3 us
    all_to_all x1, starting transfers between devices, sum_over_mesh(): lax.all_to_all(out, 'col', 0, 0, tiled=True)  21.8 us
    ppermute x6, starting transfers between devices, with_halo(): before = lax.ppermute(last, axis, up)  21.6 us
    ppermute x6, starting transfers between devices, with_halo(): after = lax.ppermute(initial, axis, down)  13.1 us
    all_to_all x1, waiting for transfers between devices, sum_over_mesh(): lax.all_to_all(out, 'col', 0, 0, tiled=True)  12.4 us
    all_to_all x1, waiting for transfers between devices, sum_over_mesh(): everything = lax.all_to_all(rest, 'row', 0, 0, tiled=True).reshape(-1)  8.97 us
    ppermute x6, waiting for transfers between devices, with_halo(): after = lax.ppermute(initial, axis, down)  7.52 us
    all_to_all x1, starting transfers between devices, sum_over_mesh(): everything = lax.all_to_all(rest, 'row', 0, 0, tiled=True).reshape(-1)  7.35 us
  transfers between devices with their start and end apart: 15, of which 8 were waited for; matrix products, arithmetic and copies ran while one was open for 13% of the time, Pallas kernels for 0%

profile of v1, /device:TPU:1, one launch (start us, length us, event | category | flops | bytes accessed | tf_op | source)
XLA Modules:
  0.0 181.1 jit_solution(5939410932619396908)
XLA Ops:
  5.2 5.4 %collective-permute-start = (bf16[1,32,256]{2,1,0:T(8,128)(2,1)S(1)}, bf16[1,32,256]{2,1,0:T(8,128)(2,1)S(1)}, u32[]{:S(2)}, u32[]{:S(2)}) collective-permute-start(bf16[1,32,256]{2,1,0:T(8,128)(2,1)S(1)} %get-tuple-element.97), channel_id=1, source_target_pairs={{0,32},{32,64},{64,96},{96,128},{128,160},{160,192},{192,224},{224... | collective-permute-start | bytes 49160 | tf_op jit(solution)/shard_map/ppermute | solution.py:30
  10.6 4.7 %collective-permute-start.1 = (bf16[1,32,256]{2,1,0:T(8,128)(2,1)S(1)}, bf16[1,32,256]{2,1,0:T(8,128)(2,1)S(1)}, u32[]{:S(2)}, u32[]{:S(2)}) collective-permute-start(bf16[1,32,256]{2,1,0:T(8,128)(2,1)S(1)} %get-tuple-element.98), channel_id=1, source_target_pairs={{32,0},{64,32},{96,64},{128,96},{160,128},{192,160},{224,192},{256... | collective-permute-start | bytes 49160 | tf_op jit(solution)/shard_map/ppermute | solution.py:31
  15.3 1.6 fusion.146
  16.9 1.9 %collective-permute-start.8 = (bf16[4,32,384]{2,1,0:T(8,128)(2,1)}, bf16[4,32,384]{2,1,0:T(8,128)(2,1)S(1)}, u32[]{:S(2)}, u32[]{:S(2)}) collective-permute-start(bf16[4,32,384]{2,1,0:T(8,128)(2,1)} %get-tuple-element.86), channel_id=1, source_target_pairs={{0,32},{32,64},{64,96},{96,128},{128,160},{160,192},{192,224},{224... | collective-permute-start | bytes 294920 | tf_op jit(solution)/shard_map/ppermute | solution.py:30
  18.8 2.4 %collective-permute-start.9 = (bf16[4,32,384]{2,1,0:T(8,128)(2,1)S(1)}, bf16[4,32,384]{2,1,0:T(8,128)(2,1)S(1)}, u32[]{:S(2)}, u32[]{:S(2)}) collective-permute-start(bf16[4,32,384]{2,1,0:T(8,128)(2,1)S(1)} %get-tuple-element.85), channel_id=1, source_target_pairs={{32,0},{64,32},{96,64},{128,96},{160,128},{192,160},{224,192},{256... | collective-permute-start | bytes 294920 | tf_op jit(solution)/shard_map/ppermute | solution.py:31
  30.6 1.4 convert_reduce_fusion.1
  33.2 1.6 collective-permute-start.2
  34.8 1.3 collective-permute-start.3
  40.6 5.1 %collective-permute-start.4 = (bf16[1,32,256]{2,1,0:T(8,128)(2,1)S(1)}, bf16[1,32,256]{2,1,0:T(8,128)(2,1)S(1)}, u32[]{:S(2)}, u32[]{:S(2)}) collective-permute-start(bf16[1,32,256]{2,1,0:T(8,128)(2,1)S(1)} %get-tuple-element.95), channel_id=1, source_target_pairs={{0,32},{32,64},{64,96},{96,128},{128,160},{160,192},{192,224},{224... | collective-permute-start | bytes 49160 | tf_op jit(solution)/shard_map/ppermute | solution.py:30
  45.7 1.9 %collective-permute-start.5 = (bf16[1,32,256]{2,1,0:T(8,128)(2,1)S(1)}, bf16[1,32,256]{2,1,0:T(8,128)(2,1)S(1)}, u32[]{:S(2)}, u32[]{:S(2)}) collective-permute-start(bf16[1,32,256]{2,1,0:T(8,128)(2,1)S(1)} %get-tuple-element.96), channel_id=1, source_target_pairs={{32,0},{64,32},{96,64},{128,96},{160,128},{192,160},{224,192},{256... | collective-permute-start | bytes 49160 | tf_op jit(solution)/shard_map/ppermute | solution.py:31
  48.4 2.4 %collective-permute-done.5 = bf16[1,32,256]{2,1,0:T(8,128)(2,1)S(1)} collective-permute-done((bf16[1,32,256]{2,1,0:T(8,128)(2,1)S(1)}, bf16[1,32,256]{2,1,0:T(8,128)(2,1)S(1)}, u32[]{:S(2)}, u32[]{:S(2)}) %collective-permute-start.5) | collective-permute-done | bytes 16416 | tf_op jit(solution)/shard_map/ppermute | solution.py:31
  50.8 1.3 collective-permute-start.6
  52.1 4.0 %collective-permute-start.7 = (bf16[18,1,256]{2,1,0:T(2,128)(2,1)S(1)}, bf16[18,1,256]{2,1,0:T(2,128)(2,1)S(1)}, u32[]{:S(2)}, u32[]{:S(2)}) collective-permute-start(bf16[18,1,256]{2,1,0:T(2,128)(2,1)S(1)} %get-tuple-element.90), channel_id=1, source_target_pairs={{0,1},{1,2},{2,3},{3,4},{4,5},{5,6},{6,7},{7,8},{8,9},{9,10},{10,1... | collective-permute-start | bytes 27656 | tf_op jit(solution)/shard_map/ppermute | solution.py:30
  59.6 3.6 %collective-permute-start.10 = (bf16[24,4,384]{2,1,0:T(4,128)(2,1)S(1)}, bf16[24,4,384]{2,1,0:T(4,128)(2,1)S(1)}, u32[]{:S(2)}, u32[]{:S(2)}) collective-permute-start(bf16[24,4,384]{2,1,0:T(4,128)(2,1)S(1)} %get-tuple-element.83), channel_id=1, source_target_pairs={{0,1},{1,2},{2,3},{3,4},{4,5},{5,6},{6,7},{7,8},{8,9},{9,10},{10,1... | collective-permute-start | bytes 221192 | tf_op jit(solution)/shard_map/ppermute | solution.py:30
  63.2 1.5 collective-permute-start.11
  65.3 4.0 %collective-permute-done.11 = bf16[24,4,384]{2,1,0:T(4,128)(2,1)S(1)} collective-permute-done((bf16[24,4,384]{2,1,0:T(4,128)(2,1)S(1)}, bf16[24,4,384]{2,1,0:T(4,128)(2,1)S(1)}, u32[]{:S(2)}, u32[]{:S(2)}) %collective-permute-start.11) | collective-permute-done | bytes 73760 | tf_op jit(solution)/shard_map/ppermute | solution.py:31
  77.6 1.5 constant_dynamic-slice_fusion.1
  79.1 2.0 %collective-permute-start.12 = (f32[8,27008]{1,0:T(8,128)S(1)}, f32[8,27008]{1,0:T(8,128)S(1)}, u32[]{:S(2)}, u32[]{:S(2)}) collective-permute-start(f32[8,27008]{1,0:T(8,128)S(1)} %bitcast.172), channel_id=1, source_target_pairs={{0,32},{32,0},{64,96},{96,64},{128,160},{160,128},{192,224},{224,1... | collective-permute-start | bytes 2592776 | tf_op jit(solution)/shard_map/ppermute | solution.py:86
  81.2 2.3 %collective-permute-done.12 = f32[8,27008]{1,0:T(8,128)S(1)} collective-permute-done((f32[8,27008]{1,0:T(8,128)S(1)}, f32[8,27008]{1,0:T(8,128)S(1)}, u32[]{:S(2)}, u32[]{:S(2)}) %collective-permute-start.12) | collective-permute-done | bytes 864288 | tf_op jit(solution)/shard_map/ppermute | solution.py:86
  83.7 37.3 %all_to_all.15 = f32[8,211,128]{2,1,0:T(8,128)S(1)} all-to-all(f32[8,211,128]{2,1,0:T(8,128)S(1)} %copy.71), channel_id=1, replica_groups={{0,64,128,192,256,320,384,448},{32,96,160,224,288,352,416,480},{1,65,12..., dimensions={0} | all-to-all | bytes 1728512 | tf_op jit(solution)/shard_map/all_to_all | solution.py:101
  122.1 21.8 %all-to-all-start.1 = ((f32[32,25,128]{2,1,0:T(8,128)}), f32[32,25,128]{2,1,0:T(8,128)S(1)}, u32[]{:S(2)}, u32[]{:S(2)}) async-start(f32[32,25,128]{2,1,0:T(8,128)} %reshape.553), calls=%async_computation.1 | async-start | bytes 1048576 | tf_op jit(solution)/shard_map/all_to_all | solution.py:111
  146.3 12.4 %all-to-all-done.1 = f32[32,25,128]{2,1,0:T(8,128)S(1)} async-done(((f32[32,25,128]{2,1,0:T(8,128)}), f32[32,25,128]{2,1,0:T(8,128)S(1)}, u32[]{:S(2)}, u32[]{:S(2)}) %all-to-all-start.1) | async-done | bytes 409632 | tf_op jit(solution)/shard_map/all_to_all | solution.py:111
  159.5 7.3 %all-to-all-start.2 = ((f32[16,19,128]{2,1,0:T(8,128)}), f32[16,19,128]{2,1,0:T(8,128)S(1)}, u32[]{:S(2)}, u32[]{:S(2)}) async-start(f32[16,19,128]{2,1,0:T(8,128)} %broadcast_in_dim.181), calls=%async_computation.2 | async-start | bytes 393216 | tf_op jit(solution)/shard_map/all_to_all | solution.py:114
  168.2 9.0 %all-to-all-done.2 = f32[16,19,128]{2,1,0:T(8,128)S(1)} async-done(((f32[16,19,128]{2,1,0:T(8,128)}), f32[16,19,128]{2,1,0:T(8,128)S(1)}, u32[]{:S(2)}, u32[]{:S(2)}) %all-to-all-start.2) | async-done | bytes 155680 | tf_op jit(solution)/shard_map/all_to_all | solution.py:114
  (278 shorter events, 41.1 us)
Async XLA Ops:
  0.6 144.1 %copy-start = (bf16[512,384]{1,0:T(8,128)(2,1)S(1)}, bf16[512,384]{1,0:T(8,128)(2,1)}, u32[]{:S(2)}) copy-start(bf16[512,384]{1,0:T(8,128)(2,1)} %param.24) | copy-start | bytes 1179652
  0.7 29.9 %copy-start.2 = (bf16[16,32,384]{2,1,0:T(8,128)(2,1)S(1)}, bf16[16,32,384]{2,1,0:T(8,128)(2,1)}, u32[]{:S(2)}) copy-start(bf16[16,32,384]{2,1,0:T(8,128)(2,1)} %param.19) | copy-start | bytes 1179652
  0.7 27.5 %copy-start.29 = (f32[9,256]{1,0:T(8,128)S(1)}, f32[9,256]{1,0:T(8,128)}, u32[]{:S(2)}) copy-start(f32[9,256]{1,0:T(8,128)} %param.34) | copy-start | bytes 27652
  0.7 27.5 %copy-start.11 = (bf16[16,32,64]{2,1,0:T(8,128)(2,1)S(1)}, bf16[16,32,64]{2,1,0:T(8,128)(2,1)}, u32[]{:S(2)}) copy-start(bf16[16,32,64]{2,1,0:T(8,128)(2,1)} %param.29) | copy-start | bytes 196612
  4.2 27.9 %copy-start.15 = (bf16[64,384]{1,0:T(8,128)(2,1)S(1)}, bf16[64,384]{1,0:T(8,128)(2,1)}, u32[]{:S(2)}) copy-start(bf16[64,384]{1,0:T(8,128)(2,1)} %param.21) | copy-start | bytes 147460
  5.2 27.2 %copy-start.12 = (bf16[256,64]{0,1:T(8,128)(2,1)S(1)}, bf16[256,64]{0,1:T(8,128)(2,1)}, u32[]{:S(2)}) copy-start(bf16[256,64]{0,1:T(8,128)(2,1)} %param.36) | copy-start | bytes 98308
  5.2 28.0 %collective-permute-start = (bf16[1,32,256]{2,1,0:T(8,128)(2,1)S(1)}, bf16[1,32,256]{2,1,0:T(8,128)(2,1)S(1)}, u32[]{:S(2)}, u32[]{:S(2)}) collective-permute-start(bf16[1,32,256]{2,1,0:T(8,128)(2,1)S(1)} %get-tuple-element.97), channel_id=1, source_target_pairs={{0,32},{32,64},{64,96},{96,128},{128,160},{160,192},{192,224},{224... | collective-permute-start | bytes 49160 | tf_op jit(solution)/shard_map/ppermute | solution.py:30
  10.6 22.6 %collective-permute-start.1 = (bf16[1,32,256]{2,1,0:T(8,128)(2,1)S(1)}, bf16[1,32,256]{2,1,0:T(8,128)(2,1)S(1)}, u32[]{:S(2)}, u32[]{:S(2)}) collective-permute-start(bf16[1,32,256]{2,1,0:T(8,128)(2,1)S(1)} %get-tuple-element.98), channel_id=1, source_target_pairs={{32,0},{64,32},{96,64},{128,96},{160,128},{192,160},{224,192},{256... | collective-permute-start | bytes 49160 | tf_op jit(solution)/shard_map/ppermute | solution.py:31
  16.9 42.5 %collective-permute-start.8 = (bf16[4,32,384]{2,1,0:T(8,128)(2,1)}, bf16[4,32,384]{2,1,0:T(8,128)(2,1)S(1)}, u32[]{:S(2)}, u32[]{:S(2)}) collective-permute-start(bf16[4,32,384]{2,1,0:T(8,128)(2,1)} %get-tuple-element.86), channel_id=1, source_target_pairs={{0,32},{32,64},{64,96},{96,128},{128,160},{160,192},{192,224},{224... | collective-permute-start | bytes 294920 | tf_op jit(solution)/shard_map/ppermute | solution.py:30
  18.8 40.7 %collective-permute-start.9 = (bf16[4,32,384]{2,1,0:T(8,128)(2,1)S(1)}, bf16[4,32,384]{2,1,0:T(8,128)(2,1)S(1)}, u32[]{:S(2)}, u32[]{:S(2)}) collective-permute-start(bf16[4,32,384]{2,1,0:T(8,128)(2,1)S(1)} %get-tuple-element.85), channel_id=1, source_target_pairs={{32,0},{64,32},{96,64},{128,96},{160,128},{192,160},{224,192},{256... | collective-permute-start | bytes 294920 | tf_op jit(solution)/shard_map/ppermute | solution.py:31
  33.2 4.9 %collective-permute-start.2 = (bf16[18,1,256]{2,1,0:T(2,128)(2,1)S(1)}, bf16[18,1,256]{2,1,0:T(2,128)(2,1)S(1)}, u32[]{:S(2)}, u32[]{:S(2)}) collective-permute-start(bf16[18,1,256]{2,1,0:T(2,128)(2,1)S(1)} %get-tuple-element.94), channel_id=1, source_target_pairs={{0,1},{1,2},{2,3},{3,4},{4,5},{5,6},{6,7},{7,8},{8,9},{9,10},{10,1... | collective-permute-start | bytes 27656 | tf_op jit(solution)/shard_map/ppermute | solution.py:30
  34.8 4.5 %collective-permute-start.3 = (bf16[18,1,256]{2,1,0:T(2,128)(2,1)S(1)}, bf16[18,1,256]{2,1,0:T(2,128)(2,1)S(1)}, u32[]{:S(2)}, u32[]{:S(2)}) collective-permute-start(bf16[18,1,256]{2,1,0:T(2,128)(2,1)S(1)} %get-tuple-element.93), channel_id=1, source_target_pairs={{1,0},{2,1},{3,2},{4,3},{5,4},{6,5},{7,6},{8,7},{9,8},{10,9},{11,1... | collective-permute-start | bytes 27656 | tf_op jit(solution)/shard_map/ppermute | solution.py:31
  40.6 7.8 %collective-permute-start.4 = (bf16[1,32,256]{2,1,0:T(8,128)(2,1)S(1)}, bf16[1,32,256]{2,1,0:T(8,128)(2,1)S(1)}, u32[]{:S(2)}, u32[]{:S(2)}) collective-permute-start(bf16[1,32,256]{2,1,0:T(8,128)(2,1)S(1)} %get-tuple-element.95), channel_id=1, source_target_pairs={{0,32},{32,64},{64,96},{96,128},{128,160},{160,192},{192,224},{224... | collective-permute-start | bytes 49160 | tf_op jit(solution)/shard_map/ppermute | solution.py:30
  45.7 5.1 %collective-permute-start.5 = (bf16[1,32,256]{2,1,0:T(8,128)(2,1)S(1)}, bf16[1,32,256]{2,1,0:T(8,128)(2,1)S(1)}, u32[]{:S(2)}, u32[]{:S(2)}) collective-permute-start(bf16[1,32,256]{2,1,0:T(8,128)(2,1)S(1)} %get-tuple-element.96), channel_id=1, source_target_pairs={{32,0},{64,32},{96,64},{128,96},{160,128},{192,160},{224,192},{256... | collective-permute-start | bytes 49160 | tf_op jit(solution)/shard_map/ppermute | solution.py:31
  50.8 5.6 %collective-permute-start.6 = (bf16[18,1,256]{2,1,0:T(2,128)(2,1)S(1)}, bf16[18,1,256]{2,1,0:T(2,128)(2,1)S(1)}, u32[]{:S(2)}, u32[]{:S(2)}) collective-permute-start(bf16[18,1,256]{2,1,0:T(2,128)(2,1)S(1)} %get-tuple-element.89), channel_id=1, source_target_pairs={{1,0},{2,1},{3,2},{4,3},{5,4},{6,5},{7,6},{8,7},{9,8},{10,9},{11,1... | collective-permute-start | bytes 27656 | tf_op jit(solution)/shard_map/ppermute | solution.py:31
  52.1 4.9 %collective-permute-start.7 = (bf16[18,1,256]{2,1,0:T(2,128)(2,1)S(1)}, bf16[18,1,256]{2,1,0:T(2,128)(2,1)S(1)}, u32[]{:S(2)}, u32[]{:S(2)}) collective-permute-start(bf16[18,1,256]{2,1,0:T(2,128)(2,1)S(1)} %get-tuple-element.90), channel_id=1, source_target_pairs={{0,1},{1,2},{2,3},{3,4},{4,5},{5,6},{6,7},{7,8},{8,9},{9,10},{10,1... | collective-permute-start | bytes 27656 | tf_op jit(solution)/shard_map/ppermute | solution.py:30
  59.6 5.7 %collective-permute-start.10 = (bf16[24,4,384]{2,1,0:T(4,128)(2,1)S(1)}, bf16[24,4,384]{2,1,0:T(4,128)(2,1)S(1)}, u32[]{:S(2)}, u32[]{:S(2)}) collective-permute-start(bf16[24,4,384]{2,1,0:T(4,128)(2,1)S(1)} %get-tuple-element.83), channel_id=1, source_target_pairs={{0,1},{1,2},{2,3},{3,4},{4,5},{5,6},{6,7},{7,8},{8,9},{9,10},{10,1... | collective-permute-start | bytes 221192 | tf_op jit(solution)/shard_map/ppermute | solution.py:30
  63.2 6.1 %collective-permute-start.11 = (bf16[24,4,384]{2,1,0:T(4,128)(2,1)S(1)}, bf16[24,4,384]{2,1,0:T(4,128)(2,1)S(1)}, u32[]{:S(2)}, u32[]{:S(2)}) collective-permute-start(bf16[24,4,384]{2,1,0:T(4,128)(2,1)S(1)} %get-tuple-element.84), channel_id=1, source_target_pairs={{1,0},{2,1},{3,2},{4,3},{5,4},{6,5},{7,6},{8,7},{9,8},{10,9},{11,1... | collective-permute-start | bytes 221192 | tf_op jit(solution)/shard_map/ppermute | solution.py:31
  79.1 4.3 %collective-permute-start.12 = (f32[8,27008]{1,0:T(8,128)S(1)}, f32[8,27008]{1,0:T(8,128)S(1)}, u32[]{:S(2)}, u32[]{:S(2)}) collective-permute-start(f32[8,27008]{1,0:T(8,128)S(1)} %bitcast.172), channel_id=1, source_target_pairs={{0,32},{32,0},{64,96},{96,64},{128,160},{160,128},{192,224},{224,1... | collective-permute-start | bytes 2592776 | tf_op jit(solution)/shard_map/ppermute | solution.py:86
  121.1 24.4 %copy-start.5 = (bf16[128,384]{1,0:T(8,128)(2,1)S(1)}, bf16[128,384]{1,0:T(8,128)(2,1)}, u32[]{:S(2)}) copy-start(bf16[128,384]{1,0:T(8,128)(2,1)} %copy-done.4) | copy-start | bytes 294916
  122.1 44.7 %copy-start.8 = (bf16[320,384]{1,0:T(8,128)(2,1)S(1)}, bf16[320,384]{1,0:T(8,128)(2,1)}, u32[]{:S(2)}) copy-start(bf16[320,384]{1,0:T(8,128)(2,1)} %param.23) | copy-start | bytes 737284
  122.1 44.7 %copy-start.10 = (bf16[32,384]{1,0:T(8,128)(2,1)S(1)}, bf16[32,384]{1,0:T(8,128)(2,1)}, u32[]{:S(2)}) copy-start(bf16[32,384]{1,0:T(8,128)(2,1)} %copy-done.9) | copy-start | bytes 73732
  122.1 36.6 %all-to-all-start.1 = ((f32[32,25,128]{2,1,0:T(8,128)}), f32[32,25,128]{2,1,0:T(8,128)S(1)}, u32[]{:S(2)}, u32[]{:S(2)}) async-start(f32[32,25,128]{2,1,0:T(8,128)} %reshape.553), calls=%async_computation.1 | async-start | bytes 1048576 | tf_op jit(solution)/shard_map/all_to_all | solution.py:111
  159.5 17.7 %all-to-all-start.2 = ((f32[16,19,128]{2,1,0:T(8,128)}), f32[16,19,128]{2,1,0:T(8,128)S(1)}, u32[]{:S(2)}, u32[]{:S(2)}) async-start(f32[16,19,128]{2,1,0:T(8,128)} %broadcast_in_dim.181), calls=%async_computation.2 | async-start | bytes 393216 | tf_op jit(solution)/shard_map/all_to_all | solution.py:114
  (54 other events, 343.7 us)

commit v2 on v0

v2 whole, which is shorter than its diff:
```python
import functools
import math

import jax
import jax.numpy as jnp
from jax import lax
from jax.experimental import pallas as pl
from jax.experimental.pallas import tpu as pltpu
from jax.sharding import PartitionSpec as P

D1 = 64
D2 = 128
D3 = 320
D4 = 512
HID = 256
DEC = 384
TH = 16
TW = 32

EDGE = 4
ROWS = TH + 2 * EDGE
PITCH = 48
GROUP = 2 * EDGE
COARSE = (128, 32, 8)
BLOCK = 192
SHARE = 24

norm_eps = 1e-06
inv_root_two = 0.7071067811865476
inv_root_tau = 0.3989422804014327


def nt(left, right):
    return lax.dot_general(left, right, (((1,), (1,)), ((), ())), preferred_element_type=jnp.float32)


def tn(left, right):
    return lax.dot_general(left, right, (((0,), (0,)), ((), ())), preferred_element_type=jnp.float32)


def nn(left, right):
    return jnp.dot(left, right, preferred_element_type=jnp.float32)


def place(position):
    row = jnp.floor((position + 0.5) * (1.0 / PITCH))
    col = position - PITCH * row
    return row - EDGE, jnp.where(col < 40.0, col, col - PITCH)


def pool_matrix(scale_index, row_index, col_index, height, width):
    factor = 2**scale_index
    coarse_rows, coarse_cols = TH // factor, TW // factor
    count = coarse_rows * coarse_cols
    position = lax.broadcasted_iota(jnp.int32, (1, ROWS * PITCH), 1).astype(jnp.float32)
    row, col = place(position)
    target = lax.broadcasted_iota(jnp.int32, (count, 1), 0).astype(jnp.float32)
    target_row = jnp.floor((target + 0.5) * (1.0 / coarse_cols))
    target_col = target - coarse_cols * target_row
    row0 = (row_index * TH).astype(jnp.float32)
    col0 = (col_index * TW).astype(jnp.float32)
    at_row = jnp.clip((row + row0 + 0.5) * (1.0 / factor) - 0.5, 0.0, height // factor - 1.0)
    at_col = jnp.clip((col + col0 + 0.5) * (1.0 / factor) - 0.5, 0.0, width // factor - 1.0)
    at_row = at_row - row0 * (1.0 / factor)
    at_col = at_col - col0 * (1.0 / factor)
    weight = jnp.maximum(1.0 - jnp.abs(at_row - target_row), 0.0) * jnp.maximum(
        1.0 - jnp.abs(at_col - target_col), 0.0
    )
    return weight.astype(jnp.bfloat16)


def tile_kernel(
    height,
    width,
    joined_ref,
    pair_ref,
    top_ref,
    bottom_ref,
    side_ref,
    join_ref,
    first_ref,
    second_ref,
    third_ref,
    fourth_ref,
    feature2_ref,
    feature3_ref,
    feature4_ref,
    gain_ref,
    shift_ref,
    expand_ref,
    expand_bias_ref,
    depth_ref,
    depth_bias_ref,
    reduce_ref,
    reduce_bias_ref,
    input_grad_ref,
    grad2_ref,
    grad3_ref,
    grad4_ref,
    mine_ref,
    other_ref,
    wide_ref,
    wide_pair_ref,
    hid_ref,
    hid_before_ref,
    hid_after_ref,
    slope_ref,
    act_ref,
    pre_ref,
    pre_before_ref,
    pre_after_ref,
    hgrad_ref,
    linear_ref,
    rest_ref,
):
    row_index = lax.axis_index("row")
    col_index = lax.axis_index("col")
    scale_base = 1.0 / math.sqrt(height * width)

    wide_ref[EDGE : EDGE + TH, 0:TW] = joined_ref[...]
    wide_ref[0:EDGE, 0:TW] = top_ref[:, :, 0:DEC]
    wide_ref[EDGE + TH :, 0:TW] = bottom_ref[:, :, 0:DEC]
    wide_ref[:, TW:] = side_ref[:, :, 0:DEC]
    wide_pair_ref[EDGE : EDGE + TH, 0:TW] = pair_ref[...]
    wide_pair_ref[0:EDGE, 0:TW] = top_ref[:, :, DEC:]
    wide_pair_ref[EDGE + TH :, 0:TW] = bottom_ref[:, :, DEC:]
    wide_pair_ref[:, TW:] = side_ref[:, :, DEC:]
    rest_ref[...] = jnp.zeros_like(rest_ref)

    def keep_row(row, value):
        for piece in range(value.shape[1] // 128):
            rest_ref[row + piece : row + piece + 1, :] = value[:, 128 * piece : 128 * piece + 128]

    matrix = jnp.concatenate(
        [pool_matrix(k, row_index, col_index, height, width) for k in (1, 2, 3)], axis=0
    )
    pooled = nn(matrix, wide_ref[...].reshape(ROWS * PITCH, DEC)).astype(jnp.bfloat16)
    start = 0
    base = D1
    for k, linear, feature, grad in (
        (1, second_ref, feature2_ref, grad2_ref),
        (2, third_ref, feature3_ref, grad3_ref),
        (3, fourth_ref, feature4_ref, grad4_ref),
    ):
        count = COARSE[k - 1]
        channels = linear.shape[0]
        projection = nt(pooled[start : start + count], join_ref[k * DEC : (k + 1) * DEC, :]).astype(
            jnp.bfloat16
        )
        grad[...] = nt(projection, linear[...]).astype(jnp.bfloat16)
        linear_ref[base : base + channels, :] = tn(feature[...], projection) * (2**k * scale_base)
        keep_row(
            3 * k,
            jnp.sum(projection.astype(jnp.float32), 0, keepdims=True) * (2**k * scale_base),
        )
        start += count
        base += channels

    values = wide_pair_ref[2:22, :, 0:D1].reshape(20 * PITCH, D1).astype(jnp.float32)
    center = jnp.mean(values, -1, keepdims=True)
    offset = values - center
    spread = jnp.mean(jnp.square(offset), -1, keepdims=True)
    scaling = lax.rsqrt(spread + norm_eps)
    standard = offset * scaling
    normed = (standard * gain_ref[...] + shift_ref[...]).astype(jnp.bfloat16)

    def inside(first, rows):
        position = lax.broadcasted_iota(jnp.int32, (rows * PITCH, 1), 0).astype(jnp.float32)
        row, col = place(position + first * PITCH)
        row = row + (row_index * TH).astype(jnp.float32)
        col = col + (col_index * TW).astype(jnp.float32)
        good = (row >= 0.0) & (row < height) & (col >= 0.0) & (col < width)
        return jnp.where(good, 1.0, 0.0)

    hidden = (nn(normed, expand_ref[...]) + expand_bias_ref[...]).astype(jnp.bfloat16)
    hid_ref[...] = (hidden.astype(jnp.float32) * inside(2, 20)).reshape(20, PITCH, HID)

    def shift_hidden(i, carry):
        row = hid_ref[i]
        hid_before_ref[i] = pltpu.roll(row, 1, 0)
        hid_after_ref[i] = pltpu.roll(row, PITCH - 1, 0)
        return carry

    lax.fori_loop(0, 20, shift_hidden, 0)
    hid_refs = (hid_before_ref, hid_ref, hid_after_ref)

    def conv_row(i, carry):
        conv = jnp.broadcast_to(depth_bias_ref[...], (PITCH, HID))
        for a in range(3):
            for b in range(3):
                conv = conv + depth_ref[3 * a + b : 3 * a + b + 1, :] * hid_refs[b][i + a]
        cumulative = 0.5 * (1.0 + lax.erf(conv * inv_root_two))
        density = inv_root_tau * jnp.exp(-0.5 * conv * conv)
        act_ref[i] = (conv * cumulative).astype(jnp.bfloat16)
        slope_ref[i] = cumulative + conv * density
        return carry

    lax.fori_loop(0, 18, conv_row, 0)

    def own(value, rows):
        first = (rows - TH) // 2
        channels = value.shape[-1]
        return value.reshape(rows, PITCH, channels)[first : first + TH, 0:TW].reshape(
            TH * TW, channels
        )

    projection = nt(wide_ref[3:21].reshape(18 * PITCH, DEC), join_ref[0:DEC, :]).astype(jnp.bfloat16)
    later = wide_pair_ref[3:21, :, D1:].reshape(18 * PITCH, D1).astype(jnp.float32)
    feature_grad = (nt(projection, first_ref[...]) + later).astype(jnp.bfloat16)
    act_grad = nt(feature_grad, reduce_ref[...])
    pre_grad = (act_grad * slope_ref[...].reshape(18 * PITCH, HID)).astype(jnp.bfloat16)
    pre_ref[...] = (pre_grad.astype(jnp.float32) * inside(3, 18)).reshape(18, PITCH, HID)

    activated = act_ref[1:17, 0:TW, :].reshape(TH * TW, HID)
    own_projection = own(projection, 18)
    own_grad = own(feature_grad, 18)
    own_block = pair_ref[:, :, 0:D1].reshape(TH * TW, D1).astype(jnp.float32)
    features = (own_block + (nn(activated, reduce_ref[...]) + reduce_bias_ref[...])).astype(
        jnp.bfloat16
    )
    linear_ref[0:D1, :] = tn(features, own_projection) * scale_base
    keep_row(0, jnp.sum(own_projection.astype(jnp.float32), 0, keepdims=True) * scale_base)
    reduce_part = tn(own_grad, activated) * scale_base

    def shift_pre(i, carry):
        row = pre_ref[i]
        pre_before_ref[i] = pltpu.roll(row, 1, 0)
        pre_after_ref[i] = pltpu.roll(row, PITCH - 1, 0)
        return carry

    lax.fori_loop(0, 18, shift_pre, 0)
    pre_refs = (pre_after_ref, pre_ref, pre_before_ref)

    def fold(value):
        return jnp.sum(value.reshape(TW // 8, 8, HID), 0)

    def grad_row(i, sums):
        total = jnp.zeros((TW, HID), jnp.float32)
        center_row = pre_ref[i + 1, 0:TW, :]
        taps = []
        for a in range(3):
            for b in range(3):
                tap = 3 * a + b
                total = total + depth_ref[tap : tap + 1, :] * pre_refs[b][i + 2 - a, 0:TW, :]
                taps.append(sums[tap] + fold(hid_refs[b][i + 1 + a, 0:TW, :] * center_row))
        rounded = total.astype(jnp.bfloat16)
        hgrad_ref[i] = rounded
        taps.append(sums[9] + fold(rounded.astype(jnp.float32)))
        taps.append(sums[10] + fold(center_row))
        return tuple(taps)

    sums = lax.fori_loop(0, TH, grad_row, (jnp.zeros((8, HID), jnp.float32),) * 11)
    for n in range(11):
        keep_row(12 + 2 * n, jnp.sum(sums[n], 0, keepdims=True) * scale_base)

    hidden_grad = hgrad_ref[...].reshape(TH * TW, HID)
    own_normed = own(normed, 20)
    own_standard = own(standard, 20)
    own_scaling = own(jnp.broadcast_to(scaling, (20 * PITCH, D1)), 20)
    expand_part = tn(own_normed, hidden_grad) * scale_base
    normed_grad = nt(hidden_grad, expand_ref[...])
    fgrad = own_grad.astype(jnp.float32)
    for n, value in enumerate((fgrad, normed_grad * own_standard, normed_grad)):
        rest_ref[34 + n : 35 + n, 0:D1] = jnp.sum(value, 0, keepdims=True) * scale_base
    scaled = normed_grad * gain_ref[...]
    input_grad = fgrad + own_scaling * (
        scaled
        - jnp.mean(scaled, -1, keepdims=True)
        - own_standard * jnp.mean(scaled * own_standard, -1, keepdims=True)
    )
    input_grad_ref[...] = input_grad.astype(jnp.bfloat16).reshape(TH, TW, D1)

    def block_rows(r):
        pieces = [linear_ref[64 * r : 64 * r + 64, 128 * j : 128 * j + 128] for j in range(3)]
        lanes = slice(0, 128) if r < 8 else slice(128, 256)
        first = 8 * (r % 8)
        pieces.append(expand_part[first : first + 8, lanes])
        pieces.append(reduce_part[first : first + 8, lanes])
        pieces.append(rest_ref[8 * r : 8 * r + 8, :])
        return pieces

    even_core = row_index % 2 == 0
    for z in range(8):
        at = 0
        for even, odd in zip(block_rows(2 * z), block_rows(2 * z + 1)):
            size = even.shape[0]
            mine_ref[z, at : at + size, :] = jnp.where(even_core, even, odd)
            other_ref[z, at : at + size, :] = jnp.where(even_core, odd, even)
            at += size


def tile_pass(height, width, *operands):
    sds = jax.ShapeDtypeStruct
    bf16, f32 = jnp.bfloat16, jnp.float32
    vmem = pltpu.VMEM
    return pl.pallas_call(
        functools.partial(tile_kernel, height, width),
        out_shape=(
            sds((TH, TW, D1), bf16),
            sds((COARSE[0], D2), bf16),
            sds((COARSE[1], D3), bf16),
            sds((COARSE[2], D4), bf16),
            sds((8, BLOCK + SHARE, 128), f32),
            sds((8, BLOCK + SHARE, 128), f32),
        ),
        in_specs=[pl.BlockSpec(memory_space=vmem)] * len(operands),
        out_specs=(pl.BlockSpec(memory_space=vmem),) * 6,
        scratch_shapes=[
            vmem((ROWS, PITCH, DEC), bf16),
            vmem((ROWS, PITCH, 2 * D1), bf16),
            vmem((20, PITCH, HID), f32),
            vmem((20, PITCH, HID), f32),
            vmem((20, PITCH, HID), f32),
            vmem((18, PITCH, HID), f32),
            vmem((18, PITCH, HID), bf16),
            vmem((18, PITCH, HID), f32),
            vmem((18, PITCH, HID), f32),
            vmem((18, PITCH, HID), f32),
            vmem((TH, TW, HID), bf16),
            vmem((D1 + D2 + D3 + D4, DEC), f32),
            vmem((128, 128), f32),
        ],
        compiler_params=pltpu.CompilerParams(vmem_limit_bytes=50 * 2**20),
        name="tile_pass",
    )(*operands)


def column_kernel(received_ref, out_ref, total_ref):
    total_ref[...] = jnp.sum(received_ref[...], 0)
    share = total_ref[BLOCK:, :]
    empty = jnp.zeros((2, 128), jnp.float32)
    for c in range(out_ref.shape[0]):
        for j in range(3):
            out_ref[c, 2 * j : 2 * j + 2, :] = total_ref[64 * j + 2 * c : 64 * j + 2 * c + 2, :]
        out_ref[c, 6:8, :] = empty
        out_ref[c, 8:, :] = share


def final_kernel(received_ref, linear_ref, out_ref):
    total = jnp.sum(received_ref[...], 0)
    for p in range(2):
        for j in range(3):
            linear_ref[3 * p + j : 3 * p + j + 1, :] = total[2 * j + p : 2 * j + p + 1, :]
    for r in range(out_ref.shape[0]):
        out_ref[r] = total[8:]


def small_kernel(all_ref, biases_ref, expand_ref, reduce_ref, depth_ref, hidden_ref, channel_ref, turn_ref):
    for r in range(16):
        lanes = slice(0, 128) if r < 8 else slice(128, 256)
        first = 8 * (r % 8)
        expand_ref[first : first + 8, lanes] = all_ref[r, 0:8, :]
        turn_ref[first : first + 8, lanes] = all_ref[r, 8:16, :]
    reduce_ref[...] = turn_ref[...].T

    def row(n):
        return all_ref[n // 8, 16 + n % 8 : 17 + n % 8, :]

    for k in range(4):
        for j in range(3):
            biases_ref[k : k + 1, 128 * j : 128 * j + 128] = row(3 * k + j)
    for t in range(9):
        for j in range(2):
            depth_ref[t : t + 1, 128 * j : 128 * j + 128] = row(12 + 2 * t + j)
    for t in range(2):
        for j in range(2):
            hidden_ref[t : t + 1, 128 * j : 128 * j + 128] = row(30 + 2 * t + j)
    for t in range(3):
        channel_ref[t : t + 1, :] = row(34 + t)[:, 0:D1]


def sum_over_mesh(mine, other):
    rows = lax.axis_size("row")
    cols = lax.axis_size("col")
    chips = rows // 2
    sds = jax.ShapeDtypeStruct
    f32 = jnp.float32
    received = lax.ppermute(other, "row", [(i, i ^ 1) for i in range(rows)])
    groups = [[2 * z + c for z in range(chips)] for c in range(2)]
    along_z = lax.all_to_all(mine + received, "row", 0, 0, tiled=True, axis_index_groups=groups)
    parts = pl.pallas_call(
        column_kernel,
        out_shape=sds((cols, 8 + SHARE, 128), f32),
        scratch_shapes=[pltpu.VMEM((BLOCK + SHARE, 128), f32)],
        name="column_parts",
    )(along_z)
    along_cols = lax.all_to_all(parts, "col", 0, 0, tiled=True)
    linear, share = pl.pallas_call(
        final_kernel,
        out_shape=(sds((6, 128), f32), sds((rows, SHARE, 128), f32)),
        name="final_sums",
    )(along_cols)
    everything = lax.all_to_all(share, "row", 0, 0, tiled=True)
    small = pl.pallas_call(
        small_kernel,
        out_shape=(
            sds((4, DEC), f32),
            sds((D1, HID), f32),
            sds((HID, D1), f32),
            sds((9, HID), f32),
            sds((2, HID), f32),
            sds((3, D1), f32),
        ),
        scratch_shapes=[pltpu.VMEM((D1, HID), f32)],
        name="small_sums",
    )(everything)
    return linear.reshape(-1), small


def swap_edges(before_edge, after_edge, axis):
    devices = lax.axis_size(axis)
    up = [(i, i + 1) for i in range(devices - 1)]
    down = [(j, i) for i, j in up]
    return lax.ppermute(after_edge, axis, up), lax.ppermute(before_edge, axis, down)


def local(
    joined_grad,
    join_weight,
    linear_first,
    linear_second,
    linear_third,
    linear_fourth,
    feature_second,
    feature_third,
    feature_fourth,
    block_input,
    later_grad,
    norm_gain,
    norm_shift,
    expand_weight,
    expand_bias,
    depth_weight,
    depth_bias,
    reduce_weight,
    reduce_bias,
):
    height = TH * lax.axis_size("row")
    width = TW * lax.axis_size("col")
    pair = jnp.concatenate([block_input, later_grad], axis=2)

    def lines(rows, cols):
        return jnp.concatenate([joined_grad[rows, cols], pair[rows, cols]], axis=2)

    everything = slice(None)
    top, bottom = swap_edges(
        lines(slice(0, EDGE), everything), lines(slice(TH - EDGE, TH), everything), "row"
    )

    def columns(cols):
        return jnp.concatenate([top[:, cols], lines(everything, cols), bottom[:, cols]], axis=0)

    left, right = swap_edges(columns(slice(0, EDGE)), columns(slice(TW - EDGE, TW)), "col")
    gap = jnp.zeros((ROWS, PITCH - TW - 2 * EDGE, left.shape[2]), left.dtype)
    side = jnp.concatenate([right, gap, left], axis=1)

    input_grad, grad2, grad3, grad4, mine, other = tile_pass(
        height,
        width,
        joined_grad,
        pair,
        top,
        bottom,
        side,
        join_weight,
        linear_first,
        linear_second,
        linear_third,
        linear_fourth,
        feature_second.reshape(-1, D2),
        feature_third.reshape(-1, D3),
        feature_fourth.reshape(-1, D4),
        norm_gain.reshape(1, -1),
        norm_shift.reshape(1, -1),
        expand_weight,
        expand_bias.reshape(1, -1),
        depth_weight,
        depth_bias.reshape(1, -1),
        reduce_weight,
        reduce_bias.reshape(1, -1),
    )
    linear_grads, small = sum_over_mesh(mine, other)
    return (
        input_grad,
        grad2.reshape(TH // 2, TW // 2, D2),
        grad3.reshape(TH // 4, TW // 4, D3),
        grad4.reshape(TH // 8, TW // 8, D4),
        linear_grads,
        *small,
    )


def solution(mesh):
    tiles = P("row", "col", None)
    return jax.shard_map(
        local,
        mesh=mesh,
        in_specs=(tiles,) + (P(),) * 5 + (tiles,) * 5 + (P(),) * 8,
        out_specs=(tiles,) * 4 + (P(("row", "col")),) + (P(),) * 6,
        check_vma=False,
    )
```

time: 378 us -> 124 us (0.33)
  waiting for transfers between devices: 185 us -> 17.3 us
  blocking collectives: 114 us -> 61.3 us
  between operations: 14.9 us -> 1.06 us
  Pallas kernels: 0 us -> 13.7 us
  starting transfers between devices: 37.3 us -> 23.9 us
  matrix products: 10.4 us -> 0 us
  other arithmetic: 8.03 us -> 1.49 us
    unnamed x2 -> x0, waiting for transfers between devices: 178 us -> none
    psum x1 -> x0, blocking collectives: 114 us -> none  [local(): lax.psum((jnp.stack(bias_terms), expand_part, reduce_part, jnp.stack(dept...]
    all_to_all x0 -> x2, blocking collectives: none -> 61.3 us  [the longest x1 34.7 us: sum_over_mesh(): lax.all_to_all(mine + received, 'row', 0, 0, tiled=True, axis_index_group...]
    ppermute x12 -> x5, starting transfers between devices: 37.3 us -> 16.5 us  [the longest x2 8.51 us: swap_edges(): lax.ppermute(after_edge, axis, up)]
    pallas_call x0 -> x4, Pallas kernels: none -> 13.7 us  [the longest x1 8.19 us: tile_pass(): pl.pallas_call(functools.partial(tile_kernel, height, width), out_shape=(...]
    dot_general x23 -> x0, matrix products: 10.4 us -> none  [the longest x4 2.16 us: local(): jnp.dot(pooled[scale_index].reshape(-1, DEC), block_weight.T, preferred_e...]
    all_to_all x0 -> x1, waiting for transfers between devices: none -> 9.77 us  [sum_over_mesh(): everything = lax.all_to_all(share, 'row', 0, 0, tiled=True)]
    all_to_all x0 -> x1, starting transfers between devices: none -> 7.35 us  [sum_over_mesh(): everything = lax.all_to_all(share, 'row', 0, 0, tiled=True)]
  transfers between devices with their start and end apart: 13 -> 6, of which waited for: 6 -> 5; matrix products, arithmetic and copies ran while one was open for 4% -> 1% of each run, Pallas kernels for 0% -> 0%
where the time goes in v2:
time: 124 us; the launch traced here: 123 us
  blocking collectives  61.3 us (49%)
  starting transfers between devices  23.9 us (19%)
  waiting for transfers between devices  17.3 us (14%)
  Pallas kernels  13.7 us (11%)
  local copies, waits for them, and re-layouts  4.31 us (3%)
  other arithmetic  1.49 us (1%)
    all_to_all x1, blocking collectives, sum_over_mesh(): lax.all_to_all(mine + received, 'row', 0, 0, tiled=True, axis_index_group...  34.7 us
    all_to_all x1, blocking collectives, sum_over_mesh(): along_cols = lax.all_to_all(parts, 'col', 0, 0, tiled=True)  26.6 us
    all_to_all x1, waiting for transfers between devices, sum_over_mesh(): everything = lax.all_to_all(share, 'row', 0, 0, tiled=True)  9.77 us
    ppermute x2, starting transfers between devices, swap_edges(): lax.ppermute(after_edge, axis, up)  8.51 us
    pallas_call x1, Pallas kernels, tile_pass(): pl.pallas_call(functools.partial(tile_kernel, height, width), out_shape=(...  8.19 us
    all_to_all x1, starting transfers between devices, sum_over_mesh(): everything = lax.all_to_all(share, 'row', 0, 0, tiled=True)  7.35 us
    ppermute x2, starting transfers between devices, swap_edges(): lax.ppermute(before_edge, axis, down)  6.12 us
    ppermute x2, waiting for transfers between devices, swap_edges(): lax.ppermute(before_edge, axis, down)  4.94 us
  transfers between devices with their start and end apart: 6, of which 5 were waited for; matrix products, arithmetic and copies ran while one was open for 1% of the time, Pallas kernels for 0%

profile of v2, /device:TPU:1, one launch (start us, length us, event | category | flops | bytes accessed | tf_op | source)
XLA Modules:
  0.0 123.0 jit_solution(15909816921922210745)
XLA Ops:
  0.7 1.0 fusion.5
  1.7 0.9 fusion.1
  2.7 5.4 %collective-permute-start = (bf16[4,32,512]{2,1,0:T(8,128)(2,1)S(1)}, bf16[4,32,512]{2,1,0:T(8,128)(2,1)S(1)}, u32[]{:S(2)}, u32[]{:S(2)}) collective-permute-start(bf16[4,32,512]{2,1,0:T(8,128)(2,1)S(1)} %pad_maximum_fusion.1), channel_id=1, source_target_pairs={{0,32},{32,64},{64,96},{96,128},{128,160},{160,192},{192,224},{224... | collective-permute-start | bytes 393224 | tf_op jit(solution)/shard_map/ppermute | solution.py:414
  8.2 4.8 %collective-permute-start.1 = (bf16[4,32,512]{2,1,0:T(8,128)(2,1)S(1)}, bf16[4,32,512]{2,1,0:T(8,128)(2,1)S(1)}, u32[]{:S(2)}, u32[]{:S(2)}) collective-permute-start(bf16[4,32,512]{2,1,0:T(8,128)(2,1)S(1)} %pad_maximum_fusion.2), channel_id=1, source_target_pairs={{32,0},{64,32},{96,64},{128,96},{160,128},{192,160},{224,192},{256... | collective-permute-start | bytes 393224 | tf_op jit(solution)/shard_map/ppermute | solution.py:414
  13.2 0.1 copy.30.reduce_ref
  13.5 1.1 collective-permute-done.1.bottom_ref
  14.7 3.1 %collective-permute-start.3 = (bf16[24,4,512]{2,1,0:T(4,128)(2,1)S(1)}, bf16[24,4,512]{2,1,0:T(4,128)(2,1)S(1)}, u32[]{:S(2)}, u32[]{:S(2)}) collective-permute-start(bf16[24,4,512]{2,1,0:T(4,128)(2,1)S(1)} %pad_maximum_fusion.4), channel_id=1, source_target_pairs={{0,1},{1,2},{2,3},{3,4},{4,5},{5,6},{6,7},{7,8},{8,9},{9,10},{10,1... | collective-permute-start | bytes 294920 | tf_op jit(solution)/shard_map/ppermute | solution.py:414
  17.9 1.3 %collective-permute-start.2 = (bf16[24,4,512]{2,1,0:T(4,128)(2,1)S(1)}, bf16[24,4,512]{2,1,0:T(4,128)(2,1)S(1)}, u32[]{:S(2)}, u32[]{:S(2)}) collective-permute-start(bf16[24,4,512]{2,1,0:T(4,128)(2,1)S(1)} %pad_maximum_fusion.3), channel_id=1, source_target_pairs={{1,0},{2,1},{3,2},{4,3},{5,4},{6,5},{7,6},{8,7},{9,8},{10,9},{11,1... | collective-permute-start | bytes 294920 | tf_op jit(solution)/shard_map/ppermute | solution.py:414
  19.3 0.1 collective-permute-done.3
  19.5 3.8 %collective-permute-done.2 = bf16[24,4,512]{2,1,0:T(4,128)(2,1)S(1)} collective-permute-done((bf16[24,4,512]{2,1,0:T(4,128)(2,1)S(1)}, bf16[24,4,512]{2,1,0:T(4,128)(2,1)S(1)}, u32[]{:S(2)}, u32[]{:S(2)}) %collective-permute-start.2) | collective-permute-done | bytes 98336 | tf_op jit(solution)/shard_map/ppermute | solution.py:414
  23.3 0.1 pad_maximum_fusion.side_ref
  23.5 8.2 %tile_pass.1 = (bf16[16,32,64]{2,1,0:T(8,128)(2,1)}, bf16[128,128]{1,0:T(8,128)(2,1)}, bf16[32,320]{1,0:T(8,128)(2,1)}, bf16[8,512]{1,0:T(8,128)(2,1)S(1)}, f32[...) custom-call(bf16[16,32,384]{2,1,0:T(8,128)(2,1)S(1)} %copy-done, bf16[16,32,128]{2,1,0:T(8,128)(2,1)S(1)} %pad_maximum_fusion.5.pair_ref, ...), custom_call_target="tpu_custom_call" | custom-call | tf_op jit(solution)/shard_map/tile_pass/pallas_call | solution.py:296
  31.7 1.9 %collective-permute-start.4 = (f32[8,216,128]{2,1,0:T(8,128)S(1)}, f32[8,216,128]{2,1,0:T(8,128)S(1)}, u32[]{:S(2)}, u32[]{:S(2)}) collective-permute-start(f32[8,216,128]{2,1,0:T(8,128)S(1)} %get-tuple-element.30), channel_id=1, source_target_pairs={{0,32},{32,0},{64,96},{96,64},{128,160},{160,128},{192,224},{224,1... | collective-permute-start | bytes 2654216 | tf_op jit(solution)/shard_map/ppermute | solution.py:378
  33.7 2.4 %collective-permute-done.4 = f32[8,216,128]{2,1,0:T(8,128)S(1)} collective-permute-done((f32[8,216,128]{2,1,0:T(8,128)S(1)}, f32[8,216,128]{2,1,0:T(8,128)S(1)}, u32[]{:S(2)}, u32[]{:S(2)}) %collective-permute-start.4) | collective-permute-done | bytes 884768 | tf_op jit(solution)/shard_map/ppermute | solution.py:378
  36.2 34.7 %all_to_all.15.received_ref = f32[8,216,128]{2,1,0:T(8,128)} all-to-all(f32[8,216,128]{2,1,0:T(8,128)S(1)} %add.3), channel_id=1, replica_groups={{0,64,128,192,256,320,384,448},{32,96,160,224,288,352,416,480},{1,65,12..., dimensions={0} | all-to-all | bytes 1769472 | tf_op jit(solution)/shard_map/all_to_all | solution.py:380
  70.9 2.1 %column_parts.1 = f32[32,32,128]{2,1,0:T(8,128)} custom-call(f32[8,216,128]{2,1,0:T(8,128)} %all_to_all.15.received_ref), custom_call_target="tpu_custom_call" | custom-call | tf_op jit(solution)/shard_map/column_parts/pallas_call | solution.py:381
  73.0 26.6 %all_to_all.16.received_ref = f32[32,32,128]{2,1,0:T(8,128)} all-to-all(f32[32,32,128]{2,1,0:T(8,128)} %column_parts.1), channel_id=1, replica_groups=mesh['row'=16,'col'=32] {'col'}, dimensions={0} | all-to-all | bytes 1048576 | tf_op jit(solution)/shard_map/all_to_all | solution.py:387
  99.5 1.8 %final_sums.1 = (f32[6,128]{1,0:T(8,128)}, f32[16,24,128]{2,1,0:T(8,128)}) custom-call(f32[32,32,128]{2,1,0:T(8,128)} %all_to_all.16.received_ref), custom_call_target="tpu_custom_call" | custom-call | tf_op jit(solution)/shard_map/final_sums/pallas_call | solution.py:388
  101.3 7.3 %all-to-all-start.2 = ((f32[16,24,128]{2,1,0:T(8,128)}), f32[16,24,128]{2,1,0:T(8,128)S(1)}, u32[]{:S(2)}, u32[]{:S(2)}) async-start(f32[16,24,128]{2,1,0:T(8,128)} %get-tuple-element.32), calls=%async_computation.2 | async-start | bytes 393216 | tf_op jit(solution)/shard_map/all_to_all | solution.py:393
  108.7 0.6 reshape.68
  109.3 9.8 %all-to-all-done.2.all_ref = f32[16,24,128]{2,1,0:T(8,128)S(1)} async-done(((f32[16,24,128]{2,1,0:T(8,128)}), f32[16,24,128]{2,1,0:T(8,128)S(1)}, u32[]{:S(2)}, u32[]{:S(2)}) %all-to-all-start.2) | async-done | bytes 196640 | tf_op jit(solution)/shard_map/all_to_all | solution.py:393
  119.0 0.7 copy-done.16
  119.7 1.7 %small_sums.1 = (f32[4,384]{1,0:T(4,128)}, f32[64,256]{1,0:T(8,128)}, f32[256,64]{1,0:T(8,128)}, f32[9,256]{1,0:T(8,128)}, f32[2,256]{1,0:T(2,128)}, /*index=5*/f32[3,64]{1,0:T(4,128)}) custom-call(f32[16,24,128]{2,1,0:T(8,128)} %copy-done.16), custom_call_target="tpu_custom_call" | custom-call | tf_op jit(solution)/shard_map/small_sums/pallas_call | solution.py:394
  121.4 1.6 %copy.31 = f32[256,64]{0,1:T(8,128)} copy(f32[256,64]{1,0:T(8,128)} %get-tuple-element.46) | data formatting | bytes 131072
  (51 shorter events, 0.7 us)
Async XLA Ops:
  0.6 12.4 %copy-start = (bf16[16,32,384]{2,1,0:T(8,128)(2,1)S(1)}, bf16[16,32,384]{2,1,0:T(8,128)(2,1)}, u32[]{:S(2)}) copy-start(bf16[16,32,384]{2,1,0:T(8,128)(2,1)} %joined_ref.1) | copy-start | bytes 1179652
  0.7 12.7 %copy-start.14 = (bf16[16,32,64]{2,1,0:T(8,128)(2,1)S(1)}, bf16[16,32,64]{2,1,0:T(8,128)(2,1)}, u32[]{:S(2)}) copy-start(bf16[16,32,64]{2,1,0:T(8,128)(2,1)} %param.29) | copy-start | bytes 196612
  0.7 12.7 %copy-start.15 = (bf16[16,32,64]{2,1,0:T(8,128)(2,1)S(1)}, bf16[16,32,64]{2,1,0:T(8,128)(2,1)}, u32[]{:S(2)}) copy-start(bf16[16,32,64]{2,1,0:T(8,128)(2,1)} %param.28) | copy-start | bytes 196612
  0.7 12.4 %copy-start.18 = (bf16[2,4,512]{2,1,0:T(4,128)(2,1)S(1)}, bf16[2,4,512]{2,1,0:T(4,128)(2,1)}, u32[]{:S(2)}) copy-start(bf16[2,4,512]{2,1,0:T(4,128)(2,1)} %param.27) | copy-start | bytes 24580
  0.7 12.5 %copy-start.17 = (bf16[256,64]{0,1:T(8,128)(2,1)S(1)}, bf16[256,64]{0,1:T(8,128)(2,1)}, u32[]{:S(2)}) copy-start(bf16[256,64]{0,1:T(8,128)(2,1)} %param.36) | copy-start | bytes 98308
  2.7 10.8 %collective-permute-start = (bf16[4,32,512]{2,1,0:T(8,128)(2,1)S(1)}, bf16[4,32,512]{2,1,0:T(8,128)(2,1)S(1)}, u32[]{:S(2)}, u32[]{:S(2)}) collective-permute-start(bf16[4,32,512]{2,1,0:T(8,128)(2,1)S(1)} %pad_maximum_fusion.1), channel_id=1, source_target_pairs={{0,32},{32,64},{64,96},{96,128},{128,160},{160,192},{192,224},{224... | collective-permute-start | bytes 393224 | tf_op jit(solution)/shard_map/ppermute | solution.py:414
  8.0 15.4 %copy-start.1 = (bf16[512,384]{1,0:T(8,128)(2,1)S(1)}, bf16[512,384]{1,0:T(8,128)(2,1)}, u32[]{:S(2)}) copy-start(bf16[512,384]{1,0:T(8,128)(2,1)} %fourth_ref.1) | copy-start | bytes 1179652
  8.1 15.4 %copy-start.2 = (bf16[320,384]{1,0:T(8,128)(2,1)S(1)}, bf16[320,384]{1,0:T(8,128)(2,1)}, u32[]{:S(2)}) copy-start(bf16[320,384]{1,0:T(8,128)(2,1)} %third_ref.1) | copy-start | bytes 737284
  8.1 15.4 %copy-start.3 = (bf16[128,384]{1,0:T(8,128)(2,1)S(1)}, bf16[128,384]{1,0:T(8,128)(2,1)}, u32[]{:S(2)}) copy-start(bf16[128,384]{1,0:T(8,128)(2,1)} %second_ref.1) | copy-start | bytes 294916
  8.1 15.4 %copy-start.4 = (bf16[64,384]{1,0:T(8,128)(2,1)S(1)}, bf16[64,384]{1,0:T(8,128)(2,1)}, u32[]{:S(2)}) copy-start(bf16[64,384]{1,0:T(8,128)(2,1)} %first_ref.1) | copy-start | bytes 147460
  8.1 15.4 %copy-start.5 = (bf16[8,16,128]{2,1,0:T(8,128)(2,1)S(1)}, bf16[8,16,128]{2,1,0:T(8,128)(2,1)}, u32[]{:S(2)}) copy-start(bf16[8,16,128]{2,1,0:T(8,128)(2,1)} %param.25) | copy-start | bytes 98308
  8.1 15.4 %copy-start.6 = (bf16[64,256]{1,0:T(8,128)(2,1)S(1)}, bf16[64,256]{1,0:T(8,128)(2,1)}, u32[]{:S(2)}) copy-start(bf16[64,256]{1,0:T(8,128)(2,1)} %expand_ref.1) | copy-start | bytes 98308
  8.1 15.4 %copy-start.7 = (bf16[4,8,320]{2,1,0:T(8,128)(2,1)S(1)}, bf16[4,8,320]{2,1,0:T(8,128)(2,1)}, u32[]{:S(2)}) copy-start(bf16[4,8,320]{2,1,0:T(8,128)(2,1)} %param.26) | copy-start | bytes 61444
  8.1 15.4 %copy-start.8 = (f32[9,256]{1,0:T(8,128)S(1)}, f32[9,256]{1,0:T(8,128)}, u32[]{:S(2)}) copy-start(f32[9,256]{1,0:T(8,128)} %depth_ref.1) | copy-start | bytes 27652
  8.1 15.4 %copy-start.9 = (f32[256]{0:T(256)S(1)}, f32[256]{0:T(256)}, u32[]{:S(2)}) copy-start(f32[256]{0:T(256)} %param.33) | copy-start | bytes 3076
  8.2 15.3 %copy-start.10 = (f32[256]{0:T(256)S(1)}, f32[256]{0:T(256)}, u32[]{:S(2)}) copy-start(f32[256]{0:T(256)} %param.35) | copy-start | bytes 3076
  8.2 15.3 %copy-start.11 = (f32[64]{0:T(128)S(1)}, f32[64]{0:T(128)}, u32[]{:S(2)}) copy-start(f32[64]{0:T(128)} %param.30) | copy-start | bytes 772
  8.2 15.3 %copy-start.12 = (f32[64]{0:T(128)S(1)}, f32[64]{0:T(128)}, u32[]{:S(2)}) copy-start(f32[64]{0:T(128)} %param.31) | copy-start | bytes 772
  8.2 15.3 %copy-start.13 = (f32[64]{0:T(128)S(1)}, f32[64]{0:T(128)}, u32[]{:S(2)}) copy-start(f32[64]{0:T(128)} %param.37) | copy-start | bytes 772
  8.2 6.4 %collective-permute-start.1 = (bf16[4,32,512]{2,1,0:T(8,128)(2,1)S(1)}, bf16[4,32,512]{2,1,0:T(8,128)(2,1)S(1)}, u32[]{:S(2)}, u32[]{:S(2)}) collective-permute-start(bf16[4,32,512]{2,1,0:T(8,128)(2,1)S(1)} %pad_maximum_fusion.2), channel_id=1, source_target_pairs={{32,0},{64,32},{96,64},{128,96},{160,128},{192,160},{224,192},{256... | collective-permute-start | bytes 393224 | tf_op jit(solution)/shard_map/ppermute | solution.py:414
  14.7 4.7 %collective-permute-start.3 = (bf16[24,4,512]{2,1,0:T(4,128)(2,1)S(1)}, bf16[24,4,512]{2,1,0:T(4,128)(2,1)S(1)}, u32[]{:S(2)}, u32[]{:S(2)}) collective-permute-start(bf16[24,4,512]{2,1,0:T(4,128)(2,1)S(1)} %pad_maximum_fusion.4), channel_id=1, source_target_pairs={{0,1},{1,2},{2,3},{3,4},{4,5},{5,6},{6,7},{7,8},{8,9},{9,10},{10,1... | collective-permute-start | bytes 294920 | tf_op jit(solution)/shard_map/ppermute | solution.py:414
  17.9 5.4 %collective-permute-start.2 = (bf16[24,4,512]{2,1,0:T(4,128)(2,1)S(1)}, bf16[24,4,512]{2,1,0:T(4,128)(2,1)S(1)}, u32[]{:S(2)}, u32[]{:S(2)}) collective-permute-start(bf16[24,4,512]{2,1,0:T(4,128)(2,1)S(1)} %pad_maximum_fusion.3), channel_id=1, source_target_pairs={{1,0},{2,1},{3,2},{4,3},{5,4},{6,5},{7,6},{8,7},{9,8},{10,9},{11,1... | collective-permute-start | bytes 294920 | tf_op jit(solution)/shard_map/ppermute | solution.py:414
  31.7 4.3 %collective-permute-start.4 = (f32[8,216,128]{2,1,0:T(8,128)S(1)}, f32[8,216,128]{2,1,0:T(8,128)S(1)}, u32[]{:S(2)}, u32[]{:S(2)}) collective-permute-start(f32[8,216,128]{2,1,0:T(8,128)S(1)} %get-tuple-element.30), channel_id=1, source_target_pairs={{0,32},{32,0},{64,96},{96,64},{128,160},{160,128},{192,224},{224,1... | collective-permute-start | bytes 2654216 | tf_op jit(solution)/shard_map/ppermute | solution.py:378
  101.3 17.7 %all-to-all-start.2 = ((f32[16,24,128]{2,1,0:T(8,128)}), f32[16,24,128]{2,1,0:T(8,128)S(1)}, u32[]{:S(2)}, u32[]{:S(2)}) async-start(f32[16,24,128]{2,1,0:T(8,128)} %get-tuple-element.32), calls=%async_computation.2 | async-start | bytes 393216 | tf_op jit(solution)/shard_map/all_to_all | solution.py:393
  (1 other events, 0.7 us)

commit v3 on v2

--- a/solution.py
+++ b/solution.py
@@ -207,7 +207,7 @@
     projection = nt(wide_ref[3:21].reshape(18 * PITCH, DEC), join_ref[0:DEC, :]).astype(jnp.bfloat16)
     later = wide_pair_ref[3:21, :, D1:].reshape(18 * PITCH, D1).astype(jnp.float32)
     feature_grad = (nt(projection, first_ref[...]) + later).astype(jnp.bfloat16)
-    act_grad = nt(feature_grad, reduce_ref[...])
+    act_grad = nn(feature_grad, reduce_ref[...])
     pre_grad = (act_grad * slope_ref[...].reshape(18 * PITCH, HID)).astype(jnp.bfloat16)
     pre_ref[...] = (pre_grad.astype(jnp.float32) * inside(3, 18)).reshape(18, PITCH, HID)
 
@@ -215,7 +215,7 @@
     own_projection = own(projection, 18)
     own_grad = own(feature_grad, 18)
     own_block = pair_ref[:, :, 0:D1].reshape(TH * TW, D1).astype(jnp.float32)
-    features = (own_block + (nn(activated, reduce_ref[...]) + reduce_bias_ref[...])).astype(
+    features = (own_block + (nt(activated, reduce_ref[...]) + reduce_bias_ref[...])).astype(
         jnp.bfloat16
     )
     linear_ref[0:D1, :] = tn(features, own_projection) * scale_base
@@ -326,8 +326,9 @@
 
 
 def column_kernel(received_ref, out_ref, total_ref):
-    total_ref[...] = jnp.sum(received_ref[...], 0)
-    share = total_ref[BLOCK:, :]
+    total_ref[...] = jnp.sum(received_ref[:, 0:BLOCK, :].astype(jnp.float32), 0)
+    share = jnp.sum(received_ref[:, BLOCK:, :].astype(jnp.float32), 0)
+    share = share[0:SHARE] + share[SHARE:]
     empty = jnp.zeros((2, 128), jnp.float32)
     for c in range(out_ref.shape[0]):
         for j in range(3):
@@ -345,13 +346,12 @@
         out_ref[r] = total[8:]
 
 
-def small_kernel(all_ref, biases_ref, expand_ref, reduce_ref, depth_ref, hidden_ref, channel_ref, turn_ref):
+def small_kernel(all_ref, biases_ref, expand_ref, reduce_ref, depth_ref, hidden_ref, channel_ref):
     for r in range(16):
         lanes = slice(0, 128) if r < 8 else slice(128, 256)
         first = 8 * (r % 8)
         expand_ref[first : first + 8, lanes] = all_ref[r, 0:8, :]
-        turn_ref[first : first + 8, lanes] = all_ref[r, 8:16, :]
-    reduce_ref[...] = turn_ref[...].T
+        reduce_ref[first : first + 8, lanes] = all_ref[r, 8:16, :]
 
     def row(n):
         return all_ref[n // 8, 16 + n % 8 : 17 + n % 8, :]
@@ -369,6 +369,27 @@
         channel_ref[t : t + 1, :] = row(34 + t)[:, 0:D1]
 
 
+def in_vmem(kernel, name, out_shape, *operands, scratch=()):
+    vmem = pl.BlockSpec(memory_space=pltpu.VMEM)
+    return pl.pallas_call(
+        kernel,
+        out_shape=out_shape,
+        in_specs=[vmem] * len(operands),
+        out_specs=jax.tree.map(lambda _: vmem, out_shape),
+        scratch_shapes=scratch,
+        compiler_params=pltpu.CompilerParams(vmem_limit_bytes=16 * 2**20),
+        name=name,
+    )(*operands)
+
+
+def chip_kernel(mine_ref, received_ref, out_ref):
+    total = mine_ref[:, 0:BLOCK, :] + received_ref[:, 0:BLOCK, :]
+    out_ref[:, 0:BLOCK, :] = total.astype(jnp.bfloat16)
+    share = mine_ref[:, BLOCK:, :] + received_ref[:, BLOCK:, :]
+    high = share.astype(jnp.bfloat16).astype(jnp.float32)
+    out_ref[:, BLOCK:, :] = jnp.concatenate([high, share - high], axis=1).astype(jnp.bfloat16)
+
+
 def sum_over_mesh(mine, other):
     rows = lax.axis_size("row")
     cols = lax.axis_size("col")
@@ -377,41 +398,51 @@
     f32 = jnp.float32
     received = lax.ppermute(other, "row", [(i, i ^ 1) for i in range(rows)])
     groups = [[2 * z + c for z in range(chips)] for c in range(2)]
-    along_z = lax.all_to_all(mine + received, "row", 0, 0, tiled=True, axis_index_groups=groups)
-    parts = pl.pallas_call(
+    chip = in_vmem(
+        chip_kernel,
+        "chip_sums",
+        sds((chips, BLOCK + 2 * SHARE, 128), jnp.bfloat16),
+        mine,
+        received,
+    )
+    along_z = lax.all_to_all(chip, "row", 0, 0, tiled=True, axis_index_groups=groups)
+    parts = in_vmem(
         column_kernel,
-        out_shape=sds((cols, 8 + SHARE, 128), f32),
-        scratch_shapes=[pltpu.VMEM((BLOCK + SHARE, 128), f32)],
-        name="column_parts",
-    )(along_z)
+        "column_parts",
+        sds((cols, 8 + SHARE, 128), f32),
+        along_z,
+        scratch=[pltpu.VMEM((BLOCK, 128), f32)],
+    )
     along_cols = lax.all_to_all(parts, "col", 0, 0, tiled=True)
-    linear, share = pl.pallas_call(
-        final_kernel,
-        out_shape=(sds((6, 128), f32), sds((rows, SHARE, 128), f32)),
-        name="final_sums",
-    )(along_cols)
+    linear, share = in_vmem(
+        final_kernel, "final_sums", (sds((6, 128), f32), sds((rows, SHARE, 128), f32)), along_cols
+    )
     everything = lax.all_to_all(share, "row", 0, 0, tiled=True)
-    small = pl.pallas_call(
+    biases, expand, reduce, depth, hidden, channel = in_vmem(
         small_kernel,
-        out_shape=(
+        "small_sums",
+        (
             sds((4, DEC), f32),
             sds((D1, HID), f32),
-            sds((HID, D1), f32),
+            sds((D1, HID), f32),
             sds((9, HID), f32),
             sds((2, HID), f32),
             sds((3, D1), f32),
         ),
-        scratch_shapes=[pltpu.VMEM((D1, HID), f32)],
-        name="small_sums",
-    )(everything)
-    return linear.reshape(-1), small
-
-
-def swap_edges(before_edge, after_edge, axis):
+        everything,
+    )
+    return linear.reshape(-1), (biases, expand, reduce.T, depth, hidden, channel)
+
+
+def swap_edges(first_edge, last_edge, axis):
     devices = lax.axis_size(axis)
-    up = [(i, i + 1) for i in range(devices - 1)]
-    down = [(j, i) for i, j in up]
-    return lax.ppermute(after_edge, axis, up), lax.ppermute(before_edge, axis, down)
+    even = lax.axis_index(axis) % 2 == 0
+    near = [(i, i ^ 1) for i in range(devices)]
+    far = [(i, i + 1) for i in range(1, devices - 1, 2)]
+    far = far + [(j, i) for i, j in far]
+    from_far = lax.ppermute(jnp.where(even, first_edge, last_edge), axis, far)
+    from_near = lax.ppermute(jnp.where(even, last_edge, first_edge), axis, near)
+    return jnp.where(even, from_far, from_near), jnp.where(even, from_near, from_far)
 
 
 def local(
@@ -476,7 +507,7 @@
         expand_bias.reshape(1, -1),
         depth_weight,
         depth_bias.reshape(1, -1),
-        reduce_weight,
+        reduce_weight.T,
         reduce_bias.reshape(1, -1),
     )
     linear_grads, small = sum_over_mesh(mine, other)

time: 124 us -> 107 us (0.86)
  blocking collectives: 61.3 us -> 50.8 us
  Pallas kernels: 13.7 us -> 9.99 us
  local copies, waits for them, and re-layouts: 4.31 us -> 1.9 us
  waiting for transfers between devices: 17.3 us -> 19 us
  starting transfers between devices: 23.9 us -> 22.6 us
    all_to_all x1, blocking collectives: 34.7 us -> 22 us  [sum_over_mesh(): lax.all_to_all(chip, 'row', 0, 0, tiled=True, axis_index_groups=groups)]
    pallas_call x3 -> x4, Pallas kernels: 5.52 us -> 1.71 us  [in_vmem(): pl.pallas_call(kernel, out_shape=out_shape, in_specs=[vmem] * len(operand...]
    unnamed x40 -> x36, local copies, waits for them, and re-layouts: 2.52 us -> 0.11 us
    all_to_all x1, blocking collectives: 26.6 us -> 28.8 us  [sum_over_mesh(): along_cols = lax.all_to_all(parts, 'col', 0, 0, tiled=True)]
    ppermute x4, waiting for transfers between devices: 5.09 us -> 6.83 us  [the longest x2 4.19 us: swap_edges(): from_far = lax.ppermute(jnp.where(even, first_edge, last_edge), axis, far)]
    ppermute x4, starting transfers between devices: 14.6 us -> 13.3 us  [the longest x2 10.7 us: swap_edges(): from_near = lax.ppermute(jnp.where(even, last_edge, first_edge), axis, near)]
  transfers between devices with their start and end apart: 6 -> 6, of which waited for: 5 -> 4; matrix products, arithmetic and copies ran while one was open for 1% -> 1% of each run, Pallas kernels for 0% -> 0%
where the time goes in v3:
time: 107 us
  blocking collectives  50.8 us (47%)
  starting transfers between devices  22.6 us (21%)
  waiting for transfers between devices  19 us (18%)
  Pallas kernels  9.99 us (9%)
  local copies, waits for them, and re-layouts  1.9 us (2%)
  other arithmetic  1.46 us (1%)
  between operations  1.07 us (1%)
    all_to_all x1, blocking collectives, sum_over_mesh(): along_cols = lax.all_to_all(parts, 'col', 0, 0, tiled=True)  28.8 us
    all_to_all x1, blocking collectives, sum_over_mesh(): lax.all_to_all(chip, 'row', 0, 0, tiled=True, axis_index_groups=groups)  22 us
    ppermute x2, starting transfers between devices, swap_edges(): from_near = lax.ppermute(jnp.where(even, last_edge, first_edge), axis, near)  10.7 us
    all_to_all x1, waiting for transfers between devices, sum_over_mesh(): everything = lax.all_to_all(share, 'row', 0, 0, tiled=True)  9.77 us
    pallas_call x1, Pallas kernels, tile_pass(): pl.pallas_call(functools.partial(tile_kernel, height, width), out_shape=(...  8.28 us
    all_to_all x1, starting transfers between devices, sum_over_mesh(): everything = lax.all_to_all(share, 'row', 0, 0, tiled=True)  7.38 us
    ppermute x2, waiting for transfers between devices, swap_edges(): from_far = lax.ppermute(jnp.where(even, first_edge, last_edge), axis, far)  4.19 us
    ppermute x2, waiting for transfers between devices, swap_edges(): from_near = lax.ppermute(jnp.where(even, last_edge, first_edge), axis, near)  2.65 us
  transfers between devices with their start and end apart: 6, of which 4 were waited for; matrix products, arithmetic and copies ran while one was open for 1% of the time, Pallas kernels for 0%

profile of v3, /device:TPU:1, one launch (start us, length us, event | category | flops | bytes accessed | tf_op | source)
XLA Modules:
  0.0 106.8 jit_solution(9980114552127323010)
XLA Ops:
  0.7 1.0 fusion.5
  1.7 0.9 fusion
  2.7 8.8 %collective-permute-start.1 = (bf16[4,32,512]{2,1,0:T(8,128)(2,1)S(1)}, bf16[4,32,512]{2,1,0:T(8,128)(2,1)S(1)}, u32[]{:S(2)}, u32[]{:S(2)}) collective-permute-start(bf16[4,32,512]{2,1,0:T(8,128)(2,1)S(1)} %get-tuple-element.47), channel_id=1, source_target_pairs={{0,32},{32,0},{64,96},{96,64},{128,160},{160,128},{192,224},{224,1... | collective-permute-start | bytes 393224 | tf_op jit(solution)/shard_map/ppermute | solution.py:444
  11.5 1.9 %collective-permute-start = (bf16[4,32,512]{2,1,0:T(8,128)(2,1)S(1)}, bf16[4,32,512]{2,1,0:T(8,128)(2,1)S(1)}, u32[]{:S(2)}, u32[]{:S(2)}) collective-permute-start(bf16[4,32,512]{2,1,0:T(8,128)(2,1)S(1)} %get-tuple-element.48), channel_id=1, source_target_pairs={{32,64},{96,128},{160,192},{224,256},{288,320},{352,384},{416,448}... | collective-permute-start | bytes 393224 | tf_op jit(solution)/shard_map/ppermute | solution.py:443
  13.6 0.1 fusion.2
  13.9 4.2 %collective-permute-done = bf16[4,32,512]{2,1,0:T(8,128)(2,1)S(1)} collective-permute-done((bf16[4,32,512]{2,1,0:T(8,128)(2,1)S(1)}, bf16[4,32,512]{2,1,0:T(8,128)(2,1)S(1)}, u32[]{:S(2)}, u32[]{:S(2)}) %collective-permute-start) | collective-permute-done | bytes 131104 | tf_op jit(solution)/shard_map/ppermute | solution.py:443
  18.1 0.1 broadcast_select_fusion.7
  18.2 1.9 %collective-permute-start.2 = (bf16[24,4,512]{2,1,0:T(4,128)(2,1)S(1)}, bf16[24,4,512]{2,1,0:T(4,128)(2,1)S(1)}, u32[]{:S(2)}, u32[]{:S(2)}) collective-permute-start(bf16[24,4,512]{2,1,0:T(4,128)(2,1)S(1)} %get-tuple-element.53), channel_id=1, source_target_pairs={{0,1},{1,0},{2,3},{3,2},{4,5},{5,4},{6,7},{7,6},{8,9},{9,8},{10,11... | collective-permute-start | bytes 294920 | tf_op jit(solution)/shard_map/ppermute | solution.py:444
  20.2 0.7 collective-permute-start.3
  20.8 0.1 pad_maximum_fusion.5.pair_ref
  21.0 2.6 %collective-permute-done.2 = bf16[24,4,512]{2,1,0:T(4,128)(2,1)S(1)} collective-permute-done((bf16[24,4,512]{2,1,0:T(4,128)(2,1)S(1)}, bf16[24,4,512]{2,1,0:T(4,128)(2,1)S(1)}, u32[]{:S(2)}, u32[]{:S(2)}) %collective-permute-start.2) | collective-permute-done | bytes 98336 | tf_op jit(solution)/shard_map/ppermute | solution.py:444
  23.6 0.1 pad_maximum_fusion.side_ref
  23.9 8.3 %tile_pass.1 = (bf16[16,32,64]{2,1,0:T(8,128)(2,1)}, bf16[128,128]{1,0:T(8,128)(2,1)}, bf16[32,320]{1,0:T(8,128)(2,1)}, bf16[8,512]{1,0:T(8,128)(2,1)S(1)}, f32[...) custom-call(bf16[16,32,384]{2,1,0:T(8,128)(2,1)S(1)} %copy-done, bf16[16,32,128]{2,1,0:T(8,128)(2,1)S(1)} %pad_maximum_fusion.5.pair_ref, ...), custom_call_target="tpu_custom_call" | custom-call | tf_op jit(solution)/shard_map/tile_pass/pallas_call | solution.py:296
  32.2 1.9 %collective-permute-start.4 = (f32[8,216,128]{2,1,0:T(8,128)S(1)}, f32[8,216,128]{2,1,0:T(8,128)S(1)}, u32[]{:S(2)}, u32[]{:S(2)}) collective-permute-start(f32[8,216,128]{2,1,0:T(8,128)S(1)} %get-tuple-element.30), channel_id=1, source_target_pairs={{0,32},{32,0},{64,96},{96,64},{128,160},{160,128},{192,224},{224,1... | collective-permute-start | bytes 2654216 | tf_op jit(solution)/shard_map/ppermute | solution.py:399
  34.1 2.4 %collective-permute-done.4.received_ref = f32[8,216,128]{2,1,0:T(8,128)S(1)} collective-permute-done((f32[8,216,128]{2,1,0:T(8,128)S(1)}, f32[8,216,128]{2,1,0:T(8,128)S(1)}, u32[]{:S(2)}, u32[]{:S(2)}) %collective-permute-start.4) | collective-permute-done | bytes 884768 | tf_op jit(solution)/shard_map/ppermute | solution.py:399
  36.5 0.2 chip_sums.1
  36.7 22.0 %all_to_all.15.received_ref = bf16[8,240,128]{2,1,0:T(8,128)(2,1)S(1)} all-to-all(bf16[8,240,128]{2,1,0:T(8,128)(2,1)S(1)} %chip_sums.1), channel_id=1, replica_groups={{0,64,128,192,256,320,384,448},{32,96,160,224,288,352,416,480},{1,65,12..., dimensions={0} | all-to-all | bytes 983040 | tf_op jit(solution)/shard_map/all_to_all | solution.py:408
  58.7 0.1 column_parts.1
  58.9 28.8 %all_to_all.16.received_ref = f32[32,32,128]{2,1,0:T(8,128)S(1)} all-to-all(f32[32,32,128]{2,1,0:T(8,128)S(1)} %column_parts.1), channel_id=1, replica_groups=mesh['row'=16,'col'=32] {'col'}, dimensions={0} | all-to-all | bytes 1048576 | tf_op jit(solution)/shard_map/all_to_all | solution.py:416
  87.7 0.7 final_sums.1
  88.4 7.4 %all-to-all-start.2 = ((f32[16,24,128]{2,1,0:T(8,128)}), f32[16,24,128]{2,1,0:T(8,128)S(1)}, u32[]{:S(2)}, u32[]{:S(2)}) async-start(f32[16,24,128]{2,1,0:T(8,128)} %get-tuple-element.32), calls=%async_computation.2 | async-start | bytes 393216 | tf_op jit(solution)/shard_map/all_to_all | solution.py:420
  95.8 0.6 reshape.68
  96.4 9.8 %all-to-all-done.2.all_ref = f32[16,24,128]{2,1,0:T(8,128)S(1)} async-done(((f32[16,24,128]{2,1,0:T(8,128)}), f32[16,24,128]{2,1,0:T(8,128)S(1)}, u32[]{:S(2)}, u32[]{:S(2)}) %all-to-all-start.2) | async-done | bytes 196640 | tf_op jit(solution)/shard_map/all_to_all | solution.py:420
  106.1 0.7 small_sums.1
  (46 shorter events, 0.4 us)
Async XLA Ops:
  0.6 12.8 %copy-start = (bf16[16,32,384]{2,1,0:T(8,128)(2,1)S(1)}, bf16[16,32,384]{2,1,0:T(8,128)(2,1)}, u32[]{:S(2)}) copy-start(bf16[16,32,384]{2,1,0:T(8,128)(2,1)} %joined_ref.1) | copy-start | bytes 1179652
  0.7 12.9 %copy-start.15 = (bf16[16,32,64]{2,1,0:T(8,128)(2,1)S(1)}, bf16[16,32,64]{2,1,0:T(8,128)(2,1)}, u32[]{:S(2)}) copy-start(bf16[16,32,64]{2,1,0:T(8,128)(2,1)} %param.29) | copy-start | bytes 196612
  0.7 12.9 %copy-start.16 = (bf16[16,32,64]{2,1,0:T(8,128)(2,1)S(1)}, bf16[16,32,64]{2,1,0:T(8,128)(2,1)}, u32[]{:S(2)}) copy-start(bf16[16,32,64]{2,1,0:T(8,128)(2,1)} %param.28) | copy-start | bytes 196612
  0.7 12.8 %copy-start.17 = (bf16[2,4,512]{2,1,0:T(4,128)(2,1)S(1)}, bf16[2,4,512]{2,1,0:T(4,128)(2,1)}, u32[]{:S(2)}) copy-start(bf16[2,4,512]{2,1,0:T(4,128)(2,1)} %param.27) | copy-start | bytes 24580
  2.7 11.2 %collective-permute-start.1 = (bf16[4,32,512]{2,1,0:T(8,128)(2,1)S(1)}, bf16[4,32,512]{2,1,0:T(8,128)(2,1)S(1)}, u32[]{:S(2)}, u32[]{:S(2)}) collective-permute-start(bf16[4,32,512]{2,1,0:T(8,128)(2,1)S(1)} %get-tuple-element.47), channel_id=1, source_target_pairs={{0,32},{32,0},{64,96},{96,64},{128,160},{160,128},{192,224},{224,1... | collective-permute-start | bytes 393224 | tf_op jit(solution)/shard_map/ppermute | solution.py:444
  11.5 6.6 %collective-permute-start = (bf16[4,32,512]{2,1,0:T(8,128)(2,1)S(1)}, bf16[4,32,512]{2,1,0:T(8,128)(2,1)S(1)}, u32[]{:S(2)}, u32[]{:S(2)}) collective-permute-start(bf16[4,32,512]{2,1,0:T(8,128)(2,1)S(1)} %get-tuple-element.48), channel_id=1, source_target_pairs={{32,64},{96,128},{160,192},{224,256},{288,320},{352,384},{416,448}... | collective-permute-start | bytes 393224 | tf_op jit(solution)/shard_map/ppermute | solution.py:443
  13.7 10.1 %copy-start.1 = (bf16[512,384]{1,0:T(8,128)(2,1)S(1)}, bf16[512,384]{1,0:T(8,128)(2,1)}, u32[]{:S(2)}) copy-start(bf16[512,384]{1,0:T(8,128)(2,1)} %fourth_ref.1) | copy-start | bytes 1179652
  13.7 10.1 %copy-start.2 = (bf16[320,384]{1,0:T(8,128)(2,1)S(1)}, bf16[320,384]{1,0:T(8,128)(2,1)}, u32[]{:S(2)}) copy-start(bf16[320,384]{1,0:T(8,128)(2,1)} %third_ref.1) | copy-start | bytes 737284
  13.7 10.1 %copy-start.3 = (bf16[128,384]{1,0:T(8,128)(2,1)S(1)}, bf16[128,384]{1,0:T(8,128)(2,1)}, u32[]{:S(2)}) copy-start(bf16[128,384]{1,0:T(8,128)(2,1)} %second_ref.1) | copy-start | bytes 294916
  13.7 10.1 %copy-start.4 = (bf16[64,384]{1,0:T(8,128)(2,1)S(1)}, bf16[64,384]{1,0:T(8,128)(2,1)}, u32[]{:S(2)}) copy-start(bf16[64,384]{1,0:T(8,128)(2,1)} %first_ref.1) | copy-start | bytes 147460
  13.8 10.1 %copy-start.5 = (bf16[8,16,128]{2,1,0:T(8,128)(2,1)S(1)}, bf16[8,16,128]{2,1,0:T(8,128)(2,1)}, u32[]{:S(2)}) copy-start(bf16[8,16,128]{2,1,0:T(8,128)(2,1)} %param.25) | copy-start | bytes 98308
  13.8 10.1 %copy-start.6 = (bf16[64,256]{1,0:T(8,128)(2,1)S(1)}, bf16[64,256]{1,0:T(8,128)(2,1)}, u32[]{:S(2)}) copy-start(bf16[64,256]{1,0:T(8,128)(2,1)} %expand_ref.1) | copy-start | bytes 98308
  13.8 10.1 %copy-start.7 = (bf16[256,64]{0,1:T(8,128)(2,1)S(1)}, bf16[256,64]{0,1:T(8,128)(2,1)}, u32[]{:S(2)}) copy-start(bf16[256,64]{0,1:T(8,128)(2,1)} %param.36) | copy-start | bytes 98308
  13.8 10.1 %copy-start.8 = (bf16[4,8,320]{2,1,0:T(8,128)(2,1)S(1)}, bf16[4,8,320]{2,1,0:T(8,128)(2,1)}, u32[]{:S(2)}) copy-start(bf16[4,8,320]{2,1,0:T(8,128)(2,1)} %param.26) | copy-start | bytes 61444
  13.8 10.1 %copy-start.9 = (f32[9,256]{1,0:T(8,128)S(1)}, f32[9,256]{1,0:T(8,128)}, u32[]{:S(2)}) copy-start(f32[9,256]{1,0:T(8,128)} %depth_ref.1) | copy-start | bytes 27652
  13.8 10.1 %copy-start.10 = (f32[256]{0:T(256)S(1)}, f32[256]{0:T(256)}, u32[]{:S(2)}) copy-start(f32[256]{0:T(256)} %param.33) | copy-start | bytes 3076
  13.8 10.1 %copy-start.11 = (f32[256]{0:T(256)S(1)}, f32[256]{0:T(256)}, u32[]{:S(2)}) copy-start(f32[256]{0:T(256)} %param.35) | copy-start | bytes 3076
  13.8 10.1 %copy-start.12 = (f32[64]{0:T(128)S(1)}, f32[64]{0:T(128)}, u32[]{:S(2)}) copy-start(f32[64]{0:T(128)} %param.30) | copy-start | bytes 772
  13.8 10.1 %copy-start.13 = (f32[64]{0:T(128)S(1)}, f32[64]{0:T(128)}, u32[]{:S(2)}) copy-start(f32[64]{0:T(128)} %param.31) | copy-start | bytes 772
  13.9 10.1 %copy-start.14 = (f32[64]{0:T(128)S(1)}, f32[64]{0:T(128)}, u32[]{:S(2)}) copy-start(f32[64]{0:T(128)} %param.37) | copy-start | bytes 772
  18.2 5.4 %collective-permute-start.2 = (bf16[24,4,512]{2,1,0:T(4,128)(2,1)S(1)}, bf16[24,4,512]{2,1,0:T(4,128)(2,1)S(1)}, u32[]{:S(2)}, u32[]{:S(2)}) collective-permute-start(bf16[24,4,512]{2,1,0:T(4,128)(2,1)S(1)} %get-tuple-element.53), channel_id=1, source_target_pairs={{0,1},{1,0},{2,3},{3,2},{4,5},{5,4},{6,7},{7,6},{8,9},{9,8},{10,11... | collective-permute-start | bytes 294920 | tf_op jit(solution)/shard_map/ppermute | solution.py:444
  20.2 3.4 %collective-permute-start.3 = (bf16[24,4,512]{2,1,0:T(4,128)(2,1)S(1)}, bf16[24,4,512]{2,1,0:T(4,128)(2,1)S(1)}, u32[]{:S(2)}, u32[]{:S(2)}) collective-permute-start(bf16[24,4,512]{2,1,0:T(4,128)(2,1)S(1)} %get-tuple-element.54), channel_id=1, source_target_pairs={{1,2},{3,4},{5,6},{7,8},{9,10},{11,12},{13,14},{15,16},{17,18},{19... | collective-permute-start | bytes 294920 | tf_op jit(solution)/shard_map/ppermute | solution.py:443
  32.2 4.3 %collective-permute-start.4 = (f32[8,216,128]{2,1,0:T(8,128)S(1)}, f32[8,216,128]{2,1,0:T(8,128)S(1)}, u32[]{:S(2)}, u32[]{:S(2)}) collective-permute-start(f32[8,216,128]{2,1,0:T(8,128)S(1)} %get-tuple-element.30), channel_id=1, source_target_pairs={{0,32},{32,0},{64,96},{96,64},{128,160},{160,128},{192,224},{224,1... | collective-permute-start | bytes 2654216 | tf_op jit(solution)/shard_map/ppermute | solution.py:399
  88.4 17.8 %all-to-all-start.2 = ((f32[16,24,128]{2,1,0:T(8,128)}), f32[16,24,128]{2,1,0:T(8,128)S(1)}, u32[]{:S(2)}, u32[]{:S(2)}) async-start(f32[16,24,128]{2,1,0:T(8,128)} %get-tuple-element.32), calls=%async_computation.2 | async-start | bytes 393216 | tf_op jit(solution)/shard_map/all_to_all | solution.py:420

commit v4 on v3

v4 whole, which is shorter than its diff:
```python
import functools
import math

import jax
import jax.numpy as jnp
from jax import lax
from jax.experimental import pallas as pl
from jax.experimental.pallas import tpu as pltpu
from jax.sharding import PartitionSpec as P

D1 = 64
D2 = 128
D3 = 320
D4 = 512
HID = 256
DEC = 384
TH = 16
TW = 32

EDGE = 4
ROWS = TH + 2 * EDGE
PITCH = 48
USED = 40
COARSE = (128, 32, 8)

XS = 4
NEAR = 16
LINEAR_ROWS = 96
PART_ROWS = LINEAR_ROWS + 16

norm_eps = 1e-06
inv_root_two = 0.7071067811865476
inv_root_tau = 0.3989422804014327


def nt(left, right):
    return lax.dot_general(left, right, (((1,), (1,)), ((), ())), preferred_element_type=jnp.float32)


def tn(left, right):
    return lax.dot_general(left, right, (((0,), (0,)), ((), ())), preferred_element_type=jnp.float32)


def nn(left, right):
    return jnp.dot(left, right, preferred_element_type=jnp.float32)


def rest_row(n):
    return 8 * (n // 4) + 4 * (n // 2 % 2) + n % 2


def place(position, pitch):
    row = jnp.floor((position + 0.5) * (1.0 / pitch))
    col = position - pitch * row
    return row - EDGE, jnp.where(col < TW + EDGE, col, col - USED)


def regroup(channels_last):
    source = lax.broadcasted_iota(jnp.int32, (128, 128), 0)
    target = lax.broadcasted_iota(jnp.int32, (128, 128), 1)
    wanted = (
        (target & 64)
        + 8 * (target & 6)
        + ((target & 32) >> 2)
        + ((target & 24) >> 2)
        + (target & 1)
    )
    moves = jnp.where(source == wanted, 1.0, 0.0).astype(jnp.bfloat16)
    pieces = []
    for first in range(0, channels_last.shape[1], 128):
        piece = channels_last[:, first : first + 128]
        size = piece.shape[1]
        pieces.append(nn(piece, moves[0:size, 0:size]))
    return jnp.concatenate(pieces, axis=1).astype(jnp.bfloat16)


def pool_matrix(scale_index, row_index, col_index, height, width):
    factor = 2**scale_index
    coarse_rows, coarse_cols = TH // factor, TW // factor
    count = coarse_rows * coarse_cols
    position = lax.broadcasted_iota(jnp.int32, (1, ROWS * PITCH), 1).astype(jnp.float32)
    row, col = place(position, PITCH)
    target = lax.broadcasted_iota(jnp.int32, (count, 1), 0).astype(jnp.float32)
    target_row = jnp.floor((target + 0.5) * (1.0 / coarse_cols))
    target_col = target - coarse_cols * target_row
    row0 = (row_index * TH).astype(jnp.float32)
    col0 = (col_index * TW).astype(jnp.float32)
    at_row = jnp.clip((row + row0 + 0.5) * (1.0 / factor) - 0.5, 0.0, height // factor - 1.0)
    at_col = jnp.clip((col + col0 + 0.5) * (1.0 / factor) - 0.5, 0.0, width // factor - 1.0)
    at_row = at_row - row0 * (1.0 / factor)
    at_col = at_col - col0 * (1.0 / factor)
    weight = jnp.maximum(1.0 - jnp.abs(at_row - target_row), 0.0) * jnp.maximum(
        1.0 - jnp.abs(at_col - target_col), 0.0
    )
    return weight.astype(jnp.bfloat16)


def tile_kernel(
    height,
    width,
    joined_ref,
    block_ref,
    later_ref,
    top_ref,
    bottom_ref,
    side_ref,
    join_ref,
    first_ref,
    second_ref,
    third_ref,
    fourth_ref,
    feature2_ref,
    feature3_ref,
    feature4_ref,
    gain_ref,
    shift_ref,
    expand_ref,
    expand_bias_ref,
    depth_ref,
    depth_bias_ref,
    reduce_ref,
    reduce_bias_ref,
    input_grad_ref,
    grad2_ref,
    grad3_ref,
    grad4_ref,
    mine_ref,
    other_ref,
    wide_ref,
    wide_pair_ref,
    hid_ref,
    hid_before_ref,
    hid_after_ref,
    slope_ref,
    act_ref,
    pre_ref,
    pre_before_ref,
    pre_after_ref,
    hgrad_ref,
    linear_ref,
    rest_ref,
):
    row_index = lax.axis_index("row")
    col_index = lax.axis_index("col")
    scale_base = 1.0 / math.sqrt(height * width)

    wide_ref[EDGE : EDGE + TH, 0:TW] = joined_ref[...]
    wide_ref[0:EDGE, 0:TW] = top_ref[:, :, 0:DEC]
    wide_ref[EDGE + TH :, 0:TW] = bottom_ref[:, :, 0:DEC]
    wide_ref[:, TW:] = side_ref[:, :, 0:DEC]
    wide_pair_ref[EDGE : EDGE + TH, 0:TW, 0:D1] = block_ref[...]
    wide_pair_ref[EDGE : EDGE + TH, 0:TW, D1:] = later_ref[...]
    wide_pair_ref[0:EDGE, 0:TW] = top_ref[:, :, DEC:]
    wide_pair_ref[EDGE + TH :, 0:TW] = bottom_ref[:, :, DEC:]
    wide_pair_ref[:, TW:] = side_ref[:, :, DEC:]
    rest_ref[...] = jnp.zeros_like(rest_ref)

    def keep_row(row, value):
        for piece in range(value.shape[1] // 128):
            at = rest_row(row + piece)
            rest_ref[at : at + 1, :] = value[:, 128 * piece : 128 * piece + 128]

    matrix = jnp.concatenate(
        [pool_matrix(k, row_index, col_index, height, width) for k in (1, 2, 3)], axis=0
    )
    pooled = nn(matrix, wide_ref[...].reshape(ROWS * PITCH, DEC)).astype(jnp.bfloat16)
    start = 0
    base = D1
    for k, linear, feature, grad in (
        (1, second_ref, feature2_ref, grad2_ref),
        (2, third_ref, feature3_ref, grad3_ref),
        (3, fourth_ref, feature4_ref, grad4_ref),
    ):
        count = COARSE[k - 1]
        channels = linear.shape[0]
        projection = nt(pooled[start : start + count], join_ref[k * DEC : (k + 1) * DEC, :]).astype(
            jnp.bfloat16
        )
        grad[...] = nt(projection, linear[...]).astype(jnp.bfloat16)
        linear_ref[base : base + channels, :] = tn(regroup(feature[...]), projection) * (2**k * scale_base)
        keep_row(
            3 * k,
            jnp.sum(projection.astype(jnp.float32), 0, keepdims=True) * (2**k * scale_base),
        )
        start += count
        base += channels

    values = wide_pair_ref[2:22, :, 0:D1].astype(jnp.float32)
    values = values[:, 0:USED].reshape(20 * USED, D1)
    center = jnp.mean(values, -1, keepdims=True)
    offset = values - center
    spread = jnp.mean(jnp.square(offset), -1, keepdims=True)
    scaling = lax.rsqrt(spread + norm_eps)
    standard = offset * scaling
    normed = (standard * gain_ref[...] + shift_ref[...]).astype(jnp.bfloat16)

    def inside(first, rows):
        position = lax.broadcasted_iota(jnp.int32, (rows * USED, 1), 0).astype(jnp.float32)
        row, col = place(position + first * USED, USED)
        row = row + (row_index * TH).astype(jnp.float32)
        col = col + (col_index * TW).astype(jnp.float32)
        good = (row >= 0.0) & (row < height) & (col >= 0.0) & (col < width)
        return jnp.where(good, 1.0, 0.0)

    hidden = (nn(normed, expand_ref[...]) + expand_bias_ref[...]).astype(jnp.bfloat16)
    hid_ref[...] = (hidden.astype(jnp.float32) * inside(2, 20)).reshape(20, USED, HID)

    def shift_hidden(i, carry):
        row = hid_ref[i]
        hid_before_ref[i] = pltpu.roll(row, 1, 0)
        hid_after_ref[i] = pltpu.roll(row, USED - 1, 0)
        return carry

    lax.fori_loop(0, 20, shift_hidden, 0)
    hid_refs = (hid_before_ref, hid_ref, hid_after_ref)

    def conv_row(i, carry):
        conv = jnp.broadcast_to(depth_bias_ref[...], (USED, HID))
        for a in range(3):
            for b in range(3):
                conv = conv + depth_ref[3 * a + b : 3 * a + b + 1, :] * hid_refs[b][i + a]
        cumulative = 0.5 * (1.0 + lax.erf(conv * inv_root_two))
        density = inv_root_tau * jnp.exp(-0.5 * conv * conv)
        act_ref[i] = (conv * cumulative)[0:TW].astype(jnp.bfloat16)
        slope_ref[i] = cumulative + conv * density
        return carry

    lax.fori_loop(0, 18, conv_row, 0)

    def own(value, rows, pitch):
        first = (rows - TH) // 2
        channels = value.shape[-1]
        return value.reshape(rows, pitch, channels)[first : first + TH, 0:TW].reshape(
            TH * TW, channels
        )

    projection = nt(wide_ref[3:21].reshape(18 * PITCH, DEC), join_ref[0:DEC, :]).astype(jnp.bfloat16)
    later = wide_pair_ref[3:21, :, D1:].reshape(18 * PITCH, D1).astype(jnp.float32)
    feature_grad = (nt(projection, first_ref[...]) + later).astype(jnp.bfloat16)
    act_grad = nn(feature_grad, reduce_ref[...])
    act_grad = act_grad.reshape(18, PITCH, HID)[:, 0:USED]
    pre_grad = (act_grad * slope_ref[...]).astype(jnp.bfloat16).astype(jnp.float32)
    pre_ref[...] = pre_grad * inside(3, 18).reshape(18, USED, 1)

    activated = act_ref[1:17].reshape(TH * TW, HID)
    own_projection = own(projection, 18, PITCH)
    own_grad = own(feature_grad, 18, PITCH)
    own_block = block_ref[...].reshape(TH * TW, D1).astype(jnp.float32)
    features = (own_block + (nt(activated, reduce_ref[...]) + reduce_bias_ref[...])).astype(
        jnp.bfloat16
    )
    linear_ref[0:D1, :] = tn(regroup(features), own_projection) * scale_base
    keep_row(0, jnp.sum(own_projection.astype(jnp.float32), 0, keepdims=True) * scale_base)
    reduce_part = tn(own_grad, activated) * scale_base

    def shift_pre(i, carry):
        row = pre_ref[i]
        pre_before_ref[i] = pltpu.roll(row, 1, 0)
        pre_after_ref[i] = pltpu.roll(row, USED - 1, 0)
        return carry

    lax.fori_loop(0, 18, shift_pre, 0)
    pre_refs = (pre_after_ref, pre_ref, pre_before_ref)

    def fold(value):
        return jnp.sum(value.reshape(TW // 8, 8, HID), 0)

    def grad_row(i, sums):
        total = jnp.zeros((TW, HID), jnp.float32)
        center_row = pre_ref[i + 1, 0:TW, :]
        taps = []
        for a in range(3):
            for b in range(3):
                tap = 3 * a + b
                total = total + depth_ref[tap : tap + 1, :] * pre_refs[b][i + 2 - a, 0:TW, :]
                taps.append(sums[tap] + fold(hid_refs[b][i + 1 + a, 0:TW, :] * center_row))
        rounded = total.astype(jnp.bfloat16)
        hgrad_ref[i] = rounded
        taps.append(sums[9] + fold(rounded.astype(jnp.float32)))
        taps.append(sums[10] + fold(center_row))
        return tuple(taps)

    sums = lax.fori_loop(0, TH, grad_row, (jnp.zeros((8, HID), jnp.float32),) * 11)
    for n in range(11):
        keep_row(12 + 2 * n, jnp.sum(sums[n], 0, keepdims=True) * scale_base)

    hidden_grad = hgrad_ref[...].reshape(TH * TW, HID)
    own_normed = own(normed.astype(jnp.float32), 20, USED).astype(jnp.bfloat16)
    own_standard = own(standard, 20, USED)
    own_scaling = own(jnp.broadcast_to(scaling, (20 * USED, D1)), 20, USED)
    expand_part = tn(own_normed, hidden_grad) * scale_base
    normed_grad = nt(hidden_grad, expand_ref[...])
    fgrad = own_grad.astype(jnp.float32)
    for n, value in enumerate((fgrad, normed_grad * own_standard, normed_grad)):
        at = rest_row(34 + n)
        rest_ref[at : at + 1, 0:D1] = jnp.sum(value, 0, keepdims=True) * scale_base
    scaled = normed_grad * gain_ref[...]
    input_grad = fgrad + own_scaling * (
        scaled
        - jnp.mean(scaled, -1, keepdims=True)
        - own_standard * jnp.mean(scaled * own_standard, -1, keepdims=True)
    )
    input_grad_ref[...] = input_grad.astype(jnp.bfloat16).reshape(TH, TW, D1)

    even_core = row_index % 2 == 0

    def keep(part, at, even, odd):
        mine_ref[part, at : at + 8, :] = jnp.where(even_core, even, odd)
        other_ref[part, at : at + 8, :] = jnp.where(even_core, odd, even)

    upper = lax.broadcasted_iota(jnp.int32, (8, 128), 0) < 4
    for part in range(NEAR):
        zl, within = part // 8, 8 * (part % 8)
        at = 0
        for zh in range(4):
            first = 128 * (2 * zh + zl) + within
            for j in range(3):
                lanes = slice(128 * j, 128 * j + 128)
                keep(
                    part,
                    at,
                    linear_ref[first : first + 8, lanes],
                    linear_ref[first + 64 : first + 72, lanes],
                )
                at += 8
        lanes = slice(0, 128) if part < 8 else slice(128, 256)
        expand = expand_part[within : within + 8, lanes]
        reduce = reduce_part[within : within + 8, lanes]
        keep(
            part,
            at,
            jnp.where(upper, expand, pltpu.roll(reduce, 4, 0)),
            jnp.where(upper, pltpu.roll(expand, 4, 0), reduce),
        )
        rest = rest_ref[8 * part : 8 * part + 8, :]
        keep(part, at + 8, rest, pltpu.roll(rest, 4, 0))


def border_kernel(
    joined_ref, block_ref, later_ref, far_ref, near_ref, joined_buf, block_buf, later_buf, sems
):
    copies = []
    for n, (source, target) in enumerate(
        ((joined_ref, joined_buf), (block_ref, block_buf), (later_ref, later_buf))
    ):
        for last in range(2):
            rows = slice(TH - EDGE, TH) if last else slice(0, EDGE)
            copy = pltpu.make_async_copy(source.at[rows], target.at[last], sems.at[2 * n + last])
            copy.start()
            copies.append(copy)
    for copy in copies:
        copy.wait()
    even = lax.axis_index("row") % 2 == 0
    for buf, lanes in (
        (joined_buf, slice(0, DEC)),
        (block_buf, slice(DEC, DEC + D1)),
        (later_buf, slice(DEC + D1, DEC + 2 * D1)),
    ):
        first = buf[0].astype(jnp.float32)
        last = buf[1].astype(jnp.float32)
        far_ref[:, :, lanes] = jnp.where(even, first, last).astype(jnp.bfloat16)
        near_ref[:, :, lanes] = jnp.where(even, last, first).astype(jnp.bfloat16)


def row_borders(joined, block, later):
    vmem = pl.BlockSpec(memory_space=pltpu.VMEM)
    out = jax.ShapeDtypeStruct((EDGE, TW, DEC + 2 * D1), jnp.bfloat16)
    return pl.pallas_call(
        border_kernel,
        out_shape=(out, out),
        in_specs=[pl.BlockSpec(memory_space=pltpu.HBM)] * 3,
        out_specs=(vmem, vmem),
        scratch_shapes=[pltpu.VMEM((2, EDGE) + a.shape[1:], a.dtype) for a in (joined, block, later)]
        + [pltpu.SemaphoreType.DMA((6,))],
        compiler_params=pltpu.CompilerParams(vmem_limit_bytes=56 * 2**20),
        name="row_borders",
    )(joined, block, later)


def tile_pass(height, width, *operands):
    sds = jax.ShapeDtypeStruct
    bf16, f32 = jnp.bfloat16, jnp.float32
    vmem = pltpu.VMEM
    return pl.pallas_call(
        functools.partial(tile_kernel, height, width),
        out_shape=(
            sds((TH, TW, D1), bf16),
            sds((COARSE[0], D2), bf16),
            sds((COARSE[1], D3), bf16),
            sds((COARSE[2], D4), bf16),
            sds((NEAR, PART_ROWS, 128), f32),
            sds((NEAR, PART_ROWS, 128), f32),
        ),
        in_specs=[pl.BlockSpec(memory_space=vmem)] * len(operands),
        out_specs=(pl.BlockSpec(memory_space=vmem),) * 6,
        scratch_shapes=[
            vmem((ROWS, PITCH, DEC), bf16),
            vmem((ROWS, PITCH, 2 * D1), bf16),
            vmem((20, USED, HID), f32),
            vmem((20, USED, HID), f32),
            vmem((20, USED, HID), f32),
            vmem((18, USED, HID), f32),
            vmem((18, TW, HID), bf16),
            vmem((18, USED, HID), f32),
            vmem((18, USED, HID), f32),
            vmem((18, USED, HID), f32),
            vmem((TH, TW, HID), bf16),
            vmem((D1 + D2 + D3 + D4, DEC), f32),
            vmem((128, 128), f32),
        ],
        compiler_params=pltpu.CompilerParams(vmem_limit_bytes=50 * 2**20),
        name="tile_pass",
    )(*operands)


def near_kernel(received_ref, out_ref):
    total = jnp.sum(received_ref[...].astype(jnp.float32), 0)
    share = total[LINEAR_ROWS : LINEAR_ROWS + 8]
    rest = total[LINEAR_ROWS + 8 :]
    rest = pltpu.roll(rest + pltpu.roll(rest, 4, 0), 6, 0)
    row = lax.broadcasted_iota(jnp.int32, (8, 128), 0)
    for zh in range(4):
        pieces = [total[24 * zh + 8 * j : 24 * zh + 8 * j + 8] for j in range(3)]
        for yh in range(4):
            part = rest
            for j in range(3):
                shift = (2 * j - 2 * yh) % 8
                moved = pltpu.roll(pieces[j], shift, 0) if shift else pieces[j]
                part = jnp.where((row >= 2 * j) & (row < 2 * j + 2), moved, part)
            out_ref[4 * zh + yh, 0:8, :] = part
            out_ref[4 * zh + yh, 8:16, :] = share


def final_kernel(received_ref, linear_ref, out_ref):
    total = jnp.sum(received_ref[...], 0)
    for p in range(2):
        for j in range(3):
            linear_ref[3 * p + j : 3 * p + j + 1, :] = total[2 * j + p : 2 * j + p + 1, :]
    rest = pltpu.roll(total[0:8], 2, 0)
    for n in range(out_ref.shape[0]):
        out_ref[n, 0:8, :] = total[8:16]
        out_ref[n, 8:16, :] = rest


def small_kernel(all_ref, biases_ref, expand_ref, reduce_ref, depth_ref, hidden_ref, channel_ref):
    upper = lax.broadcasted_iota(jnp.int32, (8, 128), 0) < 4
    for part in range(NEAR):
        lanes = slice(0, 128) if part < 8 else slice(128, 256)
        rows = slice(8 * (part % 8), 8 * (part % 8) + 8)
        even, odd = all_ref[2 * part, 0:8, :], all_ref[2 * part + 1, 0:8, :]
        expand_ref[rows, lanes] = jnp.where(upper, even, pltpu.roll(odd, 4, 0))
        reduce_ref[rows, lanes] = jnp.where(upper, pltpu.roll(even, 4, 0), odd)

    def row(n):
        return all_ref[n // 2, 8 + n % 2 : 9 + n % 2, :]

    for k in range(4):
        for j in range(3):
            biases_ref[k : k + 1, 128 * j : 128 * j + 128] = row(3 * k + j)
    for t in range(9):
        for j in range(2):
            depth_ref[t : t + 1, 128 * j : 128 * j + 128] = row(12 + 2 * t + j)
    for t in range(2):
        for j in range(2):
            hidden_ref[t : t + 1, 128 * j : 128 * j + 128] = row(30 + 2 * t + j)
    for t in range(3):
        channel_ref[t : t + 1, :] = row(34 + t)[:, 0:D1]


def in_vmem(kernel, name, out_shape, *operands, scratch=()):
    vmem = pl.BlockSpec(memory_space=pltpu.VMEM)
    return pl.pallas_call(
        kernel,
        out_shape=out_shape,
        in_specs=[vmem] * len(operands),
        out_specs=jax.tree.map(lambda _: vmem, out_shape),
        scratch_shapes=scratch,
        compiler_params=pltpu.CompilerParams(vmem_limit_bytes=16 * 2**20),
        name=name,
    )(*operands)


def chip_kernel(mine_ref, received_ref, out_ref):
    plain = LINEAR_ROWS + 8
    total = mine_ref[:, 0:plain, :] + received_ref[:, 0:plain, :]
    rest = mine_ref[:, plain:, :] + received_ref[:, plain:, :]
    high = rest.astype(jnp.bfloat16).astype(jnp.float32)
    row = lax.broadcasted_iota(jnp.int32, rest.shape, 1)
    low = jnp.where(row < 2, rest - high, 0.0)
    both = jnp.where(row < 2, high, pltpu.roll(low, 4, 1))
    out_ref[...] = jnp.concatenate([total, both], axis=1).astype(jnp.bfloat16)


def device_groups(chips, cols):
    half_z, half_y = range(chips // 2), range(cols // XS // 2)
    two, xs = range(2), range(XS)

    def device(zh, zl, core, yh, yl, x):
        return (2 * (2 * zh + zl) + core) * cols + XS * (2 * yh + yl) + x

    near = [
        [device(zh, zl, core, yh, yl, x) for zl in two for yl in two for x in xs]
        for core in two
        for zh in half_z
        for yh in half_y
    ]
    far = [
        [device(zh, zl, core, yh, yl, x) for zh in half_z for yh in half_y]
        for core in two
        for zl in two
        for yl in two
        for x in xs
    ]
    both = [
        [device(zh, zl, core, yh, yl, x) for zl in two for yl in two for x in xs for core in two]
        for zh in half_z
        for yh in half_y
    ]
    return near, far, both


def sum_over_mesh(mine, other):
    rows = lax.axis_size("row")
    cols = lax.axis_size("col")
    sds = jax.ShapeDtypeStruct
    f32 = jnp.float32
    near, far, both = device_groups(rows // 2, cols)

    def exchange(parts, groups):
        return lax.all_to_all(parts, ("row", "col"), 0, 0, tiled=True, axis_index_groups=groups)

    received = lax.ppermute(other, "row", [(i, i ^ 1) for i in range(rows)])
    chip = in_vmem(chip_kernel, "chip_sums", sds(mine.shape, jnp.bfloat16), mine, received)
    parts = in_vmem(near_kernel, "near_sums", sds((16, 16, 128), f32), exchange(chip, near))
    linear, share = in_vmem(
        final_kernel,
        "final_sums",
        (sds((6, 128), f32), sds((2 * NEAR, 16, 128), f32)),
        exchange(parts, far),
    )
    everything = exchange(share, both)
    biases, expand, reduce, depth, hidden, channel = in_vmem(
        small_kernel,
        "small_sums",
        (
            sds((4, DEC), f32),
            sds((D1, HID), f32),
            sds((D1, HID), f32),
            sds((9, HID), f32),
            sds((2, HID), f32),
            sds((3, D1), f32),
        ),
        everything,
    )
    return linear.reshape(-1), (biases, expand, reduce.T, depth, hidden, channel)


def swap_edges(to_far, to_near, axis):
    devices = lax.axis_size(axis)
    even = lax.axis_index(axis) % 2 == 0
    near = [(i, i ^ 1) for i in range(devices)]
    far = [(i, i + 1) for i in range(1, devices - 1, 2)]
    far = far + [(j, i) for i, j in far]
    from_far = lax.ppermute(to_far, axis, far)
    from_near = lax.ppermute(to_near, axis, near)
    return jnp.where(even, from_far, from_near), jnp.where(even, from_near, from_far)


def local(
    joined_grad,
    join_weight,
    linear_first,
    linear_second,
    linear_third,
    linear_fourth,
    feature_second,
    feature_third,
    feature_fourth,
    block_input,
    later_grad,
    norm_gain,
    norm_shift,
    expand_weight,
    expand_bias,
    depth_weight,
    depth_bias,
    reduce_weight,
    reduce_bias,
):
    height = TH * lax.axis_size("row")
    width = TW * lax.axis_size("col")
    top, bottom = swap_edges(*row_borders(joined_grad, block_input, later_grad), "row")

    def columns(cols):
        own = jnp.concatenate(
            [array[:, cols] for array in (joined_grad, block_input, later_grad)], axis=2
        )
        return jnp.concatenate([top[:, cols], own, bottom[:, cols]], axis=0)

    first, last = columns(slice(0, EDGE)), columns(slice(TW - EDGE, TW))
    even = lax.axis_index("col") % 2 == 0
    left, right = swap_edges(jnp.where(even, first, last), jnp.where(even, last, first), "col")
    gap = jnp.zeros((ROWS, PITCH - TW - 2 * EDGE, left.shape[2]), left.dtype)
    side = jnp.concatenate([right, left, gap], axis=1)

    input_grad, grad2, grad3, grad4, mine, other = tile_pass(
        height,
        width,
        joined_grad,
        block_input,
        later_grad,
        top,
        bottom,
        side,
        join_weight,
        linear_first,
        linear_second,
        linear_third,
        linear_fourth,
        feature_second.reshape(-1, D2),
        feature_third.reshape(-1, D3),
        feature_fourth.reshape(-1, D4),
        norm_gain.reshape(1, -1),
        norm_shift.reshape(1, -1),
        expand_weight,
        expand_bias.reshape(1, -1),
        depth_weight,
        depth_bias.reshape(1, -1),
        reduce_weight.T,
        reduce_bias.reshape(1, -1),
    )
    linear_grads, small = sum_over_mesh(mine, other)
    return (
        input_grad,
        grad2.reshape(TH // 2, TW // 2, D2),
        grad3.reshape(TH // 4, TW // 4, D3),
        grad4.reshape(TH // 8, TW // 8, D4),
        linear_grads,
        *small,
    )


def solution(mesh):
    tiles = P("row", "col", None)
    return jax.shard_map(
        local,
        mesh=mesh,
        in_specs=(tiles,) + (P(),) * 5 + (tiles,) * 5 + (P(),) * 8,
        out_specs=(tiles,) * 4 + (P(("row", "col")),) + (P(),) * 6,
        check_vma=False,
    )
```

time: 107 us -> 94.5 us (0.88)
  blocking collectives: 50.8 us -> 42.9 us
  waiting for transfers between devices: 19 us -> 13.6 us
  Pallas kernels: 9.99 us -> 12 us
  starting transfers between devices: 22.6 us -> 21.2 us
    all_to_all x2, blocking collectives: 50.8 us -> 42.9 us  [exchange(): lax.all_to_all(parts, ('row', 'col'), 0, 0, tiled=True, axis_index_groups...]
    ppermute x4, waiting for transfers between devices: 6.83 us -> 3.6 us  [the longest x2 3.6 us: swap_edges(): from_near = lax.ppermute(to_near, axis, near)]
    all_to_all x1, waiting for transfers between devices: 9.77 us -> 7.93 us  [exchange(): lax.all_to_all(parts, ('row', 'col'), 0, 0, tiled=True, axis_index_groups...]
    pallas_call x0 -> x1, Pallas kernels: none -> 1.8 us  [row_borders(): pl.pallas_call(border_kernel, out_shape=(out, out), in_specs=[pl.BlockSpe...]
    ppermute x4, starting transfers between devices: 13.3 us -> 12 us  [the longest x2 6.06 us: swap_edges(): from_far = lax.ppermute(to_far, axis, far)]
    concatenate x4 -> x1, other arithmetic: 1.25 us -> 0.17 us  [local(): side = jnp.concatenate([right, left, gap], axis=1)]
  transfers between devices with their start and end apart: 6 -> 6, of which waited for: 4 -> 3; matrix products, arithmetic and copies ran while one was open for 1% -> 3% of each run, Pallas kernels for 0% -> 0%
where the time goes in v4:
time: 94.5 us; the launch traced here: 94 us
  blocking collectives  42.9 us (45%)
  starting transfers between devices  21.2 us (22%)
  waiting for transfers between devices  13.6 us (14%)
  Pallas kernels  12 us (13%)
  local copies, waits for them, and re-layouts  2.67 us (3%)
  between operations  1.1 us (1%)
    all_to_all x2, blocking collectives, exchange(): lax.all_to_all(parts, ('row', 'col'), 0, 0, tiled=True, axis_index_groups...  42.9 us
    pallas_call x1, Pallas kernels, tile_pass(): pl.pallas_call(functools.partial(tile_kernel, height, width), out_shape=(...  8.59 us
    all_to_all x1, waiting for transfers between devices, exchange(): lax.all_to_all(parts, ('row', 'col'), 0, 0, tiled=True, axis_index_groups...  7.93 us
    all_to_all x1, starting transfers between devices, exchange(): lax.all_to_all(parts, ('row', 'col'), 0, 0, tiled=True, axis_index_groups...  6.48 us
    ppermute x2, starting transfers between devices, swap_edges(): from_far = lax.ppermute(to_far, axis, far)  6.06 us
    ppermute x2, starting transfers between devices, swap_edges(): from_near = lax.ppermute(to_near, axis, near)  5.99 us
    ppermute x2, waiting for transfers between devices, swap_edges(): from_near = lax.ppermute(to_near, axis, near)  3.6 us
    ppermute x1, starting transfers between devices, sum_over_mesh(): received = lax.ppermute(other, 'row', [(i, i ^ 1) for i in range(rows)])  2.69 us
  transfers between devices with their start and end apart: 6, of which 3 were waited for; matrix products, arithmetic and copies ran while one was open for 3% of the time, Pallas kernels for 0%

profile of v4, /device:TPU:1, one launch (start us, length us, event | category | flops | bytes accessed | tf_op | source)
XLA Modules:
  0.0 94.0 jit_solution(5889711341750965363)
XLA Ops:
  0.7 1.8 %row_borders.1 = (bf16[4,32,512]{2,1,0:T(8,128)(2,1)}, bf16[4,32,512]{2,1,0:T(8,128)(2,1)}) custom-call(bf16[16,32,384]{2,1,0:T(8,128)(2,1)} %joined_ref.3, bf16[16,32,64]{2,1,0:T(8,128)(2,1)} %block_ref.3, bf16[16,32,64]{2,1,0:T(8,128)(2,1)} %later_ref.3), custom_call_target="tpu_custom_call" | custom-call | tf_op jit(solution)/shard_map/row_borders/pallas_call | solution.py:368
  2.5 5.4 %collective-permute-start = (bf16[4,32,512]{2,1,0:T(8,128)(2,1)}, bf16[4,32,512]{2,1,0:T(8,128)(2,1)S(1)}, u32[]{:S(2)}, u32[]{:S(2)}) collective-permute-start(bf16[4,32,512]{2,1,0:T(8,128)(2,1)} %get-tuple-element.27), channel_id=1, source_target_pairs={{32,64},{96,128},{160,192},{224,256},{288,320},{352,384},{416,448}... | collective-permute-start | bytes 393224 | tf_op jit(solution)/shard_map/ppermute | solution.py:564
  7.9 4.1 %collective-permute-start.1 = (bf16[4,32,512]{2,1,0:T(8,128)(2,1)}, bf16[4,32,512]{2,1,0:T(8,128)(2,1)S(1)}, u32[]{:S(2)}, u32[]{:S(2)}) collective-permute-start(bf16[4,32,512]{2,1,0:T(8,128)(2,1)} %get-tuple-element.28), channel_id=1, source_target_pairs={{0,32},{32,0},{64,96},{96,64},{128,160},{160,128},{192,224},{224,1... | collective-permute-start | bytes 393224 | tf_op jit(solution)/shard_map/ppermute | solution.py:565
  11.9 1.0 %fusion = (bf16[16,4,384]{2,1,0:T(4,128)(2,1)S(1)}, bf16[16,4,384]{2,1,0:T(4,128)(2,1)S(1)}) fusion(bf16[16,32,384]{2,1,0:T(8,128)(2,1)} %joined_ref.3), kind=kLoop, calls=%fused_computation.9 | loop fusion | bytes 196608 | tf_op jit(solution)/shard_map/slice | solution.py:596
  12.9 0.8 fusion.2
  14.1 0.1 broadcast_select_fusion.4
  14.2 0.1 broadcast_select_fusion.5
  14.3 1.9 %collective-permute-start.2 = (bf16[24,4,512]{2,1,0:T(4,128)(2,1)S(1)}, bf16[24,4,512]{2,1,0:T(4,128)(2,1)S(1)}, u32[]{:S(2)}, u32[]{:S(2)}) collective-permute-start(bf16[24,4,512]{2,1,0:T(4,128)(2,1)S(1)} %broadcast_select_fusion.5), channel_id=1, source_target_pairs={{0,1},{1,0},{2,3},{3,2},{4,5},{5,4},{6,7},{7,6},{8,9},{9,8},{10,11... | collective-permute-start | bytes 294920 | tf_op jit(solution)/shard_map/ppermute | solution.py:565
  16.3 0.7 collective-permute-start.3
  17.0 0.1 pad.2.clone
  17.1 3.6 %collective-permute-done.2 = bf16[24,4,512]{2,1,0:T(4,128)(2,1)S(1)} collective-permute-done((bf16[24,4,512]{2,1,0:T(4,128)(2,1)S(1)}, bf16[24,4,512]{2,1,0:T(4,128)(2,1)S(1)}, u32[]{:S(2)}, u32[]{:S(2)}) %collective-permute-start.2) | collective-permute-done | bytes 98336 | tf_op jit(solution)/shard_map/ppermute | solution.py:565
  20.7 0.2 maximum_maximum_fusion.side_ref
  21.0 8.6 %tile_pass.1 = (bf16[16,32,64]{2,1,0:T(8,128)(2,1)}, bf16[128,128]{1,0:T(8,128)(2,1)}, bf16[32,320]{1,0:T(8,128)(2,1)}, bf16[8,512]{1,0:T(8,128)(2,1)S(1)}, f32[...) custom-call(bf16[16,32,384]{2,1,0:T(8,128)(2,1)S(1)} %copy-done, bf16[16,32,64]{2,1,0:T(8,128)(2,1)S(1)} %copy-done.1, ...), custom_call_target="tpu_custom_call" | custom-call | tf_op jit(solution)/shard_map/tile_pass/pallas_call | solution.py:384
  29.6 2.7 %collective-permute-start.4 = (f32[16,112,128]{2,1,0:T(8,128)S(1)}, f32[16,112,128]{2,1,0:T(8,128)S(1)}, u32[]{:S(2)}, u32[]{:S(2)}) collective-permute-start(f32[16,112,128]{2,1,0:T(8,128)S(1)} %get-tuple-element.34), channel_id=1, source_target_pairs={{0,32},{32,0},{64,96},{96,64},{128,160},{160,128},{192,224},{224,1... | collective-permute-start | bytes 2752520 | tf_op jit(solution)/shard_map/ppermute | solution.py:532
  32.3 2.1 %collective-permute-done.4.received_ref = f32[16,112,128]{2,1,0:T(8,128)S(1)} collective-permute-done((f32[16,112,128]{2,1,0:T(8,128)S(1)}, f32[16,112,128]{2,1,0:T(8,128)S(1)}, u32[]{:S(2)}, u32[]{:S(2)}) %collective-permute-start.4) | collective-permute-done | bytes 917536 | tf_op jit(solution)/shard_map/ppermute | solution.py:532
  34.4 0.1 chip_sums.1
  34.5 18.9 %all_to_all.15.received_ref = bf16[16,112,128]{2,1,0:T(8,128)(2,1)S(1)} all-to-all(bf16[16,112,128]{2,1,0:T(8,128)(2,1)S(1)} %chip_sums.1), channel_id=1, replica_groups={{0,1,2,3,4,5,6,7,64,65,66,67,68,69,70,71},{8,9,10,11,12,13,14,15,72,73,..., dimensions={0} | all-to-all | bytes 917504 | tf_op jit(solution)/shard_map/all_to_all | solution.py:530
  53.4 0.1 near_sums.1
  53.5 24.0 %all_to_all.16.received_ref = f32[16,16,128]{2,1,0:T(8,128)S(1)} all-to-all(f32[16,16,128]{2,1,0:T(8,128)S(1)} %near_sums.1), channel_id=1, replica_groups={{0,8,16,24,128,136,144,152,256,264,272,280,384,392,400,408},{1,9,17,25,..., dimensions={0} | all-to-all | bytes 262144 | tf_op jit(solution)/shard_map/all_to_all | solution.py:530
  77.5 0.7 final_sums.1
  78.3 6.5 %all-to-all-start.2 = ((f32[32,16,128]{2,1,0:T(8,128)}), f32[32,16,128]{2,1,0:T(8,128)S(1)}, u32[]{:S(2)}, u32[]{:S(2)}) async-start(f32[32,16,128]{2,1,0:T(8,128)} %get-tuple-element.36), calls=%async_computation.2 | async-start | bytes 524288 | tf_op jit(solution)/shard_map/all_to_all | solution.py:530
  84.7 0.6 reshape.68
  85.4 7.9 %all-to-all-done.2.all_ref = f32[32,16,128]{2,1,0:T(8,128)S(1)} async-done(((f32[32,16,128]{2,1,0:T(8,128)}), f32[32,16,128]{2,1,0:T(8,128)S(1)}, u32[]{:S(2)}, u32[]{:S(2)}) %all-to-all-start.2) | async-done | bytes 262176 | tf_op jit(solution)/shard_map/all_to_all | solution.py:530
  93.3 0.7 small_sums.1
  (44 shorter events, 0.2 us)
Async XLA Ops:
  0.6 16.3 %copy-start.17 = (bf16[2,4,512]{2,1,0:T(4,128)(2,1)S(1)}, bf16[2,4,512]{2,1,0:T(4,128)(2,1)}, u32[]{:S(2)}) copy-start(bf16[2,4,512]{2,1,0:T(4,128)(2,1)} %param.27) | copy-start | bytes 24580
  2.5 11.5 %collective-permute-start = (bf16[4,32,512]{2,1,0:T(8,128)(2,1)}, bf16[4,32,512]{2,1,0:T(8,128)(2,1)S(1)}, u32[]{:S(2)}, u32[]{:S(2)}) collective-permute-start(bf16[4,32,512]{2,1,0:T(8,128)(2,1)} %get-tuple-element.27), channel_id=1, source_target_pairs={{32,64},{96,128},{160,192},{224,256},{288,320},{352,384},{416,448}... | collective-permute-start | bytes 393224 | tf_op jit(solution)/shard_map/ppermute | solution.py:564
  7.9 6.2 %collective-permute-start.1 = (bf16[4,32,512]{2,1,0:T(8,128)(2,1)}, bf16[4,32,512]{2,1,0:T(8,128)(2,1)S(1)}, u32[]{:S(2)}, u32[]{:S(2)}) collective-permute-start(bf16[4,32,512]{2,1,0:T(8,128)(2,1)} %get-tuple-element.28), channel_id=1, source_target_pairs={{0,32},{32,0},{64,96},{96,64},{128,160},{160,128},{192,224},{224,1... | collective-permute-start | bytes 393224 | tf_op jit(solution)/shard_map/ppermute | solution.py:565
  13.8 7.1 %copy-start = (bf16[16,32,384]{2,1,0:T(8,128)(2,1)S(1)}, bf16[16,32,384]{2,1,0:T(8,128)(2,1)}, u32[]{:S(2)}) copy-start(bf16[16,32,384]{2,1,0:T(8,128)(2,1)} %joined_ref.3) | copy-start | bytes 1179652
  13.8 7.1 %copy-start.1 = (bf16[16,32,64]{2,1,0:T(8,128)(2,1)S(1)}, bf16[16,32,64]{2,1,0:T(8,128)(2,1)}, u32[]{:S(2)}) copy-start(bf16[16,32,64]{2,1,0:T(8,128)(2,1)} %block_ref.3) | copy-start | bytes 196612
  13.8 7.1 %copy-start.2 = (bf16[16,32,64]{2,1,0:T(8,128)(2,1)S(1)}, bf16[16,32,64]{2,1,0:T(8,128)(2,1)}, u32[]{:S(2)}) copy-start(bf16[16,32,64]{2,1,0:T(8,128)(2,1)} %later_ref.3) | copy-start | bytes 196612
  13.8 7.1 %copy-start.3 = (bf16[512,384]{1,0:T(8,128)(2,1)S(1)}, bf16[512,384]{1,0:T(8,128)(2,1)}, u32[]{:S(2)}) copy-start(bf16[512,384]{1,0:T(8,128)(2,1)} %fourth_ref.1) | copy-start | bytes 1179652
  13.8 7.1 %copy-start.4 = (bf16[320,384]{1,0:T(8,128)(2,1)S(1)}, bf16[320,384]{1,0:T(8,128)(2,1)}, u32[]{:S(2)}) copy-start(bf16[320,384]{1,0:T(8,128)(2,1)} %third_ref.1) | copy-start | bytes 737284
  13.9 7.1 %copy-start.5 = (bf16[128,384]{1,0:T(8,128)(2,1)S(1)}, bf16[128,384]{1,0:T(8,128)(2,1)}, u32[]{:S(2)}) copy-start(bf16[128,384]{1,0:T(8,128)(2,1)} %second_ref.1) | copy-start | bytes 294916
  13.9 7.1 %copy-start.6 = (bf16[64,384]{1,0:T(8,128)(2,1)S(1)}, bf16[64,384]{1,0:T(8,128)(2,1)}, u32[]{:S(2)}) copy-start(bf16[64,384]{1,0:T(8,128)(2,1)} %first_ref.1) | copy-start | bytes 147460
  13.9 7.0 %copy-start.7 = (bf16[8,16,128]{2,1,0:T(8,128)(2,1)S(1)}, bf16[8,16,128]{2,1,0:T(8,128)(2,1)}, u32[]{:S(2)}) copy-start(bf16[8,16,128]{2,1,0:T(8,128)(2,1)} %param.25) | copy-start | bytes 98308
  13.9 7.0 %copy-start.8 = (bf16[64,256]{1,0:T(8,128)(2,1)S(1)}, bf16[64,256]{1,0:T(8,128)(2,1)}, u32[]{:S(2)}) copy-start(bf16[64,256]{1,0:T(8,128)(2,1)} %expand_ref.1) | copy-start | bytes 98308
  13.9 7.0 %copy-start.9 = (bf16[256,64]{0,1:T(8,128)(2,1)S(1)}, bf16[256,64]{0,1:T(8,128)(2,1)}, u32[]{:S(2)}) copy-start(bf16[256,64]{0,1:T(8,128)(2,1)} %param.36) | copy-start | bytes 98308
  13.9 7.0 %copy-start.10 = (bf16[4,8,320]{2,1,0:T(8,128)(2,1)S(1)}, bf16[4,8,320]{2,1,0:T(8,128)(2,1)}, u32[]{:S(2)}) copy-start(bf16[4,8,320]{2,1,0:T(8,128)(2,1)} %param.26) | copy-start | bytes 61444
  13.9 7.0 %copy-start.11 = (f32[9,256]{1,0:T(8,128)S(1)}, f32[9,256]{1,0:T(8,128)}, u32[]{:S(2)}) copy-start(f32[9,256]{1,0:T(8,128)} %depth_ref.1) | copy-start | bytes 27652
  13.9 7.0 %copy-start.12 = (f32[256]{0:T(256)S(1)}, f32[256]{0:T(256)}, u32[]{:S(2)}) copy-start(f32[256]{0:T(256)} %param.33) | copy-start | bytes 3076
  14.0 7.0 %copy-start.13 = (f32[256]{0:T(256)S(1)}, f32[256]{0:T(256)}, u32[]{:S(2)}) copy-start(f32[256]{0:T(256)} %param.35) | copy-start | bytes 3076
  14.0 7.0 %copy-start.14 = (f32[64]{0:T(128)S(1)}, f32[64]{0:T(128)}, u32[]{:S(2)}) copy-start(f32[64]{0:T(128)} %param.30) | copy-start | bytes 772
  14.0 7.0 %copy-start.15 = (f32[64]{0:T(128)S(1)}, f32[64]{0:T(128)}, u32[]{:S(2)}) copy-start(f32[64]{0:T(128)} %param.31) | copy-start | bytes 772
  14.0 7.0 %copy-start.16 = (f32[64]{0:T(128)S(1)}, f32[64]{0:T(128)}, u32[]{:S(2)}) copy-start(f32[64]{0:T(128)} %param.37) | copy-start | bytes 772
  14.3 6.3 %collective-permute-start.2 = (bf16[24,4,512]{2,1,0:T(4,128)(2,1)S(1)}, bf16[24,4,512]{2,1,0:T(4,128)(2,1)S(1)}, u32[]{:S(2)}, u32[]{:S(2)}) collective-permute-start(bf16[24,4,512]{2,1,0:T(4,128)(2,1)S(1)} %broadcast_select_fusion.5), channel_id=1, source_target_pairs={{0,1},{1,0},{2,3},{3,2},{4,5},{5,4},{6,7},{7,6},{8,9},{9,8},{10,11... | collective-permute-start | bytes 294920 | tf_op jit(solution)/shard_map/ppermute | solution.py:565
  16.3 4.4 %collective-permute-start.3 = (bf16[24,4,512]{2,1,0:T(4,128)(2,1)S(1)}, bf16[24,4,512]{2,1,0:T(4,128)(2,1)S(1)}, u32[]{:S(2)}, u32[]{:S(2)}) collective-permute-start(bf16[24,4,512]{2,1,0:T(4,128)(2,1)S(1)} %broadcast_select_fusion.4), channel_id=1, source_target_pairs={{1,2},{3,4},{5,6},{7,8},{9,10},{11,12},{13,14},{15,16},{17,18},{19... | collective-permute-start | bytes 294920 | tf_op jit(solution)/shard_map/ppermute | solution.py:564
  29.6 4.8 %collective-permute-start.4 = (f32[16,112,128]{2,1,0:T(8,128)S(1)}, f32[16,112,128]{2,1,0:T(8,128)S(1)}, u32[]{:S(2)}, u32[]{:S(2)}) collective-permute-start(f32[16,112,128]{2,1,0:T(8,128)S(1)} %get-tuple-element.34), channel_id=1, source_target_pairs={{0,32},{32,0},{64,96},{96,64},{128,160},{160,128},{192,224},{224,1... | collective-permute-start | bytes 2752520 | tf_op jit(solution)/shard_map/ppermute | solution.py:532
  78.3 15.0 %all-to-all-start.2 = ((f32[32,16,128]{2,1,0:T(8,128)}), f32[32,16,128]{2,1,0:T(8,128)S(1)}, u32[]{:S(2)}, u32[]{:S(2)}) async-start(f32[32,16,128]{2,1,0:T(8,128)} %get-tuple-element.36), calls=%async_computation.2 | async-start | bytes 524288 | tf_op jit(solution)/shard_map/all_to_all | solution.py:530

commit v5 on v4

--- a/solution.py
+++ b/solution.py
@@ -52,7 +52,36 @@
 def place(position, pitch):
     row = jnp.floor((position + 0.5) * (1.0 / pitch))
     col = position - pitch * row
-    return row - EDGE, jnp.where(col < TW + EDGE, col, col - USED)
+    if pitch < TW:
+        col = jnp.where(col < EDGE, col + TW, col - 2 * EDGE)
+    elif pitch > TW:
+        col = jnp.where(col < TW + EDGE, col, col - USED)
+    return row - EDGE, col
+
+
+def count_up(shape, axis):
+    return lax.broadcasted_iota(jnp.int32, shape, axis).astype(jnp.float32)
+
+
+def inside(first, rows, pitch, height, width):
+    row, col = place(count_up((rows * pitch, 1), 0) + first * pitch, pitch)
+    row = row + (lax.axis_index("row") * TH).astype(jnp.float32)
+    col = col + (lax.axis_index("col") * TW).astype(jnp.float32)
+    good = (row >= 0.0) & (row < height) & (col >= 0.0) & (col < width)
+    return jnp.where(good, 1.0, 0.0)
+
+
+def normalize(values, gain, shift):
+    center = jnp.mean(values, -1, keepdims=True)
+    offset = values - center
+    spread = jnp.mean(jnp.square(offset), -1, keepdims=True)
+    scaling = lax.rsqrt(spread + norm_eps)
+    standard = offset * scaling
+    return (standard * gain + shift).astype(jnp.bfloat16), standard, scaling
+
+
+def expand(normed, weight, bias):
+    return (nn(normed, weight) + bias).astype(jnp.bfloat16).astype(jnp.float32)
 
 
 def regroup(channels_last):
@@ -74,13 +103,24 @@
     return jnp.concatenate(pieces, axis=1).astype(jnp.bfloat16)
 
 
-def pool_matrix(scale_index, row_index, col_index, height, width):
+def split_rest(rest):
+    axis = rest.ndim - 2
+    row = lax.broadcasted_iota(jnp.int32, rest.shape, axis)
+    high = rest.astype(jnp.bfloat16).astype(jnp.float32)
+    low = jnp.where(row < 2, rest - high, 0.0)
+    return jnp.where(row < 2, high, pltpu.roll(low, 4, axis))
+
+
+def join_rest(rest):
+    return rest + pltpu.roll(rest, 4, rest.ndim - 2)
+
+
+def pool_matrix(scale_index, pitch, row_index, col_index, height, width):
     factor = 2**scale_index
     coarse_rows, coarse_cols = TH // factor, TW // factor
     count = coarse_rows * coarse_cols
-    position = lax.broadcasted_iota(jnp.int32, (1, ROWS * PITCH), 1).astype(jnp.float32)
-    row, col = place(position, PITCH)
-    target = lax.broadcasted_iota(jnp.int32, (count, 1), 0).astype(jnp.float32)
+    row, col = place(count_up((1, ROWS * pitch), 1), pitch)
+    target = count_up((count, 1), 0)
     target_row = jnp.floor((target + 0.5) * (1.0 / coarse_cols))
     target_col = target - coarse_cols * target_row
     row0 = (row_index * TH).astype(jnp.float32)
@@ -95,10 +135,106 @@
     return weight.astype(jnp.bfloat16)
 
 
+def own_kernel(
+    height,
+    width,
+    joined_ref,
+    block_ref,
+    top_ref,
+    bottom_ref,
+    join_ref,
+    gain_ref,
+    shift_ref,
+    expand_ref,
+    expand_bias_ref,
+    feature2_ref,
+    feature3_ref,
+    feature4_ref,
+    pooled_ref,
+    side_matrix_ref,
+    projection_ref,
+    hidden_ref,
+    normed_ref,
+    standard_ref,
+    scaling_ref,
+    grouped2_ref,
+    grouped3_ref,
+    grouped4_ref,
+    wide_ref,
+):
+    row_index = lax.axis_index("row")
+    col_index = lax.axis_index("col")
+    wide_ref[EDGE : EDGE + TH] = joined_ref[...]
+    wide_ref[0:EDGE] = top_ref[:, :, 0:DEC]
+    wide_ref[EDGE + TH :] = bottom_ref[:, :, 0:DEC]
+
+    def matrix(pitch):
+        return jnp.concatenate(
+            [pool_matrix(k, pitch, row_index, col_index, height, width) for k in (1, 2, 3)], axis=0
+        )
+
+    pooled_ref[...] = nn(matrix(TW), wide_ref[...].reshape(ROWS * TW, DEC))
+    side_matrix_ref[...] = matrix(PITCH - TW)
+    projection_ref[...] = (
+        nt(wide_ref[3:21].reshape(18 * TW, DEC), join_ref[0:DEC, :])
+        .astype(jnp.bfloat16)
+        .reshape(18, TW, DEC)
+    )
+
+    values = jnp.concatenate(
+        [top_ref[2:4, :, DEC : DEC + D1], block_ref[...], bottom_ref[0:2, :, DEC : DEC + D1]], axis=0
+    )
+    normed, standard, scaling = normalize(
+        values.reshape(20 * TW, D1).astype(jnp.float32), gain_ref[...], shift_ref[...]
+    )
+    hidden = expand(normed, expand_ref[...], expand_bias_ref[...])
+    hidden_ref[...] = (hidden * inside(2, 20, TW, height, width)).reshape(20, TW, HID)
+    own = slice(2 * TW, 18 * TW)
+    normed_ref[...] = normed[own]
+    standard_ref[...] = standard[own]
+    scaling_ref[...] = jnp.broadcast_to(scaling[own], (TH * TW, D1))
+    grouped2_ref[...] = regroup(feature2_ref[...])
+    grouped3_ref[...] = regroup(feature3_ref[...])
+    grouped4_ref[...] = regroup(feature4_ref[...])
+
+
+def own_pass(height, width, *operands):
+    sds = jax.ShapeDtypeStruct
+    bf16, f32 = jnp.bfloat16, jnp.float32
+    pixels = TH * TW
+    return in_vmem(
+        functools.partial(own_kernel, height, width),
+        "own_pass",
+        (
+            sds((sum(COARSE), DEC), f32),
+            sds((sum(COARSE), ROWS * (PITCH - TW)), bf16),
+            sds((18, TW, DEC), bf16),
+            sds((20, TW, HID), f32),
+            sds((pixels, D1), bf16),
+            sds((pixels, D1), f32),
+            sds((pixels, D1), f32),
+            sds((COARSE[0], D2), bf16),
+            sds((COARSE[1], D3), bf16),
+            sds((COARSE[2], D4), bf16),
+        ),
+        *operands,
+        scratch=[pltpu.VMEM((ROWS, TW, DEC), bf16)],
+    )
+
+
 def tile_kernel(
     height,
     width,
-    joined_ref,
+    pooled_ref,
+    side_matrix_ref,
+    own_projection_ref,
+    own_hidden_ref,
+    normed_ref,
+    standard_ref,
+    scaling_ref,
+    feature2_ref,
+    feature3_ref,
+    feature4_ref,
     block_ref,
     later_ref,
     top_ref,
@@ -109,9 +245,6 @@
     second_ref,
     third_ref,
     fourth_ref,
-    feature2_ref,
-    feature3_ref,
-    feature4_ref,
     gain_ref,
     shift_ref,
     expand_ref,
@@ -126,33 +259,24 @@
     grad4_ref,
     mine_ref,
     other_ref,
-    wide_ref,
-    wide_pair_ref,
+    projection_ref,
+    wide_later_ref,
     hid_ref,
-    hid_before_ref,
-    hid_after_ref,
     slope_ref,
     act_ref,
     pre_ref,
-    pre_before_ref,
-    pre_after_ref,
     hgrad_ref,
     linear_ref,
     rest_ref,
 ):
     row_index = lax.axis_index("row")
-    col_index = lax.axis_index("col")
     scale_base = 1.0 / math.sqrt(height * width)
 
-    wide_ref[EDGE : EDGE + TH, 0:TW] = joined_ref[...]
-    wide_ref[0:EDGE, 0:TW] = top_ref[:, :, 0:DEC]
-    wide_ref[EDGE + TH :, 0:TW] = bottom_ref[:, :, 0:DEC]
-    wide_ref[:, TW:] = side_ref[:, :, 0:DEC]
-    wide_pair_ref[EDGE : EDGE + TH, 0:TW, 0:D1] = block_ref[...]
-    wide_pair_ref[EDGE : EDGE + TH, 0:TW, D1:] = later_ref[...]
-    wide_pair_ref[0:EDGE, 0:TW] = top_ref[:, :, DEC:]
-    wide_pair_ref[EDGE + TH :, 0:TW] = bottom_ref[:, :, DEC:]
-    wide_pair_ref[:, TW:] = side_ref[:, :, DEC:]
+    later_lanes = slice(DEC + D1, DEC + 2 * D1)
+    wide_later_ref[1 : 1 + TH, 0:TW] = later_ref[...]
+    wide_later_ref[0:1, 0:TW] = top_ref[EDGE - 1 :, :, later_lanes]
+    wide_later_ref[1 + TH :, 0:TW] = bottom_ref[0:1, :, later_lanes]
+    wide_later_ref[:, TW:] = side_ref[3:21, :, later_lanes]
     rest_ref[...] = jnp.zeros_like(rest_ref)
 
     def keep_row(row, value):
@@ -160,10 +284,8 @@
             at = rest_row(row + piece)
             rest_ref[at : at + 1, :] = value[:, 128 * piece : 128 * piece + 128]
 
-    matrix = jnp.concatenate(
-        [pool_matrix(k, row_index, col_index, height, width) for k in (1, 2, 3)], axis=0
-    )
-    pooled = nn(matrix, wide_ref[...].reshape(ROWS * PITCH, DEC)).astype(jnp.bfloat16)
+    side_joined = side_ref[:, :, 0:DEC].reshape(ROWS * (PITCH - TW), DEC)
+    pooled = (pooled_ref[...] + nn(side_matrix_ref[...], side_joined)).astype(jnp.bfloat16)
     start = 0
     base = D1
     for k, linear, feature, grad in (
@@ -177,7 +299,7 @@
             jnp.bfloat16
         )
         grad[...] = nt(projection, linear[...]).astype(jnp.bfloat16)
-        linear_ref[base : base + channels, :] = tn(regroup(feature[...]), projection) * (2**k * scale_base)
+        linear_ref[base : base + channels, :] = tn(feature[...], projection) * (2**k * scale_base)
         keep_row(
             3 * k,
             jnp.sum(projection.astype(jnp.float32), 0, keepdims=True) * (2**k * scale_base),
@@ -185,40 +307,22 @@
         start += count
         base += channels
 
-    values = wide_pair_ref[2:22, :, 0:D1].astype(jnp.float32)
-    values = values[:, 0:USED].reshape(20 * USED, D1)
-    center = jnp.mean(values, -1, keepdims=True)
-    offset = values - center
-    spread = jnp.mean(jnp.square(offset), -1, keepdims=True)
-    scaling = lax.rsqrt(spread + norm_eps)
-    standard = offset * scaling
-    normed = (standard * gain_ref[...] + shift_ref[...]).astype(jnp.bfloat16)
-
-    def inside(first, rows):
-        position = lax.broadcasted_iota(jnp.int32, (rows * USED, 1), 0).astype(jnp.float32)
-        row, col = place(position + first * USED, USED)
-        row = row + (row_index * TH).astype(jnp.float32)
-        col = col + (col_index * TW).astype(jnp.float32)
-        good = (row >= 0.0) & (row < height) & (col >= 0.0) & (col < width)
-        return jnp.where(good, 1.0, 0.0)
-
-    hidden = (nn(normed, expand_ref[...]) + expand_bias_ref[...]).astype(jnp.bfloat16)
-    hid_ref[...] = (hidden.astype(jnp.float32) * inside(2, 20)).reshape(20, USED, HID)
-
-    def shift_hidden(i, carry):
-        row = hid_ref[i]
-        hid_before_ref[i] = pltpu.roll(row, 1, 0)
-        hid_after_ref[i] = pltpu.roll(row, USED - 1, 0)
-        return carry
-
-    lax.fori_loop(0, 20, shift_hidden, 0)
-    hid_refs = (hid_before_ref, hid_ref, hid_after_ref)
+    values = side_ref[2:22, :, DEC : DEC + D1].astype(jnp.float32)[:, 0 : 2 * EDGE]
+    normed, _, _ = normalize(values.reshape(20 * 2 * EDGE, D1), gain_ref[...], shift_ref[...])
+    hidden = expand(normed, expand_ref[...], expand_bias_ref[...])
+    hid_ref[:, 0:TW] = own_hidden_ref[...]
+    hid_ref[:, TW:] = (hidden * inside(2, 20, 2 * EDGE, height, width)).reshape(20, 2 * EDGE, HID)
+
+    def across(before, same, after):
+        return pltpu.roll(before, 1, 0) + same + pltpu.roll(after, USED - 1, 0)
 
     def conv_row(i, carry):
-        conv = jnp.broadcast_to(depth_bias_ref[...], (USED, HID))
-        for a in range(3):
-            for b in range(3):
-                conv = conv + depth_ref[3 * a + b : 3 * a + b + 1, :] * hid_refs[b][i + a]
+        rows = [hid_ref[i + a] for a in range(3)]
+        sums = [
+            sum(depth_ref[3 * a + b : 3 * a + b + 1, :] * rows[a] for a in range(3))
+            for b in range(3)
+        ]
+        conv = across(*sums) + depth_bias_ref[...]
         cumulative = 0.5 * (1.0 + lax.erf(conv * inv_root_two))
         density = inv_root_tau * jnp.exp(-0.5 * conv * conv)
         act_ref[i] = (conv * cumulative)[0:TW].astype(jnp.bfloat16)
@@ -234,16 +338,21 @@
             TH * TW, channels
         )
 
-    projection = nt(wide_ref[3:21].reshape(18 * PITCH, DEC), join_ref[0:DEC, :]).astype(jnp.bfloat16)
-    later = wide_pair_ref[3:21, :, D1:].reshape(18 * PITCH, D1).astype(jnp.float32)
+    side_projection = nt(
+        side_ref[3:21, :, 0:DEC].reshape(18 * (PITCH - TW), DEC), join_ref[0:DEC, :]
+    ).astype(jnp.bfloat16)
+    projection_ref[:, 0:TW] = own_projection_ref[...]
+    projection_ref[:, TW:] = side_projection.reshape(18, PITCH - TW, DEC)
+    projection = projection_ref[...].reshape(18 * PITCH, DEC)
+    later = wide_later_ref[...].reshape(18 * PITCH, D1).astype(jnp.float32)
     feature_grad = (nt(projection, first_ref[...]) + later).astype(jnp.bfloat16)
     act_grad = nn(feature_grad, reduce_ref[...])
     act_grad = act_grad.reshape(18, PITCH, HID)[:, 0:USED]
     pre_grad = (act_grad * slope_ref[...]).astype(jnp.bfloat16).astype(jnp.float32)
-    pre_ref[...] = pre_grad * inside(3, 18).reshape(18, USED, 1)
+    pre_ref[...] = pre_grad * inside(3, 18, USED, height, width).reshape(18, USED, 1)
 
     activated = act_ref[1:17].reshape(TH * TW, HID)
-    own_projection = own(projection, 18, PITCH)
+    own_projection = own_projection_ref[1 : 1 + TH].reshape(TH * TW, DEC)
     own_grad = own(feature_grad, 18, PITCH)
     own_block = block_ref[...].reshape(TH * TW, D1).astype(jnp.float32)
     features = (own_block + (nt(activated, reduce_ref[...]) + reduce_bias_ref[...])).astype(
@@ -253,27 +362,24 @@
     keep_row(0, jnp.sum(own_projection.astype(jnp.float32), 0, keepdims=True) * scale_base)
     reduce_part = tn(own_grad, activated) * scale_base
 
-    def shift_pre(i, carry):
-        row = pre_ref[i]
-        pre_before_ref[i] = pltpu.roll(row, 1, 0)
-        pre_after_ref[i] = pltpu.roll(row, USED - 1, 0)
-        return carry
-
-    lax.fori_loop(0, 18, shift_pre, 0)
-    pre_refs = (pre_after_ref, pre_ref, pre_before_ref)
-
     def fold(value):
-        return jnp.sum(value.reshape(TW // 8, 8, HID), 0)
+        return jnp.sum(value.reshape(-1, 8, HID), 0)
 
     def grad_row(i, sums):
-        total = jnp.zeros((TW, HID), jnp.float32)
         center_row = pre_ref[i + 1, 0:TW, :]
+        own_row = jnp.concatenate([center_row, jnp.zeros((USED - TW, HID), jnp.float32)], axis=0)
+        rows = [pre_ref[i + 2 - a] for a in range(3)]
+        sums_b = [
+            sum(depth_ref[3 * a + b : 3 * a + b + 1, :] * rows[a] for a in range(3))
+            for b in range(3)
+        ]
+        total = across(sums_b[2], sums_b[1], sums_b[0])[0:TW]
+        moved = [pltpu.roll(own_row, USED - 1, 0), own_row, pltpu.roll(own_row, 1, 0)]
         taps = []
         for a in range(3):
+            hid_row = hid_ref[i + 1 + a]
             for b in range(3):
-                tap = 3 * a + b
-                total = total + depth_ref[tap : tap + 1, :] * pre_refs[b][i + 2 - a, 0:TW, :]
-                taps.append(sums[tap] + fold(hid_refs[b][i + 1 + a, 0:TW, :] * center_row))
+                taps.append(sums[3 * a + b] + fold(hid_row * moved[b]))
         rounded = total.astype(jnp.bfloat16)
         hgrad_ref[i] = rounded
         taps.append(sums[9] + fold(rounded.astype(jnp.float32)))
@@ -285,17 +391,15 @@
         keep_row(12 + 2 * n, jnp.sum(sums[n], 0, keepdims=True) * scale_base)
 
     hidden_grad = hgrad_ref[...].reshape(TH * TW, HID)
-    own_normed = own(normed.astype(jnp.float32), 20, USED).astype(jnp.bfloat16)
-    own_standard = own(standard, 20, USED)
-    own_scaling = own(jnp.broadcast_to(scaling, (20 * USED, D1)), 20, USED)
-    expand_part = tn(own_normed, hidden_grad) * scale_base
+    own_standard = standard_ref[...]
+    expand_part = tn(normed_ref[...], hidden_grad) * scale_base
     normed_grad = nt(hidden_grad, expand_ref[...])
     fgrad = own_grad.astype(jnp.float32)
     for n, value in enumerate((fgrad, normed_grad * own_standard, normed_grad)):
         at = rest_row(34 + n)
         rest_ref[at : at + 1, 0:D1] = jnp.sum(value, 0, keepdims=True) * scale_base
     scaled = normed_grad * gain_ref[...]
-    input_grad = fgrad + own_scaling * (
+    input_grad = fgrad + scaling_ref[...] * (
         scaled
         - jnp.mean(scaled, -1, keepdims=True)
         - own_standard * jnp.mean(scaled * own_standard, -1, keepdims=True)
@@ -304,39 +408,45 @@
 
     even_core = row_index % 2 == 0
 
-    def keep(part, at, even, odd):
-        mine_ref[part, at : at + 8, :] = jnp.where(even_core, even, odd)
-        other_ref[part, at : at + 8, :] = jnp.where(even_core, odd, even)
+    def keep(part, pairs):
+        for n in range(0, len(pairs), 2):
+            mine = [jnp.where(even_core, even, odd) for even, odd in pairs[n : n + 2]]
+            other = [jnp.where(even_core, odd, even) for even, odd in pairs[n : n + 2]]
+            if n + 2 == len(pairs):
+                other[1] = split_rest(other[1])
+            at = slice(8 * n, 8 * n + 16)
+            mine_ref[part, at, :] = jnp.concatenate(mine, axis=0)
+            other_ref[part, at, :] = jnp.concatenate(other, axis=0).astype(jnp.bfloat16)
 
     upper = lax.broadcasted_iota(jnp.int32, (8, 128), 0) < 4
     for part in range(NEAR):
         zl, within = part // 8, 8 * (part % 8)
-        at = 0
+        pairs = []
         for zh in range(4):
             first = 128 * (2 * zh + zl) + within
             for j in range(3):
                 lanes = slice(128 * j, 128 * j + 128)
-                keep(
-                    part,
-                    at,
-                    linear_ref[first : first + 8, lanes],
-                    linear_ref[first + 64 : first + 72, lanes],
+                pairs.append(
+                    (
+                        linear_ref[first : first + 8, lanes],
+                        linear_ref[first + 64 : first + 72, lanes],
+                    )
                 )
-                at += 8
         lanes = slice(0, 128) if part < 8 else slice(128, 256)
-        expand = expand_part[within : within + 8, lanes]
-        reduce = reduce_part[within : within + 8, lanes]
-        keep(
-            part,
-            at,
-            jnp.where(upper, expand, pltpu.roll(reduce, 4, 0)),
-            jnp.where(upper, pltpu.roll(expand, 4, 0), reduce),
+        expands = expand_part[within : within + 8, lanes]
+        reduces = reduce_part[within : within + 8, lanes]
+        pairs.append(
+            (
+                jnp.where(upper, expands, pltpu.roll(reduces, 4, 0)),
+                jnp.where(upper, pltpu.roll(expands, 4, 0), reduces),
+            )
         )
         rest = rest_ref[8 * part : 8 * part + 8, :]
-        keep(part, at + 8, rest, pltpu.roll(rest, 4, 0))
-
-
-def border_kernel(
+        pairs.append((rest, pltpu.roll(rest, 4, 0)))
+        keep(part, pairs)
+
+
+def row_kernel(
     joined_ref, block_ref, later_ref, far_ref, near_ref, joined_buf, block_buf, later_buf, sems
 ):
     copies = []
@@ -366,7 +476,7 @@
     vmem = pl.BlockSpec(memory_space=pltpu.VMEM)
     out = jax.ShapeDtypeStruct((EDGE, TW, DEC + 2 * D1), jnp.bfloat16)
     return pl.pallas_call(
-        border_kernel,
+        row_kernel,
         out_shape=(out, out),
         in_specs=[pl.BlockSpec(memory_space=pltpu.HBM)] * 3,
         out_specs=(vmem, vmem),
@@ -375,6 +485,22 @@
         compiler_params=pltpu.CompilerParams(vmem_limit_bytes=56 * 2**20),
         name="row_borders",
     )(joined, block, later)
+
+
+def column_kernel(joined_ref, block_ref, later_ref, top_ref, bottom_ref, far_ref, near_ref):
+    even = lax.axis_index("col") % 2 == 0
+    own_rows = slice(EDGE, EDGE + TH)
+    for ref, rows, lanes in (
+        (joined_ref, own_rows, slice(0, DEC)),
+        (block_ref, own_rows, slice(DEC, DEC + D1)),
+        (later_ref, own_rows, slice(DEC + D1, DEC + 2 * D1)),
+        (top_ref, slice(0, EDGE), slice(0, DEC + 2 * D1)),
+        (bottom_ref, slice(EDGE + TH, ROWS), slice(0, DEC + 2 * D1)),
+    ):
+        first = ref[:, 0:16].astype(jnp.float32)[:, 0:EDGE]
+        last = ref[:, TW - 16 : TW].astype(jnp.float32)[:, 16 - EDGE : 16]
+        far_ref[rows, :, lanes] = jnp.where(even, first, last).astype(jnp.bfloat16)
+        near_ref[rows, :, lanes] = jnp.where(even, last, first).astype(jnp.bfloat16)
 
 
 def tile_pass(height, width, *operands):
@@ -389,26 +515,22 @@
             sds((COARSE[1], D3), bf16),
             sds((COARSE[2], D4), bf16),
             sds((NEAR, PART_ROWS, 128), f32),
-            sds((NEAR, PART_ROWS, 128), f32),
+            sds((NEAR, PART_ROWS, 128), bf16),
         ),
         in_specs=[pl.BlockSpec(memory_space=vmem)] * len(operands),
         out_specs=(pl.BlockSpec(memory_space=vmem),) * 6,
         scratch_shapes=[
-            vmem((ROWS, PITCH, DEC), bf16),
-            vmem((ROWS, PITCH, 2 * D1), bf16),
-            vmem((20, USED, HID), f32),
-            vmem((20, USED, HID), f32),
+            vmem((18, PITCH, DEC), bf16),
+            vmem((18, PITCH, D1), bf16),
             vmem((20, USED, HID), f32),
             vmem((18, USED, HID), f32),
             vmem((18, TW, HID), bf16),
-            vmem((18, USED, HID), f32),
-            vmem((18, USED, HID), f32),
             vmem((18, USED, HID), f32),
             vmem((TH, TW, HID), bf16),
             vmem((D1 + D2 + D3 + D4, DEC), f32),
             vmem((128, 128), f32),
         ],
-        compiler_params=pltpu.CompilerParams(vmem_limit_bytes=50 * 2**20),
+        compiler_params=pltpu.CompilerParams(vmem_limit_bytes=28 * 2**20),
         name="tile_pass",
     )(*operands)
 
@@ -417,7 +539,7 @@
     total = jnp.sum(received_ref[...].astype(jnp.float32), 0)
     share = total[LINEAR_ROWS : LINEAR_ROWS + 8]
     rest = total[LINEAR_ROWS + 8 :]
-    rest = pltpu.roll(rest + pltpu.roll(rest, 4, 0), 6, 0)
+    rest = pltpu.roll(join_rest(rest), 6, 0)
     row = lax.broadcasted_iota(jnp.int32, (8, 128), 0)
     for zh in range(4):
         pieces = [total[24 * zh + 8 * j : 24 * zh + 8 * j + 8] for j in range(3)]
@@ -436,23 +558,23 @@
     for p in range(2):
         for j in range(3):
             linear_ref[3 * p + j : 3 * p + j + 1, :] = total[2 * j + p : 2 * j + p + 1, :]
-    rest = pltpu.roll(total[0:8], 2, 0)
     for n in range(out_ref.shape[0]):
-        out_ref[n, 0:8, :] = total[8:16]
-        out_ref[n, 8:16, :] = rest
+        for i in range(4):
+            out_ref[n, i] = total[8 + 2 * i : 10 + 2 * i]
+        out_ref[n, 4] = total[6:8]
 
 
 def small_kernel(all_ref, biases_ref, expand_ref, reduce_ref, depth_ref, hidden_ref, channel_ref):
-    upper = lax.broadcasted_iota(jnp.int32, (8, 128), 0) < 4
-    for part in range(NEAR):
-        lanes = slice(0, 128) if part < 8 else slice(128, 256)
-        rows = slice(8 * (part % 8), 8 * (part % 8) + 8)
-        even, odd = all_ref[2 * part, 0:8, :], all_ref[2 * part + 1, 0:8, :]
-        expand_ref[rows, lanes] = jnp.where(upper, even, pltpu.roll(odd, 4, 0))
-        reduce_ref[rows, lanes] = jnp.where(upper, pltpu.roll(even, 4, 0), odd)
+    for share in range(2 * NEAR):
+        lanes = slice(0, 128) if share < NEAR else slice(128, 256)
+        first = 4 * (share % NEAR)
+        for i in range(2):
+            rows = slice(first + 2 * i, first + 2 * i + 2)
+            expand_ref[rows, lanes] = all_ref[share, i]
+            reduce_ref[rows, lanes] = all_ref[share, 2 + i]
 
     def row(n):
-        return all_ref[n // 2, 8 + n % 2 : 9 + n % 2, :]
+        return all_ref[n // 2, 4, n % 2 : n % 2 + 1, :]
 
     for k in range(4):
         for j in range(3):
@@ -482,13 +604,10 @@
 
 def chip_kernel(mine_ref, received_ref, out_ref):
     plain = LINEAR_ROWS + 8
-    total = mine_ref[:, 0:plain, :] + received_ref[:, 0:plain, :]
-    rest = mine_ref[:, plain:, :] + received_ref[:, plain:, :]
-    high = rest.astype(jnp.bfloat16).astype(jnp.float32)
-    row = lax.broadcasted_iota(jnp.int32, rest.shape, 1)
-    low = jnp.where(row < 2, rest - high, 0.0)
-    both = jnp.where(row < 2, high, pltpu.roll(low, 4, 1))
-    out_ref[...] = jnp.concatenate([total, both], axis=1).astype(jnp.bfloat16)
+    received = received_ref[...].astype(jnp.float32)
+    total = mine_ref[:, 0:plain, :] + received[:, 0:plain]
+    rest = split_rest(mine_ref[:, plain:, :] + join_rest(received[:, plain:]))
+    out_ref[...] = jnp.concatenate([total, rest], axis=1).astype(jnp.bfloat16)
 
 
 def device_groups(chips, cols):
@@ -530,12 +649,12 @@
         return lax.all_to_all(parts, ("row", "col"), 0, 0, tiled=True, axis_index_groups=groups)
 
     received = lax.ppermute(other, "row", [(i, i ^ 1) for i in range(rows)])
-    chip = in_vmem(chip_kernel, "chip_sums", sds(mine.shape, jnp.bfloat16), mine, received)
+    chip = in_vmem(chip_kernel, "chip_sums", sds(other.shape, other.dtype), mine, received)
     parts = in_vmem(near_kernel, "near_sums", sds((16, 16, 128), f32), exchange(chip, near))
     linear, share = in_vmem(
         final_kernel,
         "final_sums",
-        (sds((6, 128), f32), sds((2 * NEAR, 16, 128), f32)),
+        (sds((6, 128), f32), sds((2 * NEAR, 5, 2, 128), f32)),
         exchange(parts, far),
     )
     everything = exchange(share, both)
@@ -590,23 +709,43 @@
     height = TH * lax.axis_size("row")
     width = TW * lax.axis_size("col")
     top, bottom = swap_edges(*row_borders(joined_grad, block_input, later_grad), "row")
-
-    def columns(cols):
-        own = jnp.concatenate(
-            [array[:, cols] for array in (joined_grad, block_input, later_grad)], axis=2
-        )
-        return jnp.concatenate([top[:, cols], own, bottom[:, cols]], axis=0)
-
-    first, last = columns(slice(0, EDGE)), columns(slice(TW - EDGE, TW))
-    even = lax.axis_index("col") % 2 == 0
-    left, right = swap_edges(jnp.where(even, first, last), jnp.where(even, last, first), "col")
+    column = jax.ShapeDtypeStruct((ROWS, EDGE, DEC + 2 * D1), jnp.bfloat16)
+    left, right = swap_edges(
+        *in_vmem(
+            column_kernel,
+            "column_borders",
+            (column, column),
+            joined_grad,
+            block_input,
+            later_grad,
+            top,
+            bottom,
+        ),
+        "col",
+    )
+    early = own_pass(
+        height,
+        width,
+        joined_grad,
+        block_input,
+        top,
+        bottom,
+        join_weight,
+        norm_gain.reshape(1, -1),
+        norm_shift.reshape(1, -1),
+        expand_weight,
+        expand_bias.reshape(1, -1),
+        feature_second.reshape(-1, D2),
+        feature_third.reshape(-1, D3),
+        feature_fourth.reshape(-1, D4),
+    )
     gap = jnp.zeros((ROWS, PITCH - TW - 2 * EDGE, left.shape[2]), left.dtype)
     side = jnp.concatenate([right, left, gap], axis=1)
 
     input_grad, grad2, grad3, grad4, mine, other = tile_pass(
         height,
         width,
-        joined_grad,
+        *early,
         block_input,
         later_grad,
         top,
@@ -617,9 +756,6 @@
         linear_second,
         linear_third,
         linear_fourth,
-        feature_second.reshape(-1, D2),
-        feature_third.reshape(-1, D3),
-        feature_fourth.reshape(-1, D4),
         norm_gain.reshape(1, -1),
         norm_shift.reshape(1, -1),
         expand_weight,

time: 94.5 us -> 90.1 us (0.953)
  waiting for transfers between devices: 13.6 us -> 11.5 us
  local copies, waits for them, and re-layouts: 2.67 us -> 0.8 us
  Pallas kernels: 12 us -> 10.8 us
  blocking collectives: 42.9 us -> 44 us
    pallas_call x1, Pallas kernels: 8.59 us -> 5.99 us  [tile_pass(): pl.pallas_call(functools.partial(tile_kernel, height, width), out_shape=(...]
    slice x3 -> x0, local copies, waits for them, and re-layouts: 1.86 us -> none  [the longest x2 1.83 us: columns(): array[:, cols]]
    pallas_call x4 -> x6, Pallas kernels: 1.62 us -> 2.85 us  [in_vmem(): pl.pallas_call(kernel, out_shape=out_shape, in_specs=[vmem] * len(operand...]
    all_to_all x2, blocking collectives: 42.9 us -> 44 us  [exchange(): lax.all_to_all(parts, ('row', 'col'), 0, 0, tiled=True, axis_index_groups...]
    all_to_all x1, waiting for transfers between devices: 7.93 us -> 6.9 us  [exchange(): lax.all_to_all(parts, ('row', 'col'), 0, 0, tiled=True, axis_index_groups...]
  transfers between devices with their start and end apart: 6 -> 6, of which waited for: 3 -> 4; matrix products, arithmetic and copies ran while one was open for 3% -> 1% of each run, Pallas kernels for 0% -> 1%
where the time goes in v5:
time: 90.1 us; the launch traced here: 89.7 us
  blocking collectives  44 us (49%)
  starting transfers between devices  21.5 us (24%)
  waiting for transfers between devices  11.5 us (13%)
  Pallas kernels  10.8 us (12%)
  between operations  1.06 us (1%)
    all_to_all x2, blocking collectives, exchange(): lax.all_to_all(parts, ('row', 'col'), 0, 0, tiled=True, axis_index_groups...  44 us
    all_to_all x1, waiting for transfers between devices, exchange(): lax.all_to_all(parts, ('row', 'col'), 0, 0, tiled=True, axis_index_groups...  6.9 us
    all_to_all x1, starting transfers between devices, exchange(): lax.all_to_all(parts, ('row', 'col'), 0, 0, tiled=True, axis_index_groups...  6.34 us
    ppermute x2, starting transfers between devices, swap_edges(): from_far = lax.ppermute(to_far, axis, far)  6.06 us
    pallas_call x1, Pallas kernels, tile_pass(): pl.pallas_call(functools.partial(tile_kernel, height, width), out_shape=(...  5.99 us
    ppermute x2, starting transfers between devices, swap_edges(): from_near = lax.ppermute(to_near, axis, near)  5.99 us
    ppermute x2, waiting for transfers between devices, swap_edges(): from_near = lax.ppermute(to_near, axis, near)  3.13 us
    ppermute x1, starting transfers between devices, sum_over_mesh(): received = lax.ppermute(other, 'row', [(i, i ^ 1) for i in range(rows)])  3.09 us
  transfers between devices with their start and end apart: 6, of which 4 were waited for; matrix products, arithmetic and copies ran while one was open for 1% of the time, Pallas kernels for 1%

profile of v5, /device:TPU:1, one launch (start us, length us, event | category | flops | bytes accessed | tf_op | source)
XLA Modules:
  0.0 89.7 jit_solution(521267506004971286)
XLA Ops:
  0.8 1.9 %row_borders.1 = (bf16[4,32,512]{2,1,0:T(8,128)(2,1)}, bf16[4,32,512]{2,1,0:T(8,128)(2,1)}) custom-call(bf16[16,32,384]{2,1,0:T(8,128)(2,1)} %joined_ref.5, bf16[16,32,64]{2,1,0:T(8,128)(2,1)} %block_ref.7, bf16[16,32,64]{2,1,0:T(8,128)(2,1)} %later_ref.5), custom_call_target="tpu_custom_call" | custom-call | tf_op jit(solution)/shard_map/row_borders/pallas_call | solution.py:478
  2.7 5.4 %collective-permute-start = (bf16[4,32,512]{2,1,0:T(8,128)(2,1)}, bf16[4,32,512]{2,1,0:T(8,128)(2,1)S(1)}, u32[]{:S(2)}, u32[]{:S(2)}) collective-permute-start(bf16[4,32,512]{2,1,0:T(8,128)(2,1)} %get-tuple-element.39), channel_id=1, source_target_pairs={{32,64},{96,128},{160,192},{224,256},{288,320},{352,384},{416,448}... | collective-permute-start | bytes 393224 | tf_op jit(solution)/shard_map/ppermute | solution.py:683
  8.1 4.1 %collective-permute-start.1 = (bf16[4,32,512]{2,1,0:T(8,128)(2,1)}, bf16[4,32,512]{2,1,0:T(8,128)(2,1)S(1)}, u32[]{:S(2)}, u32[]{:S(2)}) collective-permute-start(bf16[4,32,512]{2,1,0:T(8,128)(2,1)} %get-tuple-element.40), channel_id=1, source_target_pairs={{0,32},{32,0},{64,96},{96,64},{128,160},{160,128},{192,224},{224,1... | collective-permute-start | bytes 393224 | tf_op jit(solution)/shard_map/ppermute | solution.py:684
  12.2 1.2 %collective-permute-done.1 = bf16[4,32,512]{2,1,0:T(8,128)(2,1)S(1)} collective-permute-done((bf16[4,32,512]{2,1,0:T(8,128)(2,1)}, bf16[4,32,512]{2,1,0:T(8,128)(2,1)S(1)}, u32[]{:S(2)}, u32[]{:S(2)}) %collective-permute-start.1) | collective-permute-done | bytes 131104 | tf_op jit(solution)/shard_map/ppermute | solution.py:684
  13.4 0.2 column_borders.1
  13.6 1.9 %collective-permute-start.2 = (bf16[24,4,512]{2,1,0:T(4,128)(2,1)S(1)}, bf16[24,4,512]{2,1,0:T(4,128)(2,1)S(1)}, u32[]{:S(2)}, u32[]{:S(2)}) collective-permute-start(bf16[24,4,512]{2,1,0:T(4,128)(2,1)S(1)} %get-tuple-element.51), channel_id=1, source_target_pairs={{0,1},{1,0},{2,3},{3,2},{4,5},{5,4},{6,7},{7,6},{8,9},{9,8},{10,11... | collective-permute-start | bytes 294920 | tf_op jit(solution)/shard_map/ppermute | solution.py:684
  15.5 0.7 collective-permute-start.3
  16.2 0.1 pad.2.clone
  16.3 0.0 copy-start.5
  16.4 1.1 %own_pass.1 = (f32[168,384]{1,0:T(8,128)S(1)}, bf16[168,384]{1,0:T(8,128)(2,1)S(1)}, bf16[18,32,384]{2,1,0:T(8,128)(2,1)S(1)}, f32[20,32,256]{2,1,0:T(8,128)S(1)...) custom-call(bf16[16,32,384]{2,1,0:T(8,128)(2,1)S(1)} %copy-done.1, ...), custom_call_target="tpu_custom_call" | custom-call | tf_op jit(solution)/shard_map/own_pass/pallas_call | solution.py:594
  17.5 2.0 %collective-permute-done.2 = bf16[24,4,512]{2,1,0:T(4,128)(2,1)S(1)} collective-permute-done((bf16[24,4,512]{2,1,0:T(4,128)(2,1)S(1)}, bf16[24,4,512]{2,1,0:T(4,128)(2,1)S(1)}, u32[]{:S(2)}, u32[]{:S(2)}) %collective-permute-start.2) | collective-permute-done | bytes 98336 | tf_op jit(solution)/shard_map/ppermute | solution.py:684
  19.5 0.2 maximum_maximum_fusion.side_ref
  19.8 6.0 %tile_pass.1 = (bf16[16,32,64]{2,1,0:T(8,128)(2,1)}, bf16[128,128]{1,0:T(8,128)(2,1)}, bf16[32,320]{1,0:T(8,128)(2,1)}, bf16[8,512]{1,0:T(8,128)(2,1)S(1)}, f32[...) custom-call(f32[168,384]{1,0:T(8,128)S(1)} %get-tuple-element.41.pooled_ref, ...), custom_call_target="tpu_custom_call" | custom-call | tf_op jit(solution)/shard_map/tile_pass/pallas_call | solution.py:510
  25.8 3.1 %collective-permute-start.4 = (bf16[16,112,128]{2,1,0:T(8,128)(2,1)S(1)}, bf16[16,112,128]{2,1,0:T(8,128)(2,1)S(1)}, u32[]{:S(2)}, u32[]{:S(2)}) collective-permute-start(bf16[16,112,128]{2,1,0:T(8,128)(2,1)S(1)} %get-tuple-element.58), channel_id=1, source_target_pairs={{0,32},{32,0},{64,96},{96,64},{128,160},{160,128},{192,224},{224,1... | collective-permute-start | bytes 1376264 | tf_op jit(solution)/shard_map/ppermute | solution.py:651
  28.9 1.4 %collective-permute-done.4.received_ref = bf16[16,112,128]{2,1,0:T(8,128)(2,1)S(1)} collective-permute-done((bf16[16,112,128]{2,1,0:T(8,128)(2,1)S(1)}, bf16[16,112,128]{2,1,0:T(8,128)(2,1)S(1)}, u32[]{:S(2)}, u32[]{:S(2)}) %collective-permute-start.4) | collective-permute-done | bytes 458784 | tf_op jit(solution)/shard_map/ppermute | solution.py:651
  30.3 0.1 chip_sums.1
  30.4 19.1 %all_to_all.15.received_ref = bf16[16,112,128]{2,1,0:T(8,128)(2,1)S(1)} all-to-all(bf16[16,112,128]{2,1,0:T(8,128)(2,1)S(1)} %chip_sums.1), channel_id=1, replica_groups={{0,1,2,3,4,5,6,7,64,65,66,67,68,69,70,71},{8,9,10,11,12,13,14,15,72,73,..., dimensions={0} | all-to-all | bytes 917504 | tf_op jit(solution)/shard_map/all_to_all | solution.py:649
  49.5 0.1 near_sums.1
  49.6 24.9 %all_to_all.16.received_ref = f32[16,16,128]{2,1,0:T(8,128)S(1)} all-to-all(f32[16,16,128]{2,1,0:T(8,128)S(1)} %near_sums.1), channel_id=1, replica_groups={{0,8,16,24,128,136,144,152,256,264,272,280,384,392,400,408},{1,9,17,25,..., dimensions={0} | all-to-all | bytes 262144 | tf_op jit(solution)/shard_map/all_to_all | solution.py:649
  74.5 0.7 final_sums.1
  75.2 6.3 %all-to-all-start.2 = ((f32[32,5,2,128]{3,2,1,0:T(2,128)}), f32[32,5,2,128]{3,2,1,0:T(2,128)S(1)}, u32[]{:S(2)}, u32[]{:S(2)}) async-start(f32[32,5,2,128]{3,2,1,0:T(2,128)} %get-tuple-element.60), calls=%async_computation.2 | async-start | bytes 327680 | tf_op jit(solution)/shard_map/all_to_all | solution.py:649
  81.5 0.6 reshape.71
  82.1 6.9 %all-to-all-done.2.all_ref = f32[32,5,2,128]{3,2,1,0:T(2,128)S(1)} async-done(((f32[32,5,2,128]{3,2,1,0:T(2,128)}), f32[32,5,2,128]{3,2,1,0:T(2,128)S(1)}, u32[]{:S(2)}, u32[]{:S(2)}) %all-to-all-start.2) | async-done | bytes 163872 | tf_op jit(solution)/shard_map/all_to_all | solution.py:649
  89.0 0.7 small_sums.1
  (43 shorter events, 0.2 us)
Async XLA Ops:
  0.6 12.7 %copy-start.2 = (bf16[16,32,64]{2,1,0:T(8,128)(2,1)S(1)}, bf16[16,32,64]{2,1,0:T(8,128)(2,1)}, u32[]{:S(2)}) copy-start(bf16[16,32,64]{2,1,0:T(8,128)(2,1)} %block_ref.7) | copy-start | bytes 196612
  0.7 12.7 %copy-start.3 = (bf16[16,32,64]{2,1,0:T(8,128)(2,1)S(1)}, bf16[16,32,64]{2,1,0:T(8,128)(2,1)}, u32[]{:S(2)}) copy-start(bf16[16,32,64]{2,1,0:T(8,128)(2,1)} %later_ref.5) | copy-start | bytes 196612
  0.7 12.7 %copy-start.1 = (bf16[16,32,384]{2,1,0:T(8,128)(2,1)S(1)}, bf16[16,32,384]{2,1,0:T(8,128)(2,1)}, u32[]{:S(2)}) copy-start(bf16[16,32,384]{2,1,0:T(8,128)(2,1)} %joined_ref.5) | copy-start | bytes 1179652
  0.7 15.5 %copy-start.18 = (bf16[2,4,512]{2,1,0:T(4,128)(2,1)S(1)}, bf16[2,4,512]{2,1,0:T(4,128)(2,1)}, u32[]{:S(2)}) copy-start(bf16[2,4,512]{2,1,0:T(4,128)(2,1)} %param.27) | copy-start | bytes 24580
  0.7 15.6 %copy-start.6 = (bf16[64,256]{1,0:T(8,128)(2,1)S(1)}, bf16[64,256]{1,0:T(8,128)(2,1)}, u32[]{:S(2)}) copy-start(bf16[64,256]{1,0:T(8,128)(2,1)} %expand_ref.3) | copy-start | bytes 98308
  0.7 15.6 %copy-start = (bf16[1536,384]{1,0:T(8,128)(2,1)S(1)}, bf16[1536,384]{1,0:T(8,128)(2,1)}, u32[]{:S(2)}) copy-start(bf16[1536,384]{1,0:T(8,128)(2,1)} %join_ref.3) | copy-start | bytes 3538948
  0.7 15.6 %copy-start.13 = (f32[256]{0:T(256)S(1)}, f32[256]{0:T(256)}, u32[]{:S(2)}) copy-start(f32[256]{0:T(256)} %param.33) | copy-start | bytes 3076
  0.7 15.6 %copy-start.15 = (f32[64]{0:T(128)S(1)}, f32[64]{0:T(128)}, u32[]{:S(2)}) copy-start(f32[64]{0:T(128)} %param.31) | copy-start | bytes 772
  0.7 15.6 %copy-start.14 = (f32[64]{0:T(128)S(1)}, f32[64]{0:T(128)}, u32[]{:S(2)}) copy-start(f32[64]{0:T(128)} %param.30) | copy-start | bytes 772
  0.7 15.6 %copy-start.11 = (bf16[4,8,320]{2,1,0:T(8,128)(2,1)S(1)}, bf16[4,8,320]{2,1,0:T(8,128)(2,1)}, u32[]{:S(2)}) copy-start(bf16[4,8,320]{2,1,0:T(8,128)(2,1)} %param.26) | copy-start | bytes 61444
  0.7 15.6 %copy-start.9 = (bf16[8,16,128]{2,1,0:T(8,128)(2,1)S(1)}, bf16[8,16,128]{2,1,0:T(8,128)(2,1)}, u32[]{:S(2)}) copy-start(bf16[8,16,128]{2,1,0:T(8,128)(2,1)} %param.25) | copy-start | bytes 98308
  2.7 9.5 %collective-permute-start = (bf16[4,32,512]{2,1,0:T(8,128)(2,1)}, bf16[4,32,512]{2,1,0:T(8,128)(2,1)S(1)}, u32[]{:S(2)}, u32[]{:S(2)}) collective-permute-start(bf16[4,32,512]{2,1,0:T(8,128)(2,1)} %get-tuple-element.39), channel_id=1, source_target_pairs={{32,64},{96,128},{160,192},{224,256},{288,320},{352,384},{416,448}... | collective-permute-start | bytes 393224 | tf_op jit(solution)/shard_map/ppermute | solution.py:683
  8.1 5.2 %collective-permute-start.1 = (bf16[4,32,512]{2,1,0:T(8,128)(2,1)}, bf16[4,32,512]{2,1,0:T(8,128)(2,1)S(1)}, u32[]{:S(2)}, u32[]{:S(2)}) collective-permute-start(bf16[4,32,512]{2,1,0:T(8,128)(2,1)} %get-tuple-element.40), channel_id=1, source_target_pairs={{0,32},{32,0},{64,96},{96,64},{128,160},{160,128},{192,224},{224,1... | collective-permute-start | bytes 393224 | tf_op jit(solution)/shard_map/ppermute | solution.py:684
  13.6 5.9 %collective-permute-start.2 = (bf16[24,4,512]{2,1,0:T(4,128)(2,1)S(1)}, bf16[24,4,512]{2,1,0:T(4,128)(2,1)S(1)}, u32[]{:S(2)}, u32[]{:S(2)}) collective-permute-start(bf16[24,4,512]{2,1,0:T(4,128)(2,1)S(1)} %get-tuple-element.51), channel_id=1, source_target_pairs={{0,1},{1,0},{2,3},{3,2},{4,5},{5,4},{6,7},{7,6},{8,9},{9,8},{10,11... | collective-permute-start | bytes 294920 | tf_op jit(solution)/shard_map/ppermute | solution.py:684
  15.5 4.0 %collective-permute-start.3 = (bf16[24,4,512]{2,1,0:T(4,128)(2,1)S(1)}, bf16[24,4,512]{2,1,0:T(4,128)(2,1)S(1)}, u32[]{:S(2)}, u32[]{:S(2)}) collective-permute-start(bf16[24,4,512]{2,1,0:T(4,128)(2,1)S(1)} %get-tuple-element.52), channel_id=1, source_target_pairs={{1,2},{3,4},{5,6},{7,8},{9,10},{11,12},{13,14},{15,16},{17,18},{19... | collective-permute-start | bytes 294920 | tf_op jit(solution)/shard_map/ppermute | solution.py:683
  16.3 3.4 %copy-start.4 = (bf16[512,384]{1,0:T(8,128)(2,1)S(1)}, bf16[512,384]{1,0:T(8,128)(2,1)}, u32[]{:S(2)}) copy-start(bf16[512,384]{1,0:T(8,128)(2,1)} %fourth_ref.1) | copy-start | bytes 1179652
  16.3 3.3 %copy-start.5 = (bf16[320,384]{1,0:T(8,128)(2,1)S(1)}, bf16[320,384]{1,0:T(8,128)(2,1)}, u32[]{:S(2)}) copy-start(bf16[320,384]{1,0:T(8,128)(2,1)} %third_ref.1) | copy-start | bytes 737284
  16.4 3.3 %copy-start.7 = (bf16[128,384]{1,0:T(8,128)(2,1)S(1)}, bf16[128,384]{1,0:T(8,128)(2,1)}, u32[]{:S(2)}) copy-start(bf16[128,384]{1,0:T(8,128)(2,1)} %second_ref.1) | copy-start | bytes 294916
  16.4 3.3 %copy-start.8 = (bf16[64,384]{1,0:T(8,128)(2,1)S(1)}, bf16[64,384]{1,0:T(8,128)(2,1)}, u32[]{:S(2)}) copy-start(bf16[64,384]{1,0:T(8,128)(2,1)} %first_ref.1) | copy-start | bytes 147460
  16.4 3.3 %copy-start.10 = (bf16[256,64]{0,1:T(8,128)(2,1)S(1)}, bf16[256,64]{0,1:T(8,128)(2,1)}, u32[]{:S(2)}) copy-start(bf16[256,64]{0,1:T(8,128)(2,1)} %param.36) | copy-start | bytes 98308
  16.4 3.3 %copy-start.12 = (f32[9,256]{1,0:T(8,128)S(1)}, f32[9,256]{1,0:T(8,128)}, u32[]{:S(2)}) copy-start(f32[9,256]{1,0:T(8,128)} %depth_ref.1) | copy-start | bytes 27652
  16.4 3.3 %copy-start.16 = (f32[256]{0:T(256)S(1)}, f32[256]{0:T(256)}, u32[]{:S(2)}) copy-start(f32[256]{0:T(256)} %param.35) | copy-start | bytes 3076
  25.8 4.5 %collective-permute-start.4 = (bf16[16,112,128]{2,1,0:T(8,128)(2,1)S(1)}, bf16[16,112,128]{2,1,0:T(8,128)(2,1)S(1)}, u32[]{:S(2)}, u32[]{:S(2)}) collective-permute-start(bf16[16,112,128]{2,1,0:T(8,128)(2,1)S(1)} %get-tuple-element.58), channel_id=1, source_target_pairs={{0,32},{32,0},{64,96},{96,64},{128,160},{160,128},{192,224},{224,1... | collective-permute-start | bytes 1376264 | tf_op jit(solution)/shard_map/ppermute | solution.py:651
  75.2 13.9 %all-to-all-start.2 = ((f32[32,5,2,128]{3,2,1,0:T(2,128)}), f32[32,5,2,128]{3,2,1,0:T(2,128)S(1)}, u32[]{:S(2)}, u32[]{:S(2)}) async-start(f32[32,5,2,128]{3,2,1,0:T(2,128)} %get-tuple-element.60), calls=%async_computation.2 | async-start | bytes 327680 | tf_op jit(solution)/shard_map/all_to_all | solution.py:649
  (1 other events, 3.3 us)

commit v6 on v5

--- a/solution.py
+++ b/solution.py
@@ -135,14 +135,22 @@
     return weight.astype(jnp.bfloat16)
 
 
+def add_later(projection, linear, later):
+    later = later.reshape(-1, D1).astype(jnp.float32)
+    return (nt(projection, linear) + later).astype(jnp.bfloat16)
+
+
 def own_kernel(
     height,
     width,
     joined_ref,
     block_ref,
+    later_ref,
     top_ref,
     bottom_ref,
     join_ref,
+    first_ref,
+    reduce_ref,
     gain_ref,
     shift_ref,
     expand_ref,
@@ -153,6 +161,8 @@
     pooled_ref,
     side_matrix_ref,
     projection_ref,
+    grad_ref,
+    act_grad_ref,
     hidden_ref,
     normed_ref,
     standard_ref,
@@ -175,11 +185,15 @@
 
     pooled_ref[...] = nn(matrix(TW), wide_ref[...].reshape(ROWS * TW, DEC))
     side_matrix_ref[...] = matrix(PITCH - TW)
-    projection_ref[...] = (
-        nt(wide_ref[3:21].reshape(18 * TW, DEC), join_ref[0:DEC, :])
-        .astype(jnp.bfloat16)
-        .reshape(18, TW, DEC)
-    )
+    projection = nt(wide_ref[3:21].reshape(18 * TW, DEC), join_ref[0:DEC, :]).astype(jnp.bfloat16)
+    projection_ref[...] = projection[TW : 17 * TW]
+    lanes = slice(DEC + D1, DEC + 2 * D1)
+    later = jnp.concatenate(
+        [top_ref[3:4, :, lanes], later_ref[...], bottom_ref[0:1, :, lanes]], axis=0
+    )
+    feature_grad = add_later(projection, first_ref[...], later)
+    grad_ref[...] = feature_grad[TW : 17 * TW]
+    act_grad_ref[...] = nn(feature_grad, reduce_ref[...]).reshape(18, TW, HID)
 
     values = jnp.concatenate(
         [top_ref[2:4, :, DEC : DEC + D1], block_ref[...], bottom_ref[0:2, :, DEC : DEC + D1]], axis=0
@@ -208,7 +222,9 @@
         (
             sds((sum(COARSE), DEC), f32),
             sds((sum(COARSE), ROWS * (PITCH - TW)), bf16),
-            sds((18, TW, DEC), bf16),
+            sds((pixels, DEC), bf16),
+            sds((pixels, D1), bf16),
+            sds((18, TW, HID), f32),
             sds((20, TW, HID), f32),
             sds((pixels, D1), bf16),
             sds((pixels, D1), f32),
@@ -228,6 +244,8 @@
     pooled_ref,
     side_matrix_ref,
     own_projection_ref,
+    own_grad_ref,
+    own_act_grad_ref,
     own_hidden_ref,
     normed_ref,
     standard_ref,
@@ -236,9 +254,6 @@
     feature3_ref,
     feature4_ref,
     block_ref,
-    later_ref,
-    top_ref,
-    bottom_ref,
     side_ref,
     join_ref,
     first_ref,
@@ -259,8 +274,6 @@
     grad4_ref,
     mine_ref,
     other_ref,
-    projection_ref,
-    wide_later_ref,
     hid_ref,
     slope_ref,
     act_ref,
@@ -272,11 +285,6 @@
     row_index = lax.axis_index("row")
     scale_base = 1.0 / math.sqrt(height * width)
 
-    later_lanes = slice(DEC + D1, DEC + 2 * D1)
-    wide_later_ref[1 : 1 + TH, 0:TW] = later_ref[...]
-    wide_later_ref[0:1, 0:TW] = top_ref[EDGE - 1 :, :, later_lanes]
-    wide_later_ref[1 + TH :, 0:TW] = bottom_ref[0:1, :, later_lanes]
-    wide_later_ref[:, TW:] = side_ref[3:21, :, later_lanes]
     rest_ref[...] = jnp.zeros_like(rest_ref)
 
     def keep_row(row, value):
@@ -331,29 +339,22 @@
 
     lax.fori_loop(0, 18, conv_row, 0)
 
-    def own(value, rows, pitch):
-        first = (rows - TH) // 2
-        channels = value.shape[-1]
-        return value.reshape(rows, pitch, channels)[first : first + TH, 0:TW].reshape(
-            TH * TW, channels
-        )
-
-    side_projection = nt(
+    beside = slice(0, 2 * EDGE)
+    projection = nt(
         side_ref[3:21, :, 0:DEC].reshape(18 * (PITCH - TW), DEC), join_ref[0:DEC, :]
     ).astype(jnp.bfloat16)
-    projection_ref[:, 0:TW] = own_projection_ref[...]
-    projection_ref[:, TW:] = side_projection.reshape(18, PITCH - TW, DEC)
-    projection = projection_ref[...].reshape(18 * PITCH, DEC)
-    later = wide_later_ref[...].reshape(18 * PITCH, D1).astype(jnp.float32)
-    feature_grad = (nt(projection, first_ref[...]) + later).astype(jnp.bfloat16)
-    act_grad = nn(feature_grad, reduce_ref[...])
-    act_grad = act_grad.reshape(18, PITCH, HID)[:, 0:USED]
-    pre_grad = (act_grad * slope_ref[...]).astype(jnp.bfloat16).astype(jnp.float32)
-    pre_ref[...] = pre_grad * inside(3, 18, USED, height, width).reshape(18, USED, 1)
+    feature_grad = add_later(
+        projection, first_ref[...], side_ref[3:21, :, DEC + D1 : DEC + 2 * D1]
+    )
+    act_grad = nn(feature_grad, reduce_ref[...]).reshape(18, PITCH - TW, HID)[:, beside]
+    grid = inside(3, 18, USED, height, width).reshape(18, USED, 1)
+    for cols, part in ((slice(0, TW), own_act_grad_ref[...]), (slice(TW, USED), act_grad)):
+        pre_grad = (part * slope_ref[:, cols, :]).astype(jnp.bfloat16).astype(jnp.float32)
+        pre_ref[:, cols, :] = pre_grad * grid[:, cols]
 
     activated = act_ref[1:17].reshape(TH * TW, HID)
-    own_projection = own_projection_ref[1 : 1 + TH].reshape(TH * TW, DEC)
-    own_grad = own(feature_grad, 18, PITCH)
+    own_projection = own_projection_ref[...]
+    own_grad = own_grad_ref[...]
     own_block = block_ref[...].reshape(TH * TW, D1).astype(jnp.float32)
     features = (own_block + (nt(activated, reduce_ref[...]) + reduce_bias_ref[...])).astype(
         jnp.bfloat16
@@ -520,8 +521,6 @@
         in_specs=[pl.BlockSpec(memory_space=vmem)] * len(operands),
         out_specs=(pl.BlockSpec(memory_space=vmem),) * 6,
         scratch_shapes=[
-            vmem((18, PITCH, DEC), bf16),
-            vmem((18, PITCH, D1), bf16),
             vmem((20, USED, HID), f32),
             vmem((18, USED, HID), f32),
             vmem((18, TW, HID), bf16),
@@ -553,18 +552,44 @@
             out_ref[4 * zh + yh, 8:16, :] = share
 
 
-def final_kernel(received_ref, linear_ref, out_ref):
+def final_kernel(received_ref, out_ref):
     total = jnp.sum(received_ref[...], 0)
-    for p in range(2):
-        for j in range(3):
-            linear_ref[3 * p + j : 3 * p + j + 1, :] = total[2 * j + p : 2 * j + p + 1, :]
     for n in range(out_ref.shape[0]):
         for i in range(4):
             out_ref[n, i] = total[8 + 2 * i : 10 + 2 * i]
         out_ref[n, 4] = total[6:8]
 
 
-def small_kernel(all_ref, biases_ref, expand_ref, reduce_ref, depth_ref, hidden_ref, channel_ref):
+def result_kernel(
+    all_ref,
+    received_ref,
+    input_grad,
+    grad2,
+    grad3,
+    grad4,
+    input_out,
+    out2,
+    out3,
+    out4,
+    linear_ref,
+    biases_ref,
+    expand_ref,
+    reduce_ref,
+    depth_ref,
+    hidden_ref,
+    channel_ref,
+):
+    input_out[...] = input_grad[...]
+    out2[...] = grad2[...]
+    out3[...] = grad3[...]
+    last = grad4[...].astype(jnp.float32)
+    for i in range(out4.shape[0]):
+        out4[i] = last[4 * i : 4 * i + 4].astype(jnp.bfloat16)
+    total = jnp.sum(received_ref[:, 0:8, :], 0)
+    for p in range(2):
+        for j in range(3):
+            linear_ref[3 * p + j : 3 * p + j + 1, :] = total[2 * j + p : 2 * j + p + 1, :]
+
     for share in range(2 * NEAR):
         lanes = slice(0, 128) if share < NEAR else slice(128, 256)
         first = 4 * (share % NEAR)
@@ -638,7 +663,7 @@
     return near, far, both
 
 
-def sum_over_mesh(mine, other):
+def sum_over_mesh(mine, other, grads):
     rows = lax.axis_size("row")
     cols = lax.axis_size("col")
     sds = jax.ShapeDtypeStruct
@@ -651,17 +676,16 @@
     received = lax.ppermute(other, "row", [(i, i ^ 1) for i in range(rows)])
     chip = in_vmem(chip_kernel, "chip_sums", sds(other.shape, other.dtype), mine, received)
     parts = in_vmem(near_kernel, "near_sums", sds((16, 16, 128), f32), exchange(chip, near))
-    linear, share = in_vmem(
-        final_kernel,
-        "final_sums",
-        (sds((6, 128), f32), sds((2 * NEAR, 5, 2, 128), f32)),
-        exchange(parts, far),
-    )
+    received = exchange(parts, far)
+    share = in_vmem(final_kernel, "final_sums", sds((2 * NEAR, 5, 2, 128), f32), received)
     everything = exchange(share, both)
-    biases, expand, reduce, depth, hidden, channel = in_vmem(
-        small_kernel,
-        "small_sums",
+    *tiles, linear, biases, expand, reduce, depth, hidden, channel = in_vmem(
+        result_kernel,
+        "results",
         (
+            *(sds(grad.shape, grad.dtype) for grad in grads[:3]),
+            sds((TH // 8, TW // 8, D4), jnp.bfloat16),
+            sds((6, 128), f32),
             sds((4, DEC), f32),
             sds((D1, HID), f32),
             sds((D1, HID), f32),
@@ -670,8 +694,10 @@
             sds((3, D1), f32),
         ),
         everything,
-    )
-    return linear.reshape(-1), (biases, expand, reduce.T, depth, hidden, channel)
+        received,
+        *grads,
+    )
+    return tiles, (linear.reshape(-1), biases, expand, reduce.T, depth, hidden, channel)
 
 
 def swap_edges(to_far, to_near, axis):
@@ -728,9 +754,12 @@
         width,
         joined_grad,
         block_input,
+        later_grad,
         top,
         bottom,
         join_weight,
+        linear_first,
+        reduce_weight.T,
         norm_gain.reshape(1, -1),
         norm_shift.reshape(1, -1),
         expand_weight,
@@ -747,9 +776,6 @@
         width,
         *early,
         block_input,
-        later_grad,
-        top,
-        bottom,
         side,
         join_weight,
         linear_first,
@@ -765,14 +791,14 @@
         reduce_weight.T,
         reduce_bias.reshape(1, -1),
     )
-    linear_grads, small = sum_over_mesh(mine, other)
+    tiles, sums = sum_over_mesh(mine, other, (input_grad, grad2, grad3, grad4))
+    input_grad, grad2, grad3, grad4 = tiles
     return (
         input_grad,
         grad2.reshape(TH // 2, TW // 2, D2),
         grad3.reshape(TH // 4, TW // 4, D3),
-        grad4.reshape(TH // 8, TW // 8, D4),
-        linear_grads,
-        *small,
+        grad4,
+        *sums,
     )
 
 

time: 90.1 us -> 88 us (0.977)
  blocking collectives: 44 us -> 56.9 us
  waiting for transfers between devices: 11.5 us -> 3.98 us
  starting transfers between devices: 21.5 us -> 15.2 us
    all_to_all x2 -> x3, blocking collectives: 44 us -> 56.9 us  [exchange(): lax.all_to_all(parts, ('row', 'col'), 0, 0, tiled=True, axis_index_groups...]
    all_to_all x1 -> x0, waiting for transfers between devices: 6.9 us -> none  [exchange(): lax.all_to_all(parts, ('row', 'col'), 0, 0, tiled=True, axis_index_groups...]
    all_to_all x1 -> x0, starting transfers between devices: 6.34 us -> none  [exchange(): lax.all_to_all(parts, ('row', 'col'), 0, 0, tiled=True, axis_index_groups...]
  transfers between devices with their start and end apart: 6 -> 5, of which waited for: 4 -> 3; matrix products, arithmetic and copies ran while one was open for 1% -> 0% of each run, Pallas kernels for 1% -> 2%
where the time goes in v6:
time: 88 us; the launch traced here: 87.7 us
  blocking collectives  56.9 us (65%)
  starting transfers between devices  15.2 us (17%)
  Pallas kernels  10.2 us (12%)
  waiting for transfers between devices  3.98 us (5%)
  between operations  1.06 us (1%)
    all_to_all x3, blocking collectives, exchange(): lax.all_to_all(parts, ('row', 'col'), 0, 0, tiled=True, axis_index_groups...  56.9 us
    ppermute x2, starting transfers between devices, swap_edges(): from_far = lax.ppermute(to_far, axis, far)  6.06 us
    ppermute x2, starting transfers between devices, swap_edges(): from_near = lax.ppermute(to_near, axis, near)  5.99 us
    pallas_call x1, Pallas kernels, tile_pass(): pl.pallas_call(functools.partial(tile_kernel, height, width), out_shape=(...  5.38 us
    ppermute x1, starting transfers between devices, sum_over_mesh(): received = lax.ppermute(other, 'row', [(i, i ^ 1) for i in range(rows)])  3.11 us
    pallas_call x6, Pallas kernels, in_vmem(): pl.pallas_call(kernel, out_shape=out_shape, in_specs=[vmem] * len(operand...  2.86 us
    ppermute x2, waiting for transfers between devices, swap_edges(): from_near = lax.ppermute(to_near, axis, near)  2.56 us
    pallas_call x1, Pallas kernels, row_borders(): pl.pallas_call(row_kernel, out_shape=(out, out), in_specs=[pl.BlockSpec(m...  1.91 us
  transfers between devices with their start and end apart: 5, of which 3 were waited for; matrix products, arithmetic and copies ran while one was open for 0% of the time, Pallas kernels for 2%

profile of v6, /device:TPU:1, one launch (start us, length us, event | category | flops | bytes accessed | tf_op | source)
XLA Modules:
  0.0 87.7 jit_solution(15915139479148379495)
XLA Ops:
  0.8 1.9 %row_borders.1 = (bf16[4,32,512]{2,1,0:T(8,128)(2,1)}, bf16[4,32,512]{2,1,0:T(8,128)(2,1)}) custom-call(bf16[16,32,384]{2,1,0:T(8,128)(2,1)} %joined_ref.5, bf16[16,32,64]{2,1,0:T(8,128)(2,1)} %block_ref.7, bf16[16,32,64]{2,1,0:T(8,128)(2,1)} %later_ref.5), custom_call_target="tpu_custom_call" | custom-call | tf_op jit(solution)/shard_map/row_borders/pallas_call | solution.py:479
  2.7 5.4 %collective-permute-start = (bf16[4,32,512]{2,1,0:T(8,128)(2,1)}, bf16[4,32,512]{2,1,0:T(8,128)(2,1)S(1)}, u32[]{:S(2)}, u32[]{:S(2)}) collective-permute-start(bf16[4,32,512]{2,1,0:T(8,128)(2,1)} %get-tuple-element.44), channel_id=1, source_target_pairs={{32,64},{96,128},{160,192},{224,256},{288,320},{352,384},{416,448}... | collective-permute-start | bytes 393224 | tf_op jit(solution)/shard_map/ppermute | solution.py:709
  8.1 4.1 %collective-permute-start.1 = (bf16[4,32,512]{2,1,0:T(8,128)(2,1)}, bf16[4,32,512]{2,1,0:T(8,128)(2,1)S(1)}, u32[]{:S(2)}, u32[]{:S(2)}) collective-permute-start(bf16[4,32,512]{2,1,0:T(8,128)(2,1)} %get-tuple-element.45), channel_id=1, source_target_pairs={{0,32},{32,0},{64,96},{96,64},{128,160},{160,128},{192,224},{224,1... | collective-permute-start | bytes 393224 | tf_op jit(solution)/shard_map/ppermute | solution.py:710
  12.2 1.2 %collective-permute-done.1 = bf16[4,32,512]{2,1,0:T(8,128)(2,1)S(1)} collective-permute-done((bf16[4,32,512]{2,1,0:T(8,128)(2,1)}, bf16[4,32,512]{2,1,0:T(8,128)(2,1)S(1)}, u32[]{:S(2)}, u32[]{:S(2)}) %collective-permute-start.1) | collective-permute-done | bytes 131104 | tf_op jit(solution)/shard_map/ppermute | solution.py:710
  13.4 0.2 column_borders.1
  13.6 1.9 %collective-permute-start.2 = (bf16[24,4,512]{2,1,0:T(4,128)(2,1)S(1)}, bf16[24,4,512]{2,1,0:T(4,128)(2,1)S(1)}, u32[]{:S(2)}, u32[]{:S(2)}) collective-permute-start(bf16[24,4,512]{2,1,0:T(4,128)(2,1)S(1)} %get-tuple-element.58), channel_id=1, source_target_pairs={{0,1},{1,0},{2,3},{3,2},{4,5},{5,4},{6,7},{7,6},{8,9},{9,8},{10,11... | collective-permute-start | bytes 294920 | tf_op jit(solution)/shard_map/ppermute | solution.py:710
  15.5 0.7 collective-permute-start.3
  16.2 0.1 pad.2.clone
  16.4 0.0 copy-start.4
  16.4 0.0 copy-start.5
  16.4 0.0 copy-start.16
  16.4 0.0 copy-start.17
  16.4 1.6 %own_pass.1 = (f32[168,384]{1,0:T(8,128)S(1)}, bf16[168,384]{1,0:T(8,128)(2,1)S(1)}, bf16[512,384]{1,0:T(8,128)(2,1)S(1)}, bf16[512,64]{1,0:T(8,128)(2,1)S(1)}, ...) custom-call(bf16[16,32,384]{2,1,0:T(8,128)(2,1)S(1)} %copy-done.1, ...), custom_call_target="tpu_custom_call" | custom-call | tf_op jit(solution)/shard_map/own_pass/pallas_call | solution.py:619
  18.1 1.4 %collective-permute-done.2 = bf16[24,4,512]{2,1,0:T(4,128)(2,1)S(1)} collective-permute-done((bf16[24,4,512]{2,1,0:T(4,128)(2,1)S(1)}, bf16[24,4,512]{2,1,0:T(4,128)(2,1)S(1)}, u32[]{:S(2)}, u32[]{:S(2)}) %collective-permute-start.2) | collective-permute-done | bytes 98336 | tf_op jit(solution)/shard_map/ppermute | solution.py:710
  19.5 0.2 maximum_maximum_fusion.side_ref
  19.8 5.4 %tile_pass.1 = (bf16[16,32,64]{2,1,0:T(8,128)(2,1)S(1)}, bf16[128,128]{1,0:T(8,128)(2,1)S(1)}, bf16[32,320]{1,0:T(8,128)(2,1)S(1)}, bf16[8,512]{1,0:T(8,128)(2,1...) custom-call(f32[168,384]{1,0:T(8,128)S(1)} %get-tuple-element.46.pooled_ref, ...), custom_call_target="tpu_custom_call" | custom-call | tf_op jit(solution)/shard_map/tile_pass/pallas_call | solution.py:511
  25.2 3.1 %collective-permute-start.4 = (bf16[16,112,128]{2,1,0:T(8,128)(2,1)S(1)}, bf16[16,112,128]{2,1,0:T(8,128)(2,1)S(1)}, u32[]{:S(2)}, u32[]{:S(2)}) collective-permute-start(bf16[16,112,128]{2,1,0:T(8,128)(2,1)S(1)} %get-tuple-element.61), channel_id=1, source_target_pairs={{0,32},{32,0},{64,96},{96,64},{128,160},{160,128},{192,224},{224,1... | collective-permute-start | bytes 1376264 | tf_op jit(solution)/shard_map/ppermute | solution.py:676
  28.3 1.4 %collective-permute-done.4.received_ref = bf16[16,112,128]{2,1,0:T(8,128)(2,1)S(1)} collective-permute-done((bf16[16,112,128]{2,1,0:T(8,128)(2,1)S(1)}, bf16[16,112,128]{2,1,0:T(8,128)(2,1)S(1)}, u32[]{:S(2)}, u32[]{:S(2)}) %collective-permute-start.4) | collective-permute-done | bytes 458784 | tf_op jit(solution)/shard_map/ppermute | solution.py:676
  29.7 0.1 chip_sums.1
  29.8 19.1 %all_to_all.15.received_ref = bf16[16,112,128]{2,1,0:T(8,128)(2,1)S(1)} all-to-all(bf16[16,112,128]{2,1,0:T(8,128)(2,1)S(1)} %chip_sums.1), channel_id=1, replica_groups={{0,1,2,3,4,5,6,7,64,65,66,67,68,69,70,71},{8,9,10,11,12,13,14,15,72,73,..., dimensions={0} | all-to-all | bytes 917504 | tf_op jit(solution)/shard_map/all_to_all | solution.py:674
  48.9 0.1 near_sums.1
  48.9 24.9 %all_to_all.16.received_ref = f32[16,16,128]{2,1,0:T(8,128)S(1)} all-to-all(f32[16,16,128]{2,1,0:T(8,128)S(1)} %near_sums.1), channel_id=1, replica_groups={{0,8,16,24,128,136,144,152,256,264,272,280,384,392,400,408},{1,9,17,25,..., dimensions={0} | all-to-all | bytes 262144 | tf_op jit(solution)/shard_map/all_to_all | solution.py:674
  73.9 13.0 %all_to_all.17.all_ref = f32[32,5,2,128]{3,2,1,0:T(2,128)S(1)} all-to-all(f32[32,5,2,128]{3,2,1,0:T(2,128)S(1)} %final_sums.1), channel_id=1, replica_groups={{0,32,1,33,2,34,3,35,4,36,5,37,6,38,7,39,64,96,65,97,66,98,67,99,68,100..., dimensions={0} | all-to-all | bytes 327680 | tf_op jit(solution)/shard_map/all_to_all | solution.py:674
  86.9 0.8 results.1
  (41 shorter events, 0.2 us)
Async XLA Ops:
  0.6 12.7 %copy-start.2 = (bf16[16,32,64]{2,1,0:T(8,128)(2,1)S(1)}, bf16[16,32,64]{2,1,0:T(8,128)(2,1)}, u32[]{:S(2)}) copy-start(bf16[16,32,64]{2,1,0:T(8,128)(2,1)} %block_ref.7) | copy-start | bytes 196612
  0.7 12.7 %copy-start.3 = (bf16[16,32,64]{2,1,0:T(8,128)(2,1)S(1)}, bf16[16,32,64]{2,1,0:T(8,128)(2,1)}, u32[]{:S(2)}) copy-start(bf16[16,32,64]{2,1,0:T(8,128)(2,1)} %later_ref.5) | copy-start | bytes 196612
  0.7 12.7 %copy-start.1 = (bf16[16,32,384]{2,1,0:T(8,128)(2,1)S(1)}, bf16[16,32,384]{2,1,0:T(8,128)(2,1)}, u32[]{:S(2)}) copy-start(bf16[16,32,384]{2,1,0:T(8,128)(2,1)} %joined_ref.5) | copy-start | bytes 1179652
  0.7 15.5 %copy-start.18 = (bf16[2,4,512]{2,1,0:T(4,128)(2,1)S(1)}, bf16[2,4,512]{2,1,0:T(4,128)(2,1)}, u32[]{:S(2)}) copy-start(bf16[2,4,512]{2,1,0:T(4,128)(2,1)} %param.27) | copy-start | bytes 24580
  0.7 15.6 %copy-start.8 = (bf16[64,256]{1,0:T(8,128)(2,1)S(1)}, bf16[64,256]{1,0:T(8,128)(2,1)}, u32[]{:S(2)}) copy-start(bf16[64,256]{1,0:T(8,128)(2,1)} %expand_ref.3) | copy-start | bytes 98308
  0.7 15.6 %copy-start.6 = (bf16[64,384]{1,0:T(8,128)(2,1)S(1)}, bf16[64,384]{1,0:T(8,128)(2,1)}, u32[]{:S(2)}) copy-start(bf16[64,384]{1,0:T(8,128)(2,1)} %first_ref.3) | copy-start | bytes 147460
  0.7 15.6 %copy-start = (bf16[1536,384]{1,0:T(8,128)(2,1)S(1)}, bf16[1536,384]{1,0:T(8,128)(2,1)}, u32[]{:S(2)}) copy-start(bf16[1536,384]{1,0:T(8,128)(2,1)} %join_ref.3) | copy-start | bytes 3538948
  0.7 15.6 %copy-start.7 = (bf16[256,64]{0,1:T(8,128)(2,1)S(1)}, bf16[256,64]{0,1:T(8,128)(2,1)}, u32[]{:S(2)}) copy-start(bf16[256,64]{0,1:T(8,128)(2,1)} %param.36) | copy-start | bytes 98308
  0.7 15.6 %copy-start.13 = (f32[256]{0:T(256)S(1)}, f32[256]{0:T(256)}, u32[]{:S(2)}) copy-start(f32[256]{0:T(256)} %param.33) | copy-start | bytes 3076
  0.7 15.6 %copy-start.15 = (f32[64]{0:T(128)S(1)}, f32[64]{0:T(128)}, u32[]{:S(2)}) copy-start(f32[64]{0:T(128)} %param.31) | copy-start | bytes 772
  0.7 15.6 %copy-start.14 = (f32[64]{0:T(128)S(1)}, f32[64]{0:T(128)}, u32[]{:S(2)}) copy-start(f32[64]{0:T(128)} %param.30) | copy-start | bytes 772
  0.8 15.6 %copy-start.11 = (bf16[4,8,320]{2,1,0:T(8,128)(2,1)S(1)}, bf16[4,8,320]{2,1,0:T(8,128)(2,1)}, u32[]{:S(2)}) copy-start(bf16[4,8,320]{2,1,0:T(8,128)(2,1)} %param.26) | copy-start | bytes 61444
  0.8 15.6 %copy-start.10 = (bf16[8,16,128]{2,1,0:T(8,128)(2,1)S(1)}, bf16[8,16,128]{2,1,0:T(8,128)(2,1)}, u32[]{:S(2)}) copy-start(bf16[8,16,128]{2,1,0:T(8,128)(2,1)} %param.25) | copy-start | bytes 98308
  2.7 9.5 %collective-permute-start = (bf16[4,32,512]{2,1,0:T(8,128)(2,1)}, bf16[4,32,512]{2,1,0:T(8,128)(2,1)S(1)}, u32[]{:S(2)}, u32[]{:S(2)}) collective-permute-start(bf16[4,32,512]{2,1,0:T(8,128)(2,1)} %get-tuple-element.44), channel_id=1, source_target_pairs={{32,64},{96,128},{160,192},{224,256},{288,320},{352,384},{416,448}... | collective-permute-start | bytes 393224 | tf_op jit(solution)/shard_map/ppermute | solution.py:709
  8.1 5.2 %collective-permute-start.1 = (bf16[4,32,512]{2,1,0:T(8,128)(2,1)}, bf16[4,32,512]{2,1,0:T(8,128)(2,1)S(1)}, u32[]{:S(2)}, u32[]{:S(2)}) collective-permute-start(bf16[4,32,512]{2,1,0:T(8,128)(2,1)} %get-tuple-element.45), channel_id=1, source_target_pairs={{0,32},{32,0},{64,96},{96,64},{128,160},{160,128},{192,224},{224,1... | collective-permute-start | bytes 393224 | tf_op jit(solution)/shard_map/ppermute | solution.py:710
  13.6 5.9 %collective-permute-start.2 = (bf16[24,4,512]{2,1,0:T(4,128)(2,1)S(1)}, bf16[24,4,512]{2,1,0:T(4,128)(2,1)S(1)}, u32[]{:S(2)}, u32[]{:S(2)}) collective-permute-start(bf16[24,4,512]{2,1,0:T(4,128)(2,1)S(1)} %get-tuple-element.58), channel_id=1, source_target_pairs={{0,1},{1,0},{2,3},{3,2},{4,5},{5,4},{6,7},{7,6},{8,9},{9,8},{10,11... | collective-permute-start | bytes 294920 | tf_op jit(solution)/shard_map/ppermute | solution.py:710
  15.5 4.0 %collective-permute-start.3 = (bf16[24,4,512]{2,1,0:T(4,128)(2,1)S(1)}, bf16[24,4,512]{2,1,0:T(4,128)(2,1)S(1)}, u32[]{:S(2)}, u32[]{:S(2)}) collective-permute-start(bf16[24,4,512]{2,1,0:T(4,128)(2,1)S(1)} %get-tuple-element.59), channel_id=1, source_target_pairs={{1,2},{3,4},{5,6},{7,8},{9,10},{11,12},{13,14},{15,16},{17,18},{19... | collective-permute-start | bytes 294920 | tf_op jit(solution)/shard_map/ppermute | solution.py:709
  16.4 3.3 %copy-start.4 = (bf16[512,384]{1,0:T(8,128)(2,1)S(1)}, bf16[512,384]{1,0:T(8,128)(2,1)}, u32[]{:S(2)}) copy-start(bf16[512,384]{1,0:T(8,128)(2,1)} %fourth_ref.1) | copy-start | bytes 1179652
  16.4 3.3 %copy-start.5 = (bf16[320,384]{1,0:T(8,128)(2,1)S(1)}, bf16[320,384]{1,0:T(8,128)(2,1)}, u32[]{:S(2)}) copy-start(bf16[320,384]{1,0:T(8,128)(2,1)} %third_ref.1) | copy-start | bytes 737284
  16.4 3.3 %copy-start.9 = (bf16[128,384]{1,0:T(8,128)(2,1)S(1)}, bf16[128,384]{1,0:T(8,128)(2,1)}, u32[]{:S(2)}) copy-start(bf16[128,384]{1,0:T(8,128)(2,1)} %second_ref.1) | copy-start | bytes 294916
  16.4 3.3 %copy-start.12 = (f32[9,256]{1,0:T(8,128)S(1)}, f32[9,256]{1,0:T(8,128)}, u32[]{:S(2)}) copy-start(f32[9,256]{1,0:T(8,128)} %depth_ref.1) | copy-start | bytes 27652
  16.4 3.3 %copy-start.16 = (f32[256]{0:T(256)S(1)}, f32[256]{0:T(256)}, u32[]{:S(2)}) copy-start(f32[256]{0:T(256)} %param.35) | copy-start | bytes 3076
  16.4 3.3 %copy-start.17 = (f32[64]{0:T(128)S(1)}, f32[64]{0:T(128)}, u32[]{:S(2)}) copy-start(f32[64]{0:T(128)} %param.37) | copy-start | bytes 772
  25.2 4.5 %collective-permute-start.4 = (bf16[16,112,128]{2,1,0:T(8,128)(2,1)S(1)}, bf16[16,112,128]{2,1,0:T(8,128)(2,1)S(1)}, u32[]{:S(2)}, u32[]{:S(2)}) collective-permute-start(bf16[16,112,128]{2,1,0:T(8,128)(2,1)S(1)} %get-tuple-element.61), channel_id=1, source_target_pairs={{0,32},{32,0},{64,96},{96,64},{128,160},{160,128},{192,224},{224,1... | collective-permute-start | bytes 1376264 | tf_op jit(solution)/shard_map/ppermute | solution.py:676

commit v7 on v6

--- a/solution.py
+++ b/solution.py
@@ -41,6 +41,10 @@
     return lax.dot_general(left, right, (((0,), (0,)), ((), ())), preferred_element_type=jnp.float32)
 
 
+def add3(terms):
+    return terms[0] + terms[1] + terms[2]
+
+
 def nn(left, right):
     return jnp.dot(left, right, preferred_element_type=jnp.float32)
 
@@ -63,12 +67,19 @@
     return lax.broadcasted_iota(jnp.int32, shape, axis).astype(jnp.float32)
 
 
-def inside(first, rows, pitch, height, width):
-    row, col = place(count_up((rows * pitch, 1), 0) + first * pitch, pitch)
-    row = row + (lax.axis_index("row") * TH).astype(jnp.float32)
-    col = col + (lax.axis_index("col") * TW).astype(jnp.float32)
-    good = (row >= 0.0) & (row < height) & (col >= 0.0) & (col < width)
-    return jnp.where(good, 1.0, 0.0)
+def rows_inside(halo, height):
+    row_index = lax.axis_index("row")
+    above = jnp.where(row_index > 0, 1.0, 0.0)
+    below = jnp.where(row_index < height // TH - 1, 1.0, 0.0)
+    return [above] * halo + [None] * TH + [below] * halo
+
+
+def sides_inside(width):
+    col_index = lax.axis_index("col")
+    before = jnp.where(col_index > 0, 1.0, 0.0)
+    after = jnp.where(col_index < width // TW - 1, 1.0, 0.0)
+    right = lax.broadcasted_iota(jnp.int32, (2 * EDGE, HID), 0) < EDGE
+    return jnp.where(right, after, before)
 
 
 def normalize(values, gain, shift):
@@ -202,7 +213,9 @@
         values.reshape(20 * TW, D1).astype(jnp.float32), gain_ref[...], shift_ref[...]
     )
     hidden = expand(normed, expand_ref[...], expand_bias_ref[...])
-    hidden_ref[...] = (hidden * inside(2, 20, TW, height, width)).reshape(20, TW, HID)
+    hidden = hidden.reshape(20, TW, HID)
+    for i, good in enumerate(rows_inside(2, height)):
+        hidden_ref[i] = hidden[i] if good is None else hidden[i] * good
     own = slice(2 * TW, 18 * TW)
     normed_ref[...] = normed[own]
     standard_ref[...] = standard[own]
@@ -319,7 +332,10 @@
     normed, _, _ = normalize(values.reshape(20 * 2 * EDGE, D1), gain_ref[...], shift_ref[...])
     hidden = expand(normed, expand_ref[...], expand_bias_ref[...])
     hid_ref[:, 0:TW] = own_hidden_ref[...]
-    hid_ref[:, TW:] = (hidden * inside(2, 20, 2 * EDGE, height, width)).reshape(20, 2 * EDGE, HID)
+    hidden = hidden.reshape(20, 2 * EDGE, HID)
+    sides = sides_inside(width)
+    for i, good in enumerate(rows_inside(2, height)):
+        hid_ref[i, TW:] = hidden[i] * (sides if good is None else sides * good)
 
     def across(before, same, after):
         return pltpu.roll(before, 1, 0) + same + pltpu.roll(after, USED - 1, 0)
@@ -327,7 +343,7 @@
     def conv_row(i, carry):
         rows = [hid_ref[i + a] for a in range(3)]
         sums = [
-            sum(depth_ref[3 * a + b : 3 * a + b + 1, :] * rows[a] for a in range(3))
+            add3([depth_ref[3 * a + b : 3 * a + b + 1, :] * rows[a] for a in range(3)])
             for b in range(3)
         ]
         conv = across(*sums) + depth_bias_ref[...]
@@ -347,10 +363,12 @@
         projection, first_ref[...], side_ref[3:21, :, DEC + D1 : DEC + 2 * D1]
     )
     act_grad = nn(feature_grad, reduce_ref[...]).reshape(18, PITCH - TW, HID)[:, beside]
-    grid = inside(3, 18, USED, height, width).reshape(18, USED, 1)
-    for cols, part in ((slice(0, TW), own_act_grad_ref[...]), (slice(TW, USED), act_grad)):
-        pre_grad = (part * slope_ref[:, cols, :]).astype(jnp.bfloat16).astype(jnp.float32)
-        pre_ref[:, cols, :] = pre_grad * grid[:, cols]
+    for i, good in enumerate(rows_inside(1, height)):
+        for cols, part in ((slice(0, TW), own_act_grad_ref[i]), (slice(TW, USED), act_grad[i])):
+            pre_grad = (part * slope_ref[i, cols, :]).astype(jnp.bfloat16).astype(jnp.float32)
+            if cols.start:
+                pre_grad = pre_grad * sides
+            pre_ref[i, cols, :] = pre_grad if good is None else pre_grad * good
 
     activated = act_ref[1:17].reshape(TH * TW, HID)
     own_projection = own_projection_ref[...]
@@ -371,7 +389,7 @@
         own_row = jnp.concatenate([center_row, jnp.zeros((USED - TW, HID), jnp.float32)], axis=0)
         rows = [pre_ref[i + 2 - a] for a in range(3)]
         sums_b = [
-            sum(depth_ref[3 * a + b : 3 * a + b + 1, :] * rows[a] for a in range(3))
+            add3([depth_ref[3 * a + b : 3 * a + b + 1, :] * rows[a] for a in range(3)])
             for b in range(3)
         ]
         total = across(sums_b[2], sums_b[1], sums_b[0])[0:TW]

time: 88 us -> 87.6 us (level)
  no operation moved by 1% of the time
where the time goes in v7:
time: 87.6 us; the launch traced here: 87.3 us
  blocking collectives  56.9 us (65%)
  starting transfers between devices  15.1 us (17%)
  Pallas kernels  9.76 us (11%)
  waiting for transfers between devices  3.99 us (5%)
  between operations  1.06 us (1%)
    all_to_all x3, blocking collectives, exchange(): lax.all_to_all(parts, ('row', 'col'), 0, 0, tiled=True, axis_index_groups...  56.9 us
    ppermute x2, starting transfers between devices, swap_edges(): from_far = lax.ppermute(to_far, axis, far)  6.06 us
    ppermute x2, starting transfers between devices, swap_edges(): from_near = lax.ppermute(to_near, axis, near)  5.99 us
    pallas_call x1, Pallas kernels, tile_pass(): pl.pallas_call(functools.partial(tile_kernel, height, width), out_shape=(...  4.99 us
    ppermute x1, starting transfers between devices, sum_over_mesh(): received = lax.ppermute(other, 'row', [(i, i ^ 1) for i in range(rows)])  3.11 us
    pallas_call x6, Pallas kernels, in_vmem(): pl.pallas_call(kernel, out_shape=out_shape, in_specs=[vmem] * len(operand...  2.86 us
    ppermute x2, waiting for transfers between devices, swap_edges(): from_near = lax.ppermute(to_near, axis, near)  2.56 us
    pallas_call x1, Pallas kernels, row_borders(): pl.pallas_call(row_kernel, out_shape=(out, out), in_specs=[pl.BlockSpec(m...  1.91 us
  transfers between devices with their start and end apart: 5, of which 3 were waited for; matrix products, arithmetic and copies ran while one was open for 0% of the time, Pallas kernels for 2%

profile of v7, /device:TPU:1, one launch (start us, length us, event | category | flops | bytes accessed | tf_op | source)
XLA Modules:
  0.0 87.3 jit_solution(9573308170475551497)
XLA Ops:
  0.8 1.9 %row_borders.1 = (bf16[4,32,512]{2,1,0:T(8,128)(2,1)}, bf16[4,32,512]{2,1,0:T(8,128)(2,1)}) custom-call(bf16[16,32,384]{2,1,0:T(8,128)(2,1)} %joined_ref.5, bf16[16,32,64]{2,1,0:T(8,128)(2,1)} %block_ref.7, bf16[16,32,64]{2,1,0:T(8,128)(2,1)} %later_ref.5), custom_call_target="tpu_custom_call" | custom-call | tf_op jit(solution)/shard_map/row_borders/pallas_call | solution.py:497
  2.7 5.4 %collective-permute-start = (bf16[4,32,512]{2,1,0:T(8,128)(2,1)}, bf16[4,32,512]{2,1,0:T(8,128)(2,1)S(1)}, u32[]{:S(2)}, u32[]{:S(2)}) collective-permute-start(bf16[4,32,512]{2,1,0:T(8,128)(2,1)} %get-tuple-element.44), channel_id=1, source_target_pairs={{32,64},{96,128},{160,192},{224,256},{288,320},{352,384},{416,448}... | collective-permute-start | bytes 393224 | tf_op jit(solution)/shard_map/ppermute | solution.py:727
  8.1 4.1 %collective-permute-start.1 = (bf16[4,32,512]{2,1,0:T(8,128)(2,1)}, bf16[4,32,512]{2,1,0:T(8,128)(2,1)S(1)}, u32[]{:S(2)}, u32[]{:S(2)}) collective-permute-start(bf16[4,32,512]{2,1,0:T(8,128)(2,1)} %get-tuple-element.45), channel_id=1, source_target_pairs={{0,32},{32,0},{64,96},{96,64},{128,160},{160,128},{192,224},{224,1... | collective-permute-start | bytes 393224 | tf_op jit(solution)/shard_map/ppermute | solution.py:728
  12.2 1.2 %collective-permute-done.1 = bf16[4,32,512]{2,1,0:T(8,128)(2,1)S(1)} collective-permute-done((bf16[4,32,512]{2,1,0:T(8,128)(2,1)}, bf16[4,32,512]{2,1,0:T(8,128)(2,1)S(1)}, u32[]{:S(2)}, u32[]{:S(2)}) %collective-permute-start.1) | collective-permute-done | bytes 131104 | tf_op jit(solution)/shard_map/ppermute | solution.py:728
  13.4 0.2 column_borders.1
  13.6 1.9 %collective-permute-start.2 = (bf16[24,4,512]{2,1,0:T(4,128)(2,1)S(1)}, bf16[24,4,512]{2,1,0:T(4,128)(2,1)S(1)}, u32[]{:S(2)}, u32[]{:S(2)}) collective-permute-start(bf16[24,4,512]{2,1,0:T(4,128)(2,1)S(1)} %get-tuple-element.58), channel_id=1, source_target_pairs={{0,1},{1,0},{2,3},{3,2},{4,5},{5,4},{6,7},{7,6},{8,9},{9,8},{10,11... | collective-permute-start | bytes 294920 | tf_op jit(solution)/shard_map/ppermute | solution.py:728
  15.5 0.7 collective-permute-start.3
  16.2 0.1 pad.2.clone
  16.4 0.0 copy-start.4
  16.4 0.0 copy-start.5
  16.4 0.0 copy-start.16
  16.4 0.0 copy-start.17
  16.4 1.6 %own_pass.1 = (f32[168,384]{1,0:T(8,128)S(1)}, bf16[168,384]{1,0:T(8,128)(2,1)S(1)}, bf16[512,384]{1,0:T(8,128)(2,1)S(1)}, bf16[512,64]{1,0:T(8,128)(2,1)S(1)}, ...) custom-call(bf16[16,32,384]{2,1,0:T(8,128)(2,1)S(1)} %copy-done.1, ...), custom_call_target="tpu_custom_call" | custom-call | tf_op jit(solution)/shard_map/own_pass/pallas_call | solution.py:637
  18.1 1.4 %collective-permute-done.2 = bf16[24,4,512]{2,1,0:T(4,128)(2,1)S(1)} collective-permute-done((bf16[24,4,512]{2,1,0:T(4,128)(2,1)S(1)}, bf16[24,4,512]{2,1,0:T(4,128)(2,1)S(1)}, u32[]{:S(2)}, u32[]{:S(2)}) %collective-permute-start.2) | collective-permute-done | bytes 98336 | tf_op jit(solution)/shard_map/ppermute | solution.py:728
  19.5 0.2 maximum_maximum_fusion.side_ref
  19.8 5.0 %tile_pass.1 = (bf16[16,32,64]{2,1,0:T(8,128)(2,1)S(1)}, bf16[128,128]{1,0:T(8,128)(2,1)S(1)}, bf16[32,320]{1,0:T(8,128)(2,1)S(1)}, bf16[8,512]{1,0:T(8,128)(2,1...) custom-call(f32[168,384]{1,0:T(8,128)S(1)} %get-tuple-element.46.pooled_ref, ...), custom_call_target="tpu_custom_call" | custom-call | tf_op jit(solution)/shard_map/tile_pass/pallas_call | solution.py:529
  24.8 3.1 %collective-permute-start.4 = (bf16[16,112,128]{2,1,0:T(8,128)(2,1)S(1)}, bf16[16,112,128]{2,1,0:T(8,128)(2,1)S(1)}, u32[]{:S(2)}, u32[]{:S(2)}) collective-permute-start(bf16[16,112,128]{2,1,0:T(8,128)(2,1)S(1)} %get-tuple-element.61), channel_id=1, source_target_pairs={{0,32},{32,0},{64,96},{96,64},{128,160},{160,128},{192,224},{224,1... | collective-permute-start | bytes 1376264 | tf_op jit(solution)/shard_map/ppermute | solution.py:694
  27.9 1.4 %collective-permute-done.4.received_ref = bf16[16,112,128]{2,1,0:T(8,128)(2,1)S(1)} collective-permute-done((bf16[16,112,128]{2,1,0:T(8,128)(2,1)S(1)}, bf16[16,112,128]{2,1,0:T(8,128)(2,1)S(1)}, u32[]{:S(2)}, u32[]{:S(2)}) %collective-permute-start.4) | collective-permute-done | bytes 458784 | tf_op jit(solution)/shard_map/ppermute | solution.py:694
  29.3 0.1 chip_sums.1
  29.4 19.1 %all_to_all.15.received_ref = bf16[16,112,128]{2,1,0:T(8,128)(2,1)S(1)} all-to-all(bf16[16,112,128]{2,1,0:T(8,128)(2,1)S(1)} %chip_sums.1), channel_id=1, replica_groups={{0,1,2,3,4,5,6,7,64,65,66,67,68,69,70,71},{8,9,10,11,12,13,14,15,72,73,..., dimensions={0} | all-to-all | bytes 917504 | tf_op jit(solution)/shard_map/all_to_all | solution.py:692
  48.5 0.1 near_sums.1
  48.6 24.9 %all_to_all.16.received_ref = f32[16,16,128]{2,1,0:T(8,128)S(1)} all-to-all(f32[16,16,128]{2,1,0:T(8,128)S(1)} %near_sums.1), channel_id=1, replica_groups={{0,8,16,24,128,136,144,152,256,264,272,280,384,392,400,408},{1,9,17,25,..., dimensions={0} | all-to-all | bytes 262144 | tf_op jit(solution)/shard_map/all_to_all | solution.py:692
  73.5 13.0 %all_to_all.17.all_ref = f32[32,5,2,128]{3,2,1,0:T(2,128)S(1)} all-to-all(f32[32,5,2,128]{3,2,1,0:T(2,128)S(1)} %final_sums.1), channel_id=1, replica_groups={{0,32,1,33,2,34,3,35,4,36,5,37,6,38,7,39,64,96,65,97,66,98,67,99,68,100..., dimensions={0} | all-to-all | bytes 327680 | tf_op jit(solution)/shard_map/all_to_all | solution.py:692
  86.5 0.8 results.1
  (41 shorter events, 0.2 us)
Async XLA Ops:
  0.6 12.7 %copy-start.2 = (bf16[16,32,64]{2,1,0:T(8,128)(2,1)S(1)}, bf16[16,32,64]{2,1,0:T(8,128)(2,1)}, u32[]{:S(2)}) copy-start(bf16[16,32,64]{2,1,0:T(8,128)(2,1)} %block_ref.7) | copy-start | bytes 196612
  0.7 12.7 %copy-start.3 = (bf16[16,32,64]{2,1,0:T(8,128)(2,1)S(1)}, bf16[16,32,64]{2,1,0:T(8,128)(2,1)}, u32[]{:S(2)}) copy-start(bf16[16,32,64]{2,1,0:T(8,128)(2,1)} %later_ref.5) | copy-start | bytes 196612
  0.7 12.7 %copy-start.1 = (bf16[16,32,384]{2,1,0:T(8,128)(2,1)S(1)}, bf16[16,32,384]{2,1,0:T(8,128)(2,1)}, u32[]{:S(2)}) copy-start(bf16[16,32,384]{2,1,0:T(8,128)(2,1)} %joined_ref.5) | copy-start | bytes 1179652
  0.7 15.5 %copy-start.18 = (bf16[2,4,512]{2,1,0:T(4,128)(2,1)S(1)}, bf16[2,4,512]{2,1,0:T(4,128)(2,1)}, u32[]{:S(2)}) copy-start(bf16[2,4,512]{2,1,0:T(4,128)(2,1)} %param.27) | copy-start | bytes 24580
  0.7 15.6 %copy-start.8 = (bf16[64,256]{1,0:T(8,128)(2,1)S(1)}, bf16[64,256]{1,0:T(8,128)(2,1)}, u32[]{:S(2)}) copy-start(bf16[64,256]{1,0:T(8,128)(2,1)} %expand_ref.3) | copy-start | bytes 98308
  0.7 15.6 %copy-start.6 = (bf16[64,384]{1,0:T(8,128)(2,1)S(1)}, bf16[64,384]{1,0:T(8,128)(2,1)}, u32[]{:S(2)}) copy-start(bf16[64,384]{1,0:T(8,128)(2,1)} %first_ref.3) | copy-start | bytes 147460
  0.7 15.6 %copy-start = (bf16[1536,384]{1,0:T(8,128)(2,1)S(1)}, bf16[1536,384]{1,0:T(8,128)(2,1)}, u32[]{:S(2)}) copy-start(bf16[1536,384]{1,0:T(8,128)(2,1)} %join_ref.3) | copy-start | bytes 3538948
  0.7 15.6 %copy-start.7 = (bf16[256,64]{0,1:T(8,128)(2,1)S(1)}, bf16[256,64]{0,1:T(8,128)(2,1)}, u32[]{:S(2)}) copy-start(bf16[256,64]{0,1:T(8,128)(2,1)} %param.36) | copy-start | bytes 98308
  0.7 15.6 %copy-start.13 = (f32[256]{0:T(256)S(1)}, f32[256]{0:T(256)}, u32[]{:S(2)}) copy-start(f32[256]{0:T(256)} %param.33) | copy-start | bytes 3076
  0.7 15.6 %copy-start.15 = (f32[64]{0:T(128)S(1)}, f32[64]{0:T(128)}, u32[]{:S(2)}) copy-start(f32[64]{0:T(128)} %param.31) | copy-start | bytes 772
  0.7 15.6 %copy-start.14 = (f32[64]{0:T(128)S(1)}, f32[64]{0:T(128)}, u32[]{:S(2)}) copy-start(f32[64]{0:T(128)} %param.30) | copy-start | bytes 772
  0.8 15.6 %copy-start.11 = (bf16[4,8,320]{2,1,0:T(8,128)(2,1)S(1)}, bf16[4,8,320]{2,1,0:T(8,128)(2,1)}, u32[]{:S(2)}) copy-start(bf16[4,8,320]{2,1,0:T(8,128)(2,1)} %param.26) | copy-start | bytes 61444
  0.8 15.6 %copy-start.10 = (bf16[8,16,128]{2,1,0:T(8,128)(2,1)S(1)}, bf16[8,16,128]{2,1,0:T(8,128)(2,1)}, u32[]{:S(2)}) copy-start(bf16[8,16,128]{2,1,0:T(8,128)(2,1)} %param.25) | copy-start | bytes 98308
  2.7 9.5 %collective-permute-start = (bf16[4,32,512]{2,1,0:T(8,128)(2,1)}, bf16[4,32,512]{2,1,0:T(8,128)(2,1)S(1)}, u32[]{:S(2)}, u32[]{:S(2)}) collective-permute-start(bf16[4,32,512]{2,1,0:T(8,128)(2,1)} %get-tuple-element.44), channel_id=1, source_target_pairs={{32,64},{96,128},{160,192},{224,256},{288,320},{352,384},{416,448}... | collective-permute-start | bytes 393224 | tf_op jit(solution)/shard_map/ppermute | solution.py:727
  8.1 5.2 %collective-permute-start.1 = (bf16[4,32,512]{2,1,0:T(8,128)(2,1)}, bf16[4,32,512]{2,1,0:T(8,128)(2,1)S(1)}, u32[]{:S(2)}, u32[]{:S(2)}) collective-permute-start(bf16[4,32,512]{2,1,0:T(8,128)(2,1)} %get-tuple-element.45), channel_id=1, source_target_pairs={{0,32},{32,0},{64,96},{96,64},{128,160},{160,128},{192,224},{224,1... | collective-permute-start | bytes 393224 | tf_op jit(solution)/shard_map/ppermute | solution.py:728
  13.6 5.9 %collective-permute-start.2 = (bf16[24,4,512]{2,1,0:T(4,128)(2,1)S(1)}, bf16[24,4,512]{2,1,0:T(4,128)(2,1)S(1)}, u32[]{:S(2)}, u32[]{:S(2)}) collective-permute-start(bf16[24,4,512]{2,1,0:T(4,128)(2,1)S(1)} %get-tuple-element.58), channel_id=1, source_target_pairs={{0,1},{1,0},{2,3},{3,2},{4,5},{5,4},{6,7},{7,6},{8,9},{9,8},{10,11... | collective-permute-start | bytes 294920 | tf_op jit(solution)/shard_map/ppermute | solution.py:728
  15.5 4.0 %collective-permute-start.3 = (bf16[24,4,512]{2,1,0:T(4,128)(2,1)S(1)}, bf16[24,4,512]{2,1,0:T(4,128)(2,1)S(1)}, u32[]{:S(2)}, u32[]{:S(2)}) collective-permute-start(bf16[24,4,512]{2,1,0:T(4,128)(2,1)S(1)} %get-tuple-element.59), channel_id=1, source_target_pairs={{1,2},{3,4},{5,6},{7,8},{9,10},{11,12},{13,14},{15,16},{17,18},{19... | collective-permute-start | bytes 294920 | tf_op jit(solution)/shard_map/ppermute | solution.py:727
  16.4 3.3 %copy-start.4 = (bf16[512,384]{1,0:T(8,128)(2,1)S(1)}, bf16[512,384]{1,0:T(8,128)(2,1)}, u32[]{:S(2)}) copy-start(bf16[512,384]{1,0:T(8,128)(2,1)} %fourth_ref.1) | copy-start | bytes 1179652
  16.4 3.3 %copy-start.5 = (bf16[320,384]{1,0:T(8,128)(2,1)S(1)}, bf16[320,384]{1,0:T(8,128)(2,1)}, u32[]{:S(2)}) copy-start(bf16[320,384]{1,0:T(8,128)(2,1)} %third_ref.1) | copy-start | bytes 737284
  16.4 3.3 %copy-start.9 = (bf16[128,384]{1,0:T(8,128)(2,1)S(1)}, bf16[128,384]{1,0:T(8,128)(2,1)}, u32[]{:S(2)}) copy-start(bf16[128,384]{1,0:T(8,128)(2,1)} %second_ref.1) | copy-start | bytes 294916
  16.4 3.3 %copy-start.12 = (f32[9,256]{1,0:T(8,128)S(1)}, f32[9,256]{1,0:T(8,128)}, u32[]{:S(2)}) copy-start(f32[9,256]{1,0:T(8,128)} %depth_ref.1) | copy-start | bytes 27652
  16.4 3.3 %copy-start.16 = (f32[256]{0:T(256)S(1)}, f32[256]{0:T(256)}, u32[]{:S(2)}) copy-start(f32[256]{0:T(256)} %param.35) | copy-start | bytes 3076
  16.4 3.3 %copy-start.17 = (f32[64]{0:T(128)S(1)}, f32[64]{0:T(128)}, u32[]{:S(2)}) copy-start(f32[64]{0:T(128)} %param.37) | copy-start | bytes 772
  24.8 4.5 %collective-permute-start.4 = (bf16[16,112,128]{2,1,0:T(8,128)(2,1)S(1)}, bf16[16,112,128]{2,1,0:T(8,128)(2,1)S(1)}, u32[]{:S(2)}, u32[]{:S(2)}) collective-permute-start(bf16[16,112,128]{2,1,0:T(8,128)(2,1)S(1)} %get-tuple-element.61), channel_id=1, source_target_pairs={{0,32},{32,0},{64,96},{96,64},{128,160},{160,128},{192,224},{224,1... | collective-permute-start | bytes 1376264 | tf_op jit(solution)/shard_map/ppermute | solution.py:694

commit v8 on v7

--- a/solution.py
+++ b/solution.py
@@ -353,7 +353,7 @@
         slope_ref[i] = cumulative + conv * density
         return carry
 
-    lax.fori_loop(0, 18, conv_row, 0)
+    lax.fori_loop(0, 18, conv_row, 0, unroll=True)
 
     beside = slice(0, 2 * EDGE)
     projection = nt(
@@ -405,7 +405,7 @@
         taps.append(sums[10] + fold(center_row))
         return tuple(taps)
 
-    sums = lax.fori_loop(0, TH, grad_row, (jnp.zeros((8, HID), jnp.float32),) * 11)
+    sums = lax.fori_loop(0, TH, grad_row, (jnp.zeros((8, HID), jnp.float32),) * 11, unroll=True)
     for n in range(11):
         keep_row(12 + 2 * n, jnp.sum(sums[n], 0, keepdims=True) * scale_base)
 

time: 87.6 us -> 86.4 us (0.986)
  Pallas kernels: 9.76 us -> 8.52 us
    pallas_call x1, Pallas kernels: 4.99 us -> 3.75 us  [tile_pass(): pl.pallas_call(functools.partial(tile_kernel, height, width), out_shape=(...]
where the time goes in v8:
time: 86.4 us; the launch traced here: 86.1 us
  blocking collectives  56.9 us (66%)
  starting transfers between devices  15.1 us (17%)
  Pallas kernels  8.52 us (10%)
  waiting for transfers between devices  3.99 us (5%)
  between operations  1.06 us (1%)
    all_to_all x3, blocking collectives, exchange(): lax.all_to_all(parts, ('row', 'col'), 0, 0, tiled=True, axis_index_groups...  56.9 us
    ppermute x2, starting transfers between devices, swap_edges(): from_far = lax.ppermute(to_far, axis, far)  6.06 us
    ppermute x2, starting transfers between devices, swap_edges(): from_near = lax.ppermute(to_near, axis, near)  5.99 us
    pallas_call x1, Pallas kernels, tile_pass(): pl.pallas_call(functools.partial(tile_kernel, height, width), out_shape=(...  3.75 us
    ppermute x1, starting transfers between devices, sum_over_mesh(): received = lax.ppermute(other, 'row', [(i, i ^ 1) for i in range(rows)])  3.1 us
    pallas_call x6, Pallas kernels, in_vmem(): pl.pallas_call(kernel, out_shape=out_shape, in_specs=[vmem] * len(operand...  2.86 us
    ppermute x2, waiting for transfers between devices, swap_edges(): from_near = lax.ppermute(to_near, axis, near)  2.56 us
    pallas_call x1, Pallas kernels, row_borders(): pl.pallas_call(row_kernel, out_shape=(out, out), in_specs=[pl.BlockSpec(m...  1.91 us
  transfers between devices with their start and end apart: 5, of which 3 were waited for; matrix products, arithmetic and copies ran while one was open for 0% of the time, Pallas kernels for 2%

profile of v8, /device:TPU:1, one launch (start us, length us, event | category | flops | bytes accessed | tf_op | source)
XLA Modules:
  0.0 86.1 jit_solution(14872008284669508192)
XLA Ops:
  0.8 1.9 %row_borders.1 = (bf16[4,32,512]{2,1,0:T(8,128)(2,1)}, bf16[4,32,512]{2,1,0:T(8,128)(2,1)}) custom-call(bf16[16,32,384]{2,1,0:T(8,128)(2,1)} %joined_ref.5, bf16[16,32,64]{2,1,0:T(8,128)(2,1)} %block_ref.7, bf16[16,32,64]{2,1,0:T(8,128)(2,1)} %later_ref.5), custom_call_target="tpu_custom_call" | custom-call | tf_op jit(solution)/shard_map/row_borders/pallas_call | solution.py:497
  2.7 5.4 %collective-permute-start = (bf16[4,32,512]{2,1,0:T(8,128)(2,1)}, bf16[4,32,512]{2,1,0:T(8,128)(2,1)S(1)}, u32[]{:S(2)}, u32[]{:S(2)}) collective-permute-start(bf16[4,32,512]{2,1,0:T(8,128)(2,1)} %get-tuple-element.44), channel_id=1, source_target_pairs={{32,64},{96,128},{160,192},{224,256},{288,320},{352,384},{416,448}... | collective-permute-start | bytes 393224 | tf_op jit(solution)/shard_map/ppermute | solution.py:727
  8.1 4.1 %collective-permute-start.1 = (bf16[4,32,512]{2,1,0:T(8,128)(2,1)}, bf16[4,32,512]{2,1,0:T(8,128)(2,1)S(1)}, u32[]{:S(2)}, u32[]{:S(2)}) collective-permute-start(bf16[4,32,512]{2,1,0:T(8,128)(2,1)} %get-tuple-element.45), channel_id=1, source_target_pairs={{0,32},{32,0},{64,96},{96,64},{128,160},{160,128},{192,224},{224,1... | collective-permute-start | bytes 393224 | tf_op jit(solution)/shard_map/ppermute | solution.py:728
  12.2 1.2 %collective-permute-done.1 = bf16[4,32,512]{2,1,0:T(8,128)(2,1)S(1)} collective-permute-done((bf16[4,32,512]{2,1,0:T(8,128)(2,1)}, bf16[4,32,512]{2,1,0:T(8,128)(2,1)S(1)}, u32[]{:S(2)}, u32[]{:S(2)}) %collective-permute-start.1) | collective-permute-done | bytes 131104 | tf_op jit(solution)/shard_map/ppermute | solution.py:728
  13.4 0.2 column_borders.1
  13.6 1.9 %collective-permute-start.2 = (bf16[24,4,512]{2,1,0:T(4,128)(2,1)S(1)}, bf16[24,4,512]{2,1,0:T(4,128)(2,1)S(1)}, u32[]{:S(2)}, u32[]{:S(2)}) collective-permute-start(bf16[24,4,512]{2,1,0:T(4,128)(2,1)S(1)} %get-tuple-element.58), channel_id=1, source_target_pairs={{0,1},{1,0},{2,3},{3,2},{4,5},{5,4},{6,7},{7,6},{8,9},{9,8},{10,11... | collective-permute-start | bytes 294920 | tf_op jit(solution)/shard_map/ppermute | solution.py:728
  15.5 0.7 collective-permute-start.3
  16.2 0.1 pad.2.clone
  16.4 0.0 copy-start.4
  16.4 0.0 copy-start.5
  16.4 0.0 copy-start.16
  16.4 0.0 copy-start.17
  16.4 1.6 %own_pass.1 = (f32[168,384]{1,0:T(8,128)S(1)}, bf16[168,384]{1,0:T(8,128)(2,1)S(1)}, bf16[512,384]{1,0:T(8,128)(2,1)S(1)}, bf16[512,64]{1,0:T(8,128)(2,1)S(1)}, ...) custom-call(bf16[16,32,384]{2,1,0:T(8,128)(2,1)S(1)} %copy-done.1, ...), custom_call_target="tpu_custom_call" | custom-call | tf_op jit(solution)/shard_map/own_pass/pallas_call | solution.py:637
  18.1 1.4 %collective-permute-done.2 = bf16[24,4,512]{2,1,0:T(4,128)(2,1)S(1)} collective-permute-done((bf16[24,4,512]{2,1,0:T(4,128)(2,1)S(1)}, bf16[24,4,512]{2,1,0:T(4,128)(2,1)S(1)}, u32[]{:S(2)}, u32[]{:S(2)}) %collective-permute-start.2) | collective-permute-done | bytes 98336 | tf_op jit(solution)/shard_map/ppermute | solution.py:728
  19.5 0.2 maximum_maximum_fusion.side_ref
  19.8 3.8 %tile_pass.1 = (bf16[16,32,64]{2,1,0:T(8,128)(2,1)S(1)}, bf16[128,128]{1,0:T(8,128)(2,1)S(1)}, bf16[32,320]{1,0:T(8,128)(2,1)S(1)}, bf16[8,512]{1,0:T(8,128)(2,1...) custom-call(f32[168,384]{1,0:T(8,128)S(1)} %get-tuple-element.46.pooled_ref, ...), custom_call_target="tpu_custom_call" | custom-call | tf_op jit(solution)/shard_map/tile_pass/pallas_call | solution.py:529
  23.5 3.1 %collective-permute-start.4 = (bf16[16,112,128]{2,1,0:T(8,128)(2,1)S(1)}, bf16[16,112,128]{2,1,0:T(8,128)(2,1)S(1)}, u32[]{:S(2)}, u32[]{:S(2)}) collective-permute-start(bf16[16,112,128]{2,1,0:T(8,128)(2,1)S(1)} %get-tuple-element.61), channel_id=1, source_target_pairs={{0,32},{32,0},{64,96},{96,64},{128,160},{160,128},{192,224},{224,1... | collective-permute-start | bytes 1376264 | tf_op jit(solution)/shard_map/ppermute | solution.py:694
  26.6 1.4 %collective-permute-done.4.received_ref = bf16[16,112,128]{2,1,0:T(8,128)(2,1)S(1)} collective-permute-done((bf16[16,112,128]{2,1,0:T(8,128)(2,1)S(1)}, bf16[16,112,128]{2,1,0:T(8,128)(2,1)S(1)}, u32[]{:S(2)}, u32[]{:S(2)}) %collective-permute-start.4) | collective-permute-done | bytes 458784 | tf_op jit(solution)/shard_map/ppermute | solution.py:694
  28.1 0.1 chip_sums.1
  28.2 19.1 %all_to_all.15.received_ref = bf16[16,112,128]{2,1,0:T(8,128)(2,1)S(1)} all-to-all(bf16[16,112,128]{2,1,0:T(8,128)(2,1)S(1)} %chip_sums.1), channel_id=1, replica_groups={{0,1,2,3,4,5,6,7,64,65,66,67,68,69,70,71},{8,9,10,11,12,13,14,15,72,73,..., dimensions={0} | all-to-all | bytes 917504 | tf_op jit(solution)/shard_map/all_to_all | solution.py:692
  47.2 0.1 near_sums.1
  47.3 24.9 %all_to_all.16.received_ref = f32[16,16,128]{2,1,0:T(8,128)S(1)} all-to-all(f32[16,16,128]{2,1,0:T(8,128)S(1)} %near_sums.1), channel_id=1, replica_groups={{0,8,16,24,128,136,144,152,256,264,272,280,384,392,400,408},{1,9,17,25,..., dimensions={0} | all-to-all | bytes 262144 | tf_op jit(solution)/shard_map/all_to_all | solution.py:692
  72.3 13.0 %all_to_all.17.all_ref = f32[32,5,2,128]{3,2,1,0:T(2,128)S(1)} all-to-all(f32[32,5,2,128]{3,2,1,0:T(2,128)S(1)} %final_sums.1), channel_id=1, replica_groups={{0,32,1,33,2,34,3,35,4,36,5,37,6,38,7,39,64,96,65,97,66,98,67,99,68,100..., dimensions={0} | all-to-all | bytes 327680 | tf_op jit(solution)/shard_map/all_to_all | solution.py:692
  85.2 0.8 results.1
  (41 shorter events, 0.2 us)
Async XLA Ops:
  0.6 12.7 %copy-start.2 = (bf16[16,32,64]{2,1,0:T(8,128)(2,1)S(1)}, bf16[16,32,64]{2,1,0:T(8,128)(2,1)}, u32[]{:S(2)}) copy-start(bf16[16,32,64]{2,1,0:T(8,128)(2,1)} %block_ref.7) | copy-start | bytes 196612
  0.7 12.7 %copy-start.3 = (bf16[16,32,64]{2,1,0:T(8,128)(2,1)S(1)}, bf16[16,32,64]{2,1,0:T(8,128)(2,1)}, u32[]{:S(2)}) copy-start(bf16[16,32,64]{2,1,0:T(8,128)(2,1)} %later_ref.5) | copy-start | bytes 196612
  0.7 12.7 %copy-start.1 = (bf16[16,32,384]{2,1,0:T(8,128)(2,1)S(1)}, bf16[16,32,384]{2,1,0:T(8,128)(2,1)}, u32[]{:S(2)}) copy-start(bf16[16,32,384]{2,1,0:T(8,128)(2,1)} %joined_ref.5) | copy-start | bytes 1179652
  0.7 15.5 %copy-start.18 = (bf16[2,4,512]{2,1,0:T(4,128)(2,1)S(1)}, bf16[2,4,512]{2,1,0:T(4,128)(2,1)}, u32[]{:S(2)}) copy-start(bf16[2,4,512]{2,1,0:T(4,128)(2,1)} %param.27) | copy-start | bytes 24580
  0.7 15.6 %copy-start.8 = (bf16[64,256]{1,0:T(8,128)(2,1)S(1)}, bf16[64,256]{1,0:T(8,128)(2,1)}, u32[]{:S(2)}) copy-start(bf16[64,256]{1,0:T(8,128)(2,1)} %expand_ref.3) | copy-start | bytes 98308
  0.7 15.6 %copy-start.6 = (bf16[64,384]{1,0:T(8,128)(2,1)S(1)}, bf16[64,384]{1,0:T(8,128)(2,1)}, u32[]{:S(2)}) copy-start(bf16[64,384]{1,0:T(8,128)(2,1)} %first_ref.3) | copy-start | bytes 147460
  0.7 15.6 %copy-start = (bf16[1536,384]{1,0:T(8,128)(2,1)S(1)}, bf16[1536,384]{1,0:T(8,128)(2,1)}, u32[]{:S(2)}) copy-start(bf16[1536,384]{1,0:T(8,128)(2,1)} %join_ref.3) | copy-start | bytes 3538948
  0.7 15.6 %copy-start.7 = (bf16[256,64]{0,1:T(8,128)(2,1)S(1)}, bf16[256,64]{0,1:T(8,128)(2,1)}, u32[]{:S(2)}) copy-start(bf16[256,64]{0,1:T(8,128)(2,1)} %param.36) | copy-start | bytes 98308
  0.7 15.6 %copy-start.13 = (f32[256]{0:T(256)S(1)}, f32[256]{0:T(256)}, u32[]{:S(2)}) copy-start(f32[256]{0:T(256)} %param.33) | copy-start | bytes 3076
  0.7 15.6 %copy-start.15 = (f32[64]{0:T(128)S(1)}, f32[64]{0:T(128)}, u32[]{:S(2)}) copy-start(f32[64]{0:T(128)} %param.31) | copy-start | bytes 772
  0.7 15.6 %copy-start.14 = (f32[64]{0:T(128)S(1)}, f32[64]{0:T(128)}, u32[]{:S(2)}) copy-start(f32[64]{0:T(128)} %param.30) | copy-start | bytes 772
  0.8 15.6 %copy-start.11 = (bf16[4,8,320]{2,1,0:T(8,128)(2,1)S(1)}, bf16[4,8,320]{2,1,0:T(8,128)(2,1)}, u32[]{:S(2)}) copy-start(bf16[4,8,320]{2,1,0:T(8,128)(2,1)} %param.26) | copy-start | bytes 61444
  0.8 15.6 %copy-start.10 = (bf16[8,16,128]{2,1,0:T(8,128)(2,1)S(1)}, bf16[8,16,128]{2,1,0:T(8,128)(2,1)}, u32[]{:S(2)}) copy-start(bf16[8,16,128]{2,1,0:T(8,128)(2,1)} %param.25) | copy-start | bytes 98308
  2.7 9.5 %collective-permute-start = (bf16[4,32,512]{2,1,0:T(8,128)(2,1)}, bf16[4,32,512]{2,1,0:T(8,128)(2,1)S(1)}, u32[]{:S(2)}, u32[]{:S(2)}) collective-permute-start(bf16[4,32,512]{2,1,0:T(8,128)(2,1)} %get-tuple-element.44), channel_id=1, source_target_pairs={{32,64},{96,128},{160,192},{224,256},{288,320},{352,384},{416,448}... | collective-permute-start | bytes 393224 | tf_op jit(solution)/shard_map/ppermute | solution.py:727
  8.1 5.2 %collective-permute-start.1 = (bf16[4,32,512]{2,1,0:T(8,128)(2,1)}, bf16[4,32,512]{2,1,0:T(8,128)(2,1)S(1)}, u32[]{:S(2)}, u32[]{:S(2)}) collective-permute-start(bf16[4,32,512]{2,1,0:T(8,128)(2,1)} %get-tuple-element.45), channel_id=1, source_target_pairs={{0,32},{32,0},{64,96},{96,64},{128,160},{160,128},{192,224},{224,1... | collective-permute-start | bytes 393224 | tf_op jit(solution)/shard_map/ppermute | solution.py:728
  13.6 5.9 %collective-permute-start.2 = (bf16[24,4,512]{2,1,0:T(4,128)(2,1)S(1)}, bf16[24,4,512]{2,1,0:T(4,128)(2,1)S(1)}, u32[]{:S(2)}, u32[]{:S(2)}) collective-permute-start(bf16[24,4,512]{2,1,0:T(4,128)(2,1)S(1)} %get-tuple-element.58), channel_id=1, source_target_pairs={{0,1},{1,0},{2,3},{3,2},{4,5},{5,4},{6,7},{7,6},{8,9},{9,8},{10,11... | collective-permute-start | bytes 294920 | tf_op jit(solution)/shard_map/ppermute | solution.py:728
  15.5 4.0 %collective-permute-start.3 = (bf16[24,4,512]{2,1,0:T(4,128)(2,1)S(1)}, bf16[24,4,512]{2,1,0:T(4,128)(2,1)S(1)}, u32[]{:S(2)}, u32[]{:S(2)}) collective-permute-start(bf16[24,4,512]{2,1,0:T(4,128)(2,1)S(1)} %get-tuple-element.59), channel_id=1, source_target_pairs={{1,2},{3,4},{5,6},{7,8},{9,10},{11,12},{13,14},{15,16},{17,18},{19... | collective-permute-start | bytes 294920 | tf_op jit(solution)/shard_map/ppermute | solution.py:727
  16.4 3.3 %copy-start.4 = (bf16[512,384]{1,0:T(8,128)(2,1)S(1)}, bf16[512,384]{1,0:T(8,128)(2,1)}, u32[]{:S(2)}) copy-start(bf16[512,384]{1,0:T(8,128)(2,1)} %fourth_ref.1) | copy-start | bytes 1179652
  16.4 3.3 %copy-start.5 = (bf16[320,384]{1,0:T(8,128)(2,1)S(1)}, bf16[320,384]{1,0:T(8,128)(2,1)}, u32[]{:S(2)}) copy-start(bf16[320,384]{1,0:T(8,128)(2,1)} %third_ref.1) | copy-start | bytes 737284
  16.4 3.3 %copy-start.9 = (bf16[128,384]{1,0:T(8,128)(2,1)S(1)}, bf16[128,384]{1,0:T(8,128)(2,1)}, u32[]{:S(2)}) copy-start(bf16[128,384]{1,0:T(8,128)(2,1)} %second_ref.1) | copy-start | bytes 294916
  16.4 3.3 %copy-start.12 = (f32[9,256]{1,0:T(8,128)S(1)}, f32[9,256]{1,0:T(8,128)}, u32[]{:S(2)}) copy-start(f32[9,256]{1,0:T(8,128)} %depth_ref.1) | copy-start | bytes 27652
  16.4 3.3 %copy-start.16 = (f32[256]{0:T(256)S(1)}, f32[256]{0:T(256)}, u32[]{:S(2)}) copy-start(f32[256]{0:T(256)} %param.35) | copy-start | bytes 3076
  16.4 3.3 %copy-start.17 = (f32[64]{0:T(128)S(1)}, f32[64]{0:T(128)}, u32[]{:S(2)}) copy-start(f32[64]{0:T(128)} %param.37) | copy-start | bytes 772
  23.5 4.5 %collective-permute-start.4 = (bf16[16,112,128]{2,1,0:T(8,128)(2,1)S(1)}, bf16[16,112,128]{2,1,0:T(8,128)(2,1)S(1)}, u32[]{:S(2)}, u32[]{:S(2)}) collective-permute-start(bf16[16,112,128]{2,1,0:T(8,128)(2,1)S(1)} %get-tuple-element.61), channel_id=1, source_target_pairs={{0,32},{32,0},{64,96},{96,64},{128,160},{160,128},{192,224},{224,1... | collective-permute-start | bytes 1376264 | tf_op jit(solution)/shard_map/ppermute | solution.py:694
